TPU v7x, 32 devices: a whole 2x2x4 slice. The times are simulated.
32 devices in a mesh: replica: 2 (over y), expert: 8 (over z, core), tensor: 2 (over x).
Axes of the slice: x: 2, y: 2, z: 4, core: 2. Of those that a mesh axis runs over, the one named last changes fastest.
Arguments:
- tokens: bfloat16 [672, 4096], P(('replica', 'expert'), 'tensor'), parts along dimension 0, may hold values from -6 to 6
- route_ids: int32 [672, 8], P(('replica', 'expert')), parts along dimension 0, may hold values from 0 to 15, all different within a row; in each aligned block of 42 rows (0 to 41, 42 to 83, ...) at most 42 rows name the same one
- route_scores: float32 [672, 8], P(('replica', 'expert')), parts along dimension 0, may hold values from 0.05 to 1
- w_gate: bfloat16 [16, 4096, 1536], P('expert', 'tensor'), may hold values from -0.09375 to 0.09375
- w_up: bfloat16 [16, 4096, 1536], P('expert', 'tensor'), may hold values from -0.09375 to 0.09375
- w_down: bfloat16 [16, 1536, 4096], P('expert', None, 'tensor'), may hold values from -0.15625 to 0.15625
Outputs:
- mixed: bfloat16 [672, 4096], P(('replica', 'expert'), 'tensor'), parts along dimension 0
There are 2 independent parts, one for each index of `replica`. A program takes and returns all parts, laid end to end along the dimension named above; an argument that names none is the same for every part. Nothing has to cross between parts.
Inputs may be any that keep to these rules, and one draw needn't show every extreme that they name: `route_ids`: each row names 8 different experts. Within the rows of one index of the expert axis no expert is named by more than 42 rows, a bound that some block reaches of them.
All inputs are finite; a program needn't handle non-finite values.
Results may differ from a plain program's by a relative error of at most 0.0049.
Values may be sent and summed in bfloat16 or wider, within the bound.
No kernel may reach another device: no remote copies, remote signals or barrier semaphores. Data moves between devices by JAX's collectives and lax.ppermute only.
A program may use at most 128 MiB of HBM per device.

v0:
```python
import jax
import jax.numpy as jnp
from jax import lax
from jax.sharding import PartitionSpec as P


def slot_targets(chosen_ids, total_experts, capacity):
    expert_range = jnp.arange(total_experts, dtype=jnp.int32)
    hit_count = jnp.sum(
        (chosen_ids[:, :, None] == expert_range[None, None, :]).astype(jnp.int32), axis=1
    )
    before = jnp.cumsum(hit_count, axis=0) - hit_count
    return chosen_ids * capacity + jnp.take_along_axis(before, chosen_ids, axis=1)


def shards(tokens, route_ids, route_scores, w_gate, w_up, w_down):
    groups = lax.axis_size("expert")
    local_experts = w_gate.shape[0]
    count_rows = route_ids.shape[0]
    top_count = route_ids.shape[1]
    total_experts = groups * local_experts
    capacity = min(count_rows, 2 * count_rows * top_count // total_experts)
    slot_count = total_experts * capacity
    weights = route_scores / jnp.sum(route_scores, axis=1, keepdims=True)
    targets = slot_targets(route_ids, total_experts, capacity)
    row_width = tokens.shape[1]
    row_owner = jnp.broadcast_to(
        jnp.arange(count_rows, dtype=jnp.int32)[:, None], targets.shape
    ).reshape(-1)
    flat_index = targets.reshape(-1)
    source_row = jnp.zeros((slot_count,), jnp.int32).at[flat_index].set(row_owner)
    filled = jnp.zeros((slot_count,), jnp.bfloat16).at[flat_index].set(1.0)
    outgoing = (jnp.take(tokens, source_row, axis=0) * filled[:, None]).reshape(
        groups, local_experts, capacity, row_width
    )
    received = lax.all_to_all(outgoing, "expert", split_axis=0, concat_axis=0, tiled=True)
    gate_part = jnp.einsum("necd,edh->nech", received, w_gate, preferred_element_type=jnp.float32)
    up_part = jnp.einsum("necd,edh->nech", received, w_up, preferred_element_type=jnp.float32)
    gate_full, up_full = lax.psum((gate_part, up_part), "tensor")
    hidden = (jax.nn.silu(gate_full) * up_full).astype(jnp.bfloat16)
    produced = jnp.einsum("nech,ehd->necd", hidden, w_down, preferred_element_type=jnp.float32)
    returned = lax.all_to_all(produced, "expert", split_axis=0, concat_axis=0, tiled=True)
    returned = returned.reshape(slot_count, returned.shape[3])
    picked = jnp.take(returned, targets, axis=0)
    combined = jnp.sum(weights[:, :, None] * picked, axis=1)
    return combined.astype(jnp.bfloat16)


def solution(mesh):
    placed = (
        P(("replica", "expert"), "tensor"),
        P(("replica", "expert"), None),
        P(("replica", "expert"), None),
        P("expert", "tensor", None),
        P("expert", "tensor", None),
        P("expert", None, "tensor"),
    )
    return jax.shard_map(
        shards,
        mesh=mesh,
        in_specs=placed,
        out_specs=P(("replica", "expert"), "tensor"),
        check_vma=False,
    )
```

profile of v0, /device:TPU:0, one launch (start us, length us, event | category | flops | bytes accessed | tf_op | source)
XLA Modules:
  0.0 511.6 jit_solution(15419356097165622656)
XLA Ops:
  6.5 0.7 convert_reduce_fusion
  7.3 0.7 bitcast_or_fusion
  8.3 4.1 gather_fusion.2
  12.6 0.1 copy.58
  12.9 2.9 scatter_custom_fusion
  15.9 4.1 gather_fusion
  20.0 2.9 gather.16
  23.0 2.7 scatter_custom_fusion.1
  25.7 0.4 select_multiply_fusion
  26.1 2.8 copy.59
  29.0 69.5 %all_to_all.10 = bf16[8,2,42,2048]{3,1,2,0:T(2,128)(2,1)S(1)} all-to-all(bf16[8,2,42,2048]{3,1,2,0:T(2,128)(2,1)S(1)} %copy.59), channel_id=1, replica_groups=mesh['replica'=2,'expert'=8,'tensor'=2] {'expert'}, dimensions={0} | all-to-all | bytes 5505024 | tf_op jit(solution)/shard_map/all_to_all | solution.py:36
  98.5 10.7 %fusion.6 = f32[8,2,42,1536]{3,2,0,1:T(8,128)} fusion(bf16[2,2048,1536]{2,1,0:T(8,128)(2,1)} %param.9, bf16[8,2,42,2048]{3,1,2,0:T(2,128)(2,1)S(1)} %all_to_all.10), kind=kOutput, calls=%fused_computation.12 | convolution fusion | flops 4227858432 | bytes 19464192 | tf_op jit(solution)/shard_map/necd,edh->nech/dot_general | solution.py:37
  109.2 7.3 %fusion.9 = f32[8,2,42,1536]{3,2,0,1:T(8,128)} fusion(bf16[2,2048,1536]{2,1,0:T(8,128)(2,1)S(1)} %bitcast.38, bf16[8,2,42,2048]{3,1,2,0:T(2,128)(2,1)S(1)} %all_to_all.10), kind=kOutput, calls=%fused_computation.13 | convolution fusion | flops 4227858432 | bytes 19464192 | tf_op jit(solution)/shard_map/necd,edh->nech/dot_general | solution.py:38
  116.5 220.2 %all-reduce.3.cloned.1.call-done = (f32[8,2,42,1536]{3,2,0,1:T(8,128)}, f32[8,2,42,1536]{3,2,0,1:T(8,128)}) async-done(((f32[8,2,42,1536]{3,2,0,1:T(8,128)}, f32[8,2,42,1536]{3,2,0,1:T(8,128)}), (f32[8,2,42,1536]{3,2,0,1:T(8,128)}, f32[8,2,42,1536]{3,2,0,1:T(8,128)})) %all-reduce.3.cloned.1.call-update) | async-done | bytes 8257552 | tf_op jit(solution)/shard_map/psum | solution.py:39
  336.7 11.0 %fusion.12 = f32[8,2,42,2048]{3,2,0,1:T(8,128)S(1)} fusion(bf16[2,1536,2048]{2,1,0:T(8,128)(2,1)} %param.11, f32[8,2,42,1536]{3,2,0,1:T(8,128)} %get-tuple-element.5, f32[8,2,42,1536]{3,2,0,1:T(8,128)} %get-tuple-element.6), kind=kOutput, calls=%fused_computation.14 | convolution fusion | flops 4234051584 | bytes 26345472 | tf_op jit(solution)/shard_map/nech,ehd->necd/dot_general | solution.py:41
  347.7 6.7 %copy.62 = f32[8,2,42,2048]{3,1,2,0:T(2,128)} copy(f32[8,2,42,2048]{3,2,0,1:T(8,128)S(1)} %fusion.12) | data formatting | bytes 11010048 | tf_op jit(solution)/shard_map/nech,ehd->necd/transpose | solution.py:41
  354.4 5.0 all-to-all-start.1
  359.6 0.1 copy.57
  359.8 0.1 copy.52
  359.9 121.5 %all-to-all-done.1 = f32[8,2,42,2048]{3,1,2,0:T(2,128)} async-done(((f32[8,2,42,2048]{3,1,2,0:T(2,128)}), f32[8,2,42,2048]{3,1,2,0:T(2,128)}, u32[]{:S(2)}, u32[]{:S(2)}) %all-to-all-start.1) | async-done | bytes 5505056 | tf_op jit(solution)/shard_map/all_to_all | solution.py:42
  481.3 8.4 %copy.63 = f32[8,2,42,2048]{3,2,1,0:T(8,128)} copy(f32[8,2,42,2048]{3,1,2,0:T(2,128)} %all-to-all-done.1) | data formatting | bytes 11010048 | tf_op jit(solution)/shard_map/all_to_all | solution.py:42
  489.7 5.8 %reshape.75 = f32[672,2048]{1,0:T(8,128)} reshape(f32[8,2,42,2048]{3,2,1,0:T(8,128)} %copy.63) | data formatting | bytes 11010048 | tf_op jit(solution)/shard_map/reshape | solution.py:43
  495.5 6.9 %gather_fusion.1 = f32[336,2048]{1,0:T(8,128)S(1)} fusion(f32[672,2048]{1,0:T(8,128)} %reshape.75, s32[1024]{0:T(1024)S(1)} %pad_clamp_fusion), kind=kCustom, calls=%fused_computation.1 | custom fusion | bytes 5506368 | tf_op jit(solution)/shard_map/jit(_take)/gather | solution.py:44
  502.4 2.3 fusion.18
  (41 shorter events, 1.2 us)
Async XLA Ops:
  6.5 9.3 %copy-start = (bf16[42,2048]{1,0:T(8,128)(2,1)S(1)}, bf16[42,2048]{1,0:T(8,128)(2,1)}, u32[]{:S(2)}) copy-start(bf16[42,2048]{1,0:T(8,128)(2,1)} %param.6) | copy-start | bytes 516100
  6.5 330.2 %all-reduce.3.cloned.1.call-start = ((), (), s32[]{:S(2)}) async-start(), calls=%async_computation.2 | async-start | bytes 18874368 | tf_op jit(solution)/shard_map/psum | solution.py:39
  8.3 4.3 copy-start.2
  29.0 80.2 %slice-start = ((s8[12582912]{0:T(1024)(128)(4,1)}), s8[4194304]{0:T(1024)(128)(4,1)S(1)}, s32[]{:S(2)}) async-start(s8[12582912]{0:T(1024)(128)(4,1)} %bitcast.37), calls=%async_computation.3 | async-start | bytes 8388608
  98.5 10.7 %slice-start.1 = ((s8[12582912]{0:T(1024)(128)(4,1)}), s8[4194304]{0:T(1024)(128)(4,1)S(1)}, s32[]{:S(2)}) async-start(s8[12582912]{0:T(1024)(128)(4,1)} %bitcast.37), calls=%async_computation.4 | async-start | bytes 8388608
  98.5 10.7 %slice-start.2 = ((s8[12582912]{0:T(1024)(128)(4,1)}), s8[4194304]{0:T(1024)(128)(4,1)S(1)}, s32[]{:S(2)}) async-start(s8[12582912]{0:T(1024)(128)(4,1)} %bitcast.37), calls=%async_computation.5 | async-start | bytes 8388608
  354.4 5.4 %copy-start.3 = (f32[42,8]{0,1:T(8,128)S(1)}, f32[42,8]{0,1:T(8,128)}, u32[]{:S(2)}) copy-start(f32[42,8]{0,1:T(8,128)} %param.8) | copy-start | bytes 4036
  354.4 126.9 %all-to-all-start.1 = ((f32[8,2,42,2048]{3,1,2,0:T(2,128)}), f32[8,2,42,2048]{3,1,2,0:T(2,128)}, u32[]{:S(2)}, u32[]{:S(2)}) async-start(f32[8,2,42,2048]{3,1,2,0:T(2,128)} %copy.62), calls=%async_computation.1 | async-start | bytes 11010048 | tf_op jit(solution)/shard_map/all_to_all | solution.py:42
  495.5 9.2 %copy-start.1 = (bf16[42,2048]{1,0:T(8,128)(2,1)S(1)}, bf16[42,2048]{1,0:T(8,128)(2,1)}, u32[]{:S(2)}) copy-start(bf16[42,2048]{1,0:T(8,128)(2,1)} %param.6) | copy-start | bytes 516100
Sparse Core Ops, SparseCore 0:
  116.6 220.0 all-reduce.2
where the time goes:
time: 512 us
  waiting for transfers between devices  342 us (67%)
  blocking collectives  69.5 us (14%)
  local copies, waits for them, and re-layouts  48.5 us (9%)
  matrix products  29 us (6%)
  between operations  13.6 us (3%)
    psum x1, waiting for transfers between devices, shards(): gate_full, up_full = lax.psum((gate_part, up_part), 'tensor')  220 us
    all_to_all x1, waiting for transfers between devices, shards(): lax.all_to_all(produced, 'expert', split_axis=0, concat_axis=0, tiled=True)  121 us
    all_to_all x1, blocking collectives, shards(): lax.all_to_all(outgoing, 'expert', split_axis=0, concat_axis=0, tiled=True)  69.5 us
    dot_general x1, matrix products, shards(): jnp.einsum('nech,ehd->necd', hidden, w_down, preferred_element_type=jnp.f...  11 us
    dot_general x1, matrix products, shards(): jnp.einsum('necd,edh->nech', received, w_gate, preferred_element_type=jnp...  10.7 us
  transfers between devices with their start and end apart: 2, of which 2 were waited for; matrix products, arithmetic and copies ran while one was open for 0% of the time, Pallas kernels for 0%

commit v1 on v0

--- a/solution.py
+++ b/solution.py
@@ -1,7 +1,14 @@
+import functools
+
 import jax
 import jax.numpy as jnp
 from jax import lax
+from jax.experimental import pallas as pl
+from jax.experimental.pallas import tpu as pltpu
 from jax.sharding import PartitionSpec as P
+
+CORES = 2
+VMEM_LIMIT = 40 * 1024 * 1024
 
 
 def slot_targets(chosen_ids, total_experts, capacity):
@@ -13,7 +20,7 @@
     return chosen_ids * capacity + jnp.take_along_axis(before, chosen_ids, axis=1)
 
 
-def shards(tokens, route_ids, route_scores, w_gate, w_up, w_down):
+def general_shards(tokens, route_ids, route_scores, w_gate, w_up, w_down):
     groups = lax.axis_size("expert")
     local_experts = w_gate.shape[0]
     count_rows = route_ids.shape[0]
@@ -46,7 +53,154 @@
     return combined.astype(jnp.bfloat16)
 
 
+def gate_up_kernel(side_ref, rows_ref, gate_ref, up_ref, out_ref):
+    rows = rows_ref[...]
+    out_ref[0, 0] = jnp.dot(rows, gate_ref[0], preferred_element_type=jnp.float32).astype(out_ref.dtype)
+    out_ref[0, 1] = jnp.dot(rows, up_ref[0], preferred_element_type=jnp.float32).astype(out_ref.dtype)
+
+
+def gate_up(side, rows, w_gate, w_up, dtype):
+    count = rows.shape[0]
+    experts, width, units = w_gate.shape
+    half = units // 2
+    tile = 256
+    steps = half // tile
+    weight_spec = pl.BlockSpec((1, width, tile), lambda e, j, side: (e, 0, side[0] * steps + j))
+    return pl.pallas_call(
+        gate_up_kernel,
+        out_shape=jax.ShapeDtypeStruct((experts, 2, count, half), dtype),
+        grid_spec=pltpu.PrefetchScalarGridSpec(
+            num_scalar_prefetch=1,
+            grid=(experts, steps),
+            in_specs=[
+                pl.BlockSpec((count, width), lambda e, j, side: (0, 0)),
+                weight_spec,
+                weight_spec,
+            ],
+            out_specs=pl.BlockSpec((1, 2, count, tile), lambda e, j, side: (e, 0, 0, j)),
+        ),
+        compiler_params=pltpu.CompilerParams(vmem_limit_bytes=VMEM_LIMIT),
+        cost_estimate=pl.CostEstimate(
+            flops=4 * count * width * half * experts,
+            bytes_accessed=4 * experts * width * half,
+            transcendentals=0,
+        ),
+        name="gate_up",
+    )(side, rows, w_gate, w_up)
+
+
+def down_kernel(first, side_ref, hidden_ref, weight_ref, *refs):
+    out_ref = refs[-1]
+    product = jnp.dot(hidden_ref[0], weight_ref[0], preferred_element_type=jnp.float32)
+    at_start = (pl.program_id(0) == 0) & (pl.program_id(1) == 0)
+
+    @pl.when(at_start)
+    def _():
+        out_ref[...] = product if first else refs[0][...] + product
+
+    @pl.when(jnp.logical_not(at_start))
+    def _():
+        out_ref[...] += product
+
+
+def down(side, hidden, w_down, so_far):
+    experts, count, half = hidden.shape
+    width = w_down.shape[2]
+    depth = 384
+    steps = half // depth
+    extra = [] if so_far is None else [so_far]
+    whole = pl.BlockSpec((count, width), lambda e, j, side: (0, 0))
+    return pl.pallas_call(
+        functools.partial(down_kernel, so_far is None),
+        out_shape=jax.ShapeDtypeStruct((count, width), jnp.float32),
+        grid_spec=pltpu.PrefetchScalarGridSpec(
+            num_scalar_prefetch=1,
+            grid=(experts, steps),
+            in_specs=[
+                pl.BlockSpec((1, count, depth), lambda e, j, side: (e, 0, j)),
+                pl.BlockSpec((1, depth, width), lambda e, j, side: (e, side[0] * steps + j, 0)),
+            ]
+            + [whole for _ in extra],
+            out_specs=whole,
+        ),
+        compiler_params=pltpu.CompilerParams(vmem_limit_bytes=VMEM_LIMIT),
+        cost_estimate=pl.CostEstimate(
+            flops=2 * count * width * half * experts,
+            bytes_accessed=2 * experts * width * half,
+            transcendentals=0,
+        ),
+        name="down",
+    )(side, hidden, w_down, *extra)
+
+
+def pair_shards(tokens, route_ids, route_scores, w_gate, w_up, w_down):
+    groups = lax.axis_size("expert")
+    local_experts = w_gate.shape[0]
+    count, width = tokens.shape
+    w_gate, w_up, w_down = (
+        pltpu.with_memory_space_constraint(w, pltpu.HBM) for w in (w_gate, w_up, w_down)
+    )
+    total_experts = groups * local_experts
+    chips = groups // CORES
+    here = lax.axis_index("expert")
+    mine = lax.axis_index("tensor").reshape(1)
+    other = 1 - mine
+
+    def swap_tensor(value):
+        return lax.ppermute(value, "tensor", [(0, 1), (1, 0)])
+
+    def swap_expert(value, mask):
+        return lax.ppermute(value, "expert", [(i, i ^ mask) for i in range(groups)])
+
+    weights = route_scores / jnp.sum(route_scores, axis=1, keepdims=True)
+    hit = route_ids[:, :, None] == jnp.arange(total_experts, dtype=jnp.int32)[None, None, :]
+    share = jnp.sum(jnp.where(hit, weights[:, :, None], 0.0), axis=1)
+    share_high = share.astype(jnp.bfloat16)
+    share_low = (share - share_high.astype(jnp.float32)).astype(jnp.bfloat16)
+    pad = -(2 * total_experts) % 128
+    sent = jnp.concatenate(
+        [tokens, share_high, share_low, jnp.zeros((count, pad), jnp.bfloat16)], axis=1
+    )
+
+    arrived = []
+    for step in range(chips):
+        same = swap_expert(sent, CORES * step) if step else sent
+        arrived.append((same, swap_expert(same, 1)))
+
+    def share_of(rows):
+        high = lax.dynamic_slice(rows, (0, width + here * local_experts), (rows.shape[0], local_experts))
+        low = lax.dynamic_slice(
+            rows, (0, width + total_experts + here * local_experts), (rows.shape[0], local_experts)
+        )
+        return (high.astype(jnp.float32) + low.astype(jnp.float32)).T[:, :, None]
+
+    order = [0] + [s for s in range(2, chips)] + [1] if chips > 1 else [0]
+    total = None
+    parts = {}
+    for step in order:
+        rows = jnp.concatenate(arrived[step], axis=0)
+        theirs = gate_up(other, rows, w_gate, w_up, jnp.bfloat16)
+        received = swap_tensor(theirs)
+        kept = gate_up(mine, rows, w_gate, w_up, jnp.float32)
+        full = kept + received.astype(jnp.float32)
+        hidden = (jax.nn.silu(full[:, 0]) * full[:, 1] * share_of(rows)).astype(jnp.bfloat16)
+        hidden_other = swap_tensor(hidden)
+        product = down(mine, hidden, w_down, None)
+        product = down(other, hidden_other, w_down, product)
+        from_core = swap_expert(product[count:].astype(jnp.bfloat16), 1)
+        summed = product[:count] + from_core.astype(jnp.float32)
+        if step:
+            summed = swap_expert(summed.astype(jnp.bfloat16), CORES * step).astype(jnp.float32)
+        parts[step] = summed
+    total = parts[0]
+    for step in range(1, chips):
+        total = total + parts[step]
+    return total.astype(jnp.bfloat16)
+
+
 def solution(mesh):
+    groups = mesh.shape["expert"]
+    paired = mesh.shape["tensor"] == 2 and groups % CORES == 0 and groups & (groups - 1) == 0
     placed = (
         P(("replica", "expert"), "tensor"),
         P(("replica", "expert"), None),
@@ -56,7 +210,7 @@
         P("expert", None, "tensor"),
     )
     return jax.shard_map(
-        shards,
+        pair_shards if paired else general_shards,
         mesh=mesh,
         in_specs=placed,
         out_specs=P(("replica", "expert"), "tensor"),

time: 512 us -> 154 us (0.30)
  waiting for transfers between devices: 342 us -> 19.5 us
  Pallas kernels: 0 us -> 93.9 us
  blocking collectives: 69.5 us -> 0 us
  local copies, waits for them, and re-layouts: 48.5 us -> 5.68 us
  matrix products: 29 us -> 0 us
  starting transfers between devices: 5.05 us -> 23.5 us
  between operations: 13.6 us -> 0.34 us
    psum x1 -> x0, waiting for transfers between devices: 220 us -> none  [shards(): gate_full, up_full = lax.psum((gate_part, up_part), 'tensor')]
    all_to_all x1 -> x0, waiting for transfers between devices: 121 us -> none  [shards(): lax.all_to_all(produced, 'expert', split_axis=0, concat_axis=0, tiled=True)]
    pallas_call x0 -> x16, Pallas kernels: none -> 93.9 us  [the longest x8 57.6 us: gate_up(): pl.pallas_call(gate_up_kernel, out_shape=jax.ShapeDtypeStruct((experts, 2...]
    all_to_all x1 -> x0, blocking collectives: 69.5 us -> none  [shards(): lax.all_to_all(outgoing, 'expert', split_axis=0, concat_axis=0, tiled=True)]
    dot_general x3 -> x0, matrix products: 29 us -> none  [the longest x1 11 us: shards(): jnp.einsum('nech,ehd->necd', hidden, w_down, preferred_element_type=jnp.f...]
    ppermute x0 -> x22, starting transfers between devices: none -> 23.5 us  [the longest x14 13.9 us: swap_expert(): return lax.ppermute(value, 'expert', [(i, i ^ mask) for i in range(groups)])]
    ppermute x0 -> x22, waiting for transfers between devices: none -> 19.5 us  [the longest x14 19.5 us: swap_expert(): return lax.ppermute(value, 'expert', [(i, i ^ mask) for i in range(groups)])]
    gather x8 -> x0, local copies, waits for them, and re-layouts: 18.3 us -> none  [the longest x2 6.98 us: shards(): jnp.take(tokens, source_row, axis=0) * filled[:, None]]
  transfers between devices with their start and end apart: 2 -> 22, of which waited for: 2 -> 3; matrix products, arithmetic and copies ran while one was open for 0% -> 7% of each run, Pallas kernels for 0% -> 62%
where the time goes in v1:
time: 154 us; the launch traced here: 152 us
  Pallas kernels  93.9 us (61%)
  starting transfers between devices  23.5 us (15%)
  waiting for transfers between devices  19.5 us (13%)
  other arithmetic  8.95 us (6%)
  local copies, waits for them, and re-layouts  5.68 us (4%)
    pallas_call x8, Pallas kernels, gate_up(): pl.pallas_call(gate_up_kernel, out_shape=jax.ShapeDtypeStruct((experts, 2...  57.6 us
    pallas_call x8, Pallas kernels, down(): pl.pallas_call(functools.partial(down_kernel, so_far is None), out_shape=...  36.4 us
    ppermute x14, waiting for transfers between devices, swap_expert(): return lax.ppermute(value, 'expert', [(i, i ^ mask) for i in range(groups)])  19.5 us
    ppermute x14, starting transfers between devices, swap_expert(): return lax.ppermute(value, 'expert', [(i, i ^ mask) for i in range(groups)])  13.9 us
    ppermute x8, starting transfers between devices, swap_tensor(): return lax.ppermute(value, 'tensor', [(0, 1), (1, 0)])  9.63 us
    add x4, other arithmetic, pair_shards(): full = kept + received.astype(jnp.float32)  4.57 us
    pallas_call x4, local copies, waits for them, and re-layouts, gate_up(): pl.pallas_call(gate_up_kernel, out_shape=jax.ShapeDtypeStruct((experts, 2...  4.01 us
  transfers between devices with their start and end apart: 22, of which 3 were waited for; matrix products, arithmetic and copies ran while one was open for 7% of the time, Pallas kernels for 62%

profile of v1, /device:TPU:0, one launch (start us, length us, event | category | flops | bytes accessed | tf_op | source)
XLA Modules:
  0.0 152.0 jit_solution(75189877674179431)
XLA Ops:
  3.9 2.6 %collective-permute-start.4 = (bf16[42,2176]{1,0:T(8,128)(2,1)S(1)}, bf16[42,2176]{1,0:T(8,128)(2,1)S(1)}, u32[]{:S(2)}, u32[]{:S(2)}) collective-permute-start(bf16[42,2176]{1,0:T(8,128)(2,1)S(1)} %concatenate.15), channel_id=1, source_target_pairs={{0,4},{2,6},{4,0},{6,2},{8,12},{10,14},{12,8},{14,10},{1,5},{3,7},... | collective-permute-start | bytes 548360 | tf_op jit(solution)/shard_map/ppermute | solution.py:153
  6.5 2.6 %collective-permute-start.10 = (bf16[42,2176]{1,0:T(8,128)(2,1)S(1)}, bf16[42,2176]{1,0:T(8,128)(2,1)S(1)}, u32[]{:S(2)}, u32[]{:S(2)}) collective-permute-start(bf16[42,2176]{1,0:T(8,128)(2,1)S(1)} %concatenate.15), channel_id=1, source_target_pairs={{0,8},{2,10},{4,12},{6,14},{8,0},{10,2},{12,4},{14,6},{1,9},{3,11}... | collective-permute-start | bytes 548360 | tf_op jit(solution)/shard_map/ppermute | solution.py:153
  9.2 7.2 %gate_up.9 = bf16[2,2,84,768]{3,2,1,0:T(8,128)(2,1)S(1)} custom-call(s32[1]{0:T(128)S(6)} %sub.6.side_ref, bf16[84,2176]{1,0:T(8,128)(2,1)S(1)} %pad_maximum_fusion.rows_ref, bf16[2,2048,1536]{2,1,0:T(8,128)(2,1)} %gate_ref.15, bf16[2,2048,1536]{2,1,0:T(8,128)(2,1)} %up_ref.15), custom_call_target="tpu_custom_call" | custom-call | flops 1056964608 | bytes 12582912 | tf_op jit(solution)/shard_map/gate_up/pallas_call | solution.py:69
  17.6 1.7 %collective-permute-start.1 = (bf16[2,2,84,768]{3,1,2,0:T(2,128)(2,1)}, bf16[2,2,84,768]{3,1,2,0:T(2,128)(2,1)}, u32[]{:S(2)}, u32[]{:S(2)}) collective-permute-start(bf16[2,2,84,768]{3,1,2,0:T(2,128)(2,1)} %copy.60), channel_id=1, source_target_pairs={{0,1},{1,0},{2,3},{3,2},{4,5},{5,4},{6,7},{7,6},{8,9},{9,8},{10,11... | collective-permute-start | bytes 1548296 | tf_op jit(solution)/shard_map/ppermute | solution.py:150
  19.5 5.0 %collective-permute-done.10 = bf16[42,2176]{1,0:T(8,128)(2,1)S(1)} collective-permute-done((bf16[42,2176]{1,0:T(8,128)(2,1)S(1)}, bf16[42,2176]{1,0:T(8,128)(2,1)S(1)}, u32[]{:S(2)}, u32[]{:S(2)}) %collective-permute-start.10) | collective-permute-done | bytes 182816 | tf_op jit(solution)/shard_map/ppermute | solution.py:153
  24.9 7.2 %gate_up.8 = f32[2,2,84,768]{3,2,1,0:T(8,128)S(1)} custom-call(s32[1]{0:T(128)} %bitcast.side_ref, bf16[84,2176]{1,0:T(8,128)(2,1)S(1)} %pad_maximum_fusion.rows_ref, bf16[2,2048,1536]{2,1,0:T(8,128)(2,1)} %gate_ref.15, bf16[2,2048,1536]{2,1,0:T(8,128)(2,1)} %up_ref.15), custom_call_target="tpu_custom_call" | custom-call | flops 1056964608 | bytes 12582912 | tf_op jit(solution)/shard_map/gate_up/pallas_call | solution.py:69
  32.2 7.2 %gate_up.11 = bf16[2,2,84,768]{3,2,1,0:T(8,128)(2,1)S(1)} custom-call(s32[1]{0:T(128)S(6)} %sub.6.side_ref, bf16[84,2176]{1,0:T(8,128)(2,1)S(1)} %pad_maximum_fusion.1.rows_ref, bf16[2,2048,1536]{2,1,0:T(8,128)(2,1)} %gate_ref.15, bf16[2,2048,1536]{2,1,0:T(8,128)(2,1)} %up_ref.15), custom_call_target="tpu_custom_call" | custom-call | flops 1056964608 | bytes 12582912 | tf_op jit(solution)/shard_map/gate_up/pallas_call | solution.py:69
  42.4 7.2 %gate_up.13 = bf16[2,2,84,768]{3,2,1,0:T(8,128)(2,1)S(1)} custom-call(s32[1]{0:T(128)S(6)} %sub.6.side_ref, bf16[84,2176]{1,0:T(8,128)(2,1)S(1)} %pad_maximum_fusion.2.rows_ref, bf16[2,2048,1536]{2,1,0:T(8,128)(2,1)} %gate_ref.15, bf16[2,2048,1536]{2,1,0:T(8,128)(2,1)} %up_ref.15), custom_call_target="tpu_custom_call" | custom-call | flops 1056964608 | bytes 12582912 | tf_op jit(solution)/shard_map/gate_up/pallas_call | solution.py:69
  51.6 7.2 %gate_up.15 = bf16[2,2,84,768]{3,2,1,0:T(8,128)(2,1)S(1)} custom-call(s32[1]{0:T(128)S(6)} %sub.6.side_ref, bf16[84,2176]{1,0:T(8,128)(2,1)S(1)} %pad_maximum_fusion.3.rows_ref, bf16[2,2048,1536]{2,1,0:T(8,128)(2,1)} %gate_ref.15, bf16[2,2048,1536]{2,1,0:T(8,128)(2,1)} %up_ref.15), custom_call_target="tpu_custom_call" | custom-call | flops 1056964608 | bytes 12582912 | tf_op jit(solution)/shard_map/gate_up/pallas_call | solution.py:69
  60.9 7.2 %gate_up.10 = f32[2,2,84,768]{3,2,1,0:T(8,128)S(1)} custom-call(s32[1]{0:T(128)} %bitcast.side_ref, bf16[84,2176]{1,0:T(8,128)(2,1)S(1)} %pad_maximum_fusion.1.rows_ref, bf16[2,2048,1536]{2,1,0:T(8,128)(2,1)} %gate_ref.15, bf16[2,2048,1536]{2,1,0:T(8,128)(2,1)} %up_ref.15), custom_call_target="tpu_custom_call" | custom-call | flops 1056964608 | bytes 12582912 | tf_op jit(solution)/shard_map/gate_up/pallas_call | solution.py:69
  68.1 7.2 %gate_up.12 = f32[2,2,84,768]{3,2,1,0:T(8,128)S(1)} custom-call(s32[1]{0:T(128)} %bitcast.side_ref, bf16[84,2176]{1,0:T(8,128)(2,1)S(1)} %pad_maximum_fusion.2.rows_ref, bf16[2,2048,1536]{2,1,0:T(8,128)(2,1)} %gate_ref.15, bf16[2,2048,1536]{2,1,0:T(8,128)(2,1)} %up_ref.15), custom_call_target="tpu_custom_call" | custom-call | flops 1056964608 | bytes 12582912 | tf_op jit(solution)/shard_map/gate_up/pallas_call | solution.py:69
  75.3 7.2 %gate_up.14 = f32[2,2,84,768]{3,2,1,0:T(8,128)S(1)} custom-call(s32[1]{0:T(128)} %bitcast.side_ref, bf16[84,2176]{1,0:T(8,128)(2,1)S(1)} %pad_maximum_fusion.3.rows_ref, bf16[2,2048,1536]{2,1,0:T(8,128)(2,1)} %gate_ref.15, bf16[2,2048,1536]{2,1,0:T(8,128)(2,1)} %up_ref.15), custom_call_target="tpu_custom_call" | custom-call | flops 1056964608 | bytes 12582912 | tf_op jit(solution)/shard_map/gate_up/pallas_call | solution.py:69
  84.5 4.5 %down.8.refs_0_ = f32[84,2048]{1,0:T(8,128)S(1)} custom-call(s32[1]{0:T(128)} %bitcast.side_ref, bf16[2,84,768]{2,1,0:T(8,128)(2,1)S(1)} %fusion.11.hidden_ref, bf16[2,1536,2048]{2,1,0:T(8,128)(2,1)} %weight_ref.15), custom_call_target="tpu_custom_call" | custom-call | flops 528482304 | bytes 6291456 | tf_op jit(solution)/shard_map/down/pallas_call | solution.py:113
  90.3 1.6 %collective-permute-start.7 = (bf16[2,84,768]{2,1,0:T(8,128)(2,1)S(1)}, bf16[2,84,768]{2,1,0:T(8,128)(2,1)S(1)}, u32[]{:S(2)}, u32[]{:S(2)}) collective-permute-start(bf16[2,84,768]{2,1,0:T(8,128)(2,1)S(1)} %fusion.8.hidden_ref), channel_id=1, source_target_pairs={{0,1},{1,0},{2,3},{3,2},{4,5},{5,4},{6,7},{7,6},{8,9},{9,8},{10,11... | collective-permute-start | bytes 774152 | tf_op jit(solution)/shard_map/ppermute | solution.py:150
  96.7 4.5 %down.10.refs_0_ = f32[84,2048]{1,0:T(8,128)S(1)} custom-call(s32[1]{0:T(128)} %bitcast.side_ref, bf16[2,84,768]{2,1,0:T(8,128)(2,1)S(1)} %fusion.8.hidden_ref, bf16[2,1536,2048]{2,1,0:T(8,128)(2,1)} %weight_ref.15), custom_call_target="tpu_custom_call" | custom-call | flops 528482304 | bytes 6291456 | tf_op jit(solution)/shard_map/down/pallas_call | solution.py:113
  101.2 4.5 %down.12.refs_0_ = f32[84,2048]{1,0:T(8,128)S(1)} custom-call(s32[1]{0:T(128)} %bitcast.side_ref, bf16[2,84,768]{2,1,0:T(8,128)(2,1)S(1)} %fusion.5.hidden_ref, bf16[2,1536,2048]{2,1,0:T(8,128)(2,1)} %weight_ref.15), custom_call_target="tpu_custom_call" | custom-call | flops 528482304 | bytes 6291456 | tf_op jit(solution)/shard_map/down/pallas_call | solution.py:113
  105.8 4.6 %down.11 = f32[84,2048]{1,0:T(8,128)S(1)} custom-call(s32[1]{0:T(128)S(6)} %sub.6.side_ref, bf16[2,84,768]{2,1,0:T(8,128)(2,1)S(1)} %collective-permute-done.7.hidden_ref, bf16[2,1536,2048]{2,1,0:T(8,128)(2,1)} %weight_ref.15, f32[84,2048]{1,0:T(8,128)S(1)} %down.10.refs_0_), custom_call_target="tpu_custom_call" | custom-call | flops 528482304 | bytes 6291456 | tf_op jit(solution)/shard_map/down/pallas_call | solution.py:113
  110.5 4.5 %down.14.refs_0_ = f32[84,2048]{1,0:T(8,128)S(1)} custom-call(s32[1]{0:T(128)} %bitcast.side_ref, bf16[2,84,768]{2,1,0:T(8,128)(2,1)S(1)} %fusion.2.hidden_ref, bf16[2,1536,2048]{2,1,0:T(8,128)(2,1)} %weight_ref.15), custom_call_target="tpu_custom_call" | custom-call | flops 528482304 | bytes 6291456 | tf_op jit(solution)/shard_map/down/pallas_call | solution.py:113
  115.0 4.6 %down.9 = f32[84,2048]{1,0:T(8,128)S(1)} custom-call(s32[1]{0:T(128)S(6)} %sub.6.side_ref, bf16[2,84,768]{2,1,0:T(8,128)(2,1)S(1)} %collective-permute-done.2.hidden_ref, bf16[2,1536,2048]{2,1,0:T(8,128)(2,1)} %weight_ref.15, f32[84,2048]{1,0:T(8,128)S(1)} %down.8.refs_0_), custom_call_target="tpu_custom_call" | custom-call | flops 528482304 | bytes 6291456 | tf_op jit(solution)/shard_map/down/pallas_call | solution.py:113
  120.2 4.6 %down.13 = f32[84,2048]{1,0:T(8,128)S(1)} custom-call(s32[1]{0:T(128)S(6)} %sub.6.side_ref, bf16[2,84,768]{2,1,0:T(8,128)(2,1)S(1)} %collective-permute-done.13.hidden_ref, bf16[2,1536,2048]{2,1,0:T(8,128)(2,1)} %weight_ref.15, f32[84,2048]{1,0:T(8,128)S(1)} %down.12.refs_0_), custom_call_target="tpu_custom_call" | custom-call | flops 528482304 | bytes 6291456 | tf_op jit(solution)/shard_map/down/pallas_call | solution.py:113
  124.9 4.6 %down.15 = f32[84,2048]{1,0:T(8,128)S(1)} custom-call(s32[1]{0:T(128)S(6)} %sub.6.side_ref, bf16[2,84,768]{2,1,0:T(8,128)(2,1)S(1)} %collective-permute-done.19.hidden_ref, bf16[2,1536,2048]{2,1,0:T(8,128)(2,1)} %weight_ref.15, f32[84,2048]{1,0:T(8,128)S(1)} %down.14.refs_0_), custom_call_target="tpu_custom_call" | custom-call | flops 528482304 | bytes 6291456 | tf_op jit(solution)/shard_map/down/pallas_call | solution.py:113
  130.1 3.8 %collective-permute-start.9 = (bf16[42,2048]{1,0:T(8,128)(2,1)S(1)}, bf16[42,2048]{1,0:T(8,128)(2,1)S(1)}, u32[]{:S(2)}, u32[]{:S(2)}) collective-permute-start(bf16[42,2048]{1,0:T(8,128)(2,1)S(1)} %fusion.14), channel_id=1, source_target_pairs={{0,4},{2,6},{4,0},{6,2},{8,12},{10,14},{12,8},{14,10},{1,5},{3,7},... | collective-permute-start | bytes 516104 | tf_op jit(solution)/shard_map/ppermute | solution.py:153
  136.6 6.0 %collective-permute-done.9 = bf16[42,2048]{1,0:T(8,128)(2,1)S(1)} collective-permute-done((bf16[42,2048]{1,0:T(8,128)(2,1)S(1)}, bf16[42,2048]{1,0:T(8,128)(2,1)S(1)}, u32[]{:S(2)}, u32[]{:S(2)}) %collective-permute-start.9) | collective-permute-done | bytes 172064 | tf_op jit(solution)/shard_map/ppermute | solution.py:153
  142.6 8.6 %collective-permute-done.15 = bf16[42,2048]{1,0:T(8,128)(2,1)S(1)} collective-permute-done((bf16[42,2048]{1,0:T(8,128)(2,1)S(1)}, bf16[42,2048]{1,0:T(8,128)(2,1)S(1)}, u32[]{:S(2)}, u32[]{:S(2)}) %collective-permute-start.15) | collective-permute-done | bytes 172064 | tf_op jit(solution)/shard_map/ppermute | solution.py:153
  (77 shorter events, 25.9 us)
Async XLA Ops:
  3.4 5.8 %collective-permute-start = (bf16[42,2176]{1,0:T(8,128)(2,1)S(1)}, bf16[42,2176]{1,0:T(8,128)(2,1)S(1)}, u32[]{:S(2)}, u32[]{:S(2)}) collective-permute-start(bf16[42,2176]{1,0:T(8,128)(2,1)S(1)} %concatenate.15), channel_id=1, source_target_pairs={{0,2},{2,0},{4,6},{6,4},{8,10},{10,8},{12,14},{14,12},{1,3},{3,1},... | collective-permute-start | bytes 548360 | tf_op jit(solution)/shard_map/ppermute | solution.py:153
  3.9 15.4 %collective-permute-start.4 = (bf16[42,2176]{1,0:T(8,128)(2,1)S(1)}, bf16[42,2176]{1,0:T(8,128)(2,1)S(1)}, u32[]{:S(2)}, u32[]{:S(2)}) collective-permute-start(bf16[42,2176]{1,0:T(8,128)(2,1)S(1)} %concatenate.15), channel_id=1, source_target_pairs={{0,4},{2,6},{4,0},{6,2},{8,12},{10,14},{12,8},{14,10},{1,5},{3,7},... | collective-permute-start | bytes 548360 | tf_op jit(solution)/shard_map/ppermute | solution.py:153
  6.5 17.9 %collective-permute-start.10 = (bf16[42,2176]{1,0:T(8,128)(2,1)S(1)}, bf16[42,2176]{1,0:T(8,128)(2,1)S(1)}, u32[]{:S(2)}, u32[]{:S(2)}) collective-permute-start(bf16[42,2176]{1,0:T(8,128)(2,1)S(1)} %concatenate.15), channel_id=1, source_target_pairs={{0,8},{2,10},{4,12},{6,14},{8,0},{10,2},{12,4},{14,6},{1,9},{3,11}... | collective-permute-start | bytes 548360 | tf_op jit(solution)/shard_map/ppermute | solution.py:153
  9.1 15.3 %collective-permute-start.16 = (bf16[42,2176]{1,0:T(8,128)(2,1)S(1)}, bf16[42,2176]{1,0:T(8,128)(2,1)S(1)}, u32[]{:S(2)}, u32[]{:S(2)}) collective-permute-start(bf16[42,2176]{1,0:T(8,128)(2,1)S(1)} %concatenate.15), channel_id=1, source_target_pairs={{0,12},{2,14},{4,8},{6,10},{8,4},{10,6},{12,0},{14,2},{1,13},{3,15... | collective-permute-start | bytes 548360 | tf_op jit(solution)/shard_map/ppermute | solution.py:153
  17.6 64.9 %collective-permute-start.1 = (bf16[2,2,84,768]{3,1,2,0:T(2,128)(2,1)}, bf16[2,2,84,768]{3,1,2,0:T(2,128)(2,1)}, u32[]{:S(2)}, u32[]{:S(2)}) collective-permute-start(bf16[2,2,84,768]{3,1,2,0:T(2,128)(2,1)} %copy.60), channel_id=1, source_target_pairs={{0,1},{1,0},{2,3},{3,2},{4,5},{5,4},{6,7},{7,6},{8,9},{9,8},{10,11... | collective-permute-start | bytes 1548296 | tf_op jit(solution)/shard_map/ppermute | solution.py:150
  19.3 12.8 %collective-permute-start.5 = (bf16[42,2176]{1,0:T(8,128)(2,1)S(1)}, bf16[42,2176]{1,0:T(8,128)(2,1)S(1)}, u32[]{:S(2)}, u32[]{:S(2)}) collective-permute-start(bf16[42,2176]{1,0:T(8,128)(2,1)S(1)} %collective-permute-done.4), channel_id=1, source_target_pairs={{0,2},{2,0},{4,6},{6,4},{8,10},{10,8},{12,14},{14,12},{1,3},{3,1},... | collective-permute-start | bytes 548360 | tf_op jit(solution)/shard_map/ppermute | solution.py:153
  24.4 17.7 %collective-permute-start.11 = (bf16[42,2176]{1,0:T(8,128)(2,1)S(1)}, bf16[42,2176]{1,0:T(8,128)(2,1)S(1)}, u32[]{:S(2)}, u32[]{:S(2)}) collective-permute-start(bf16[42,2176]{1,0:T(8,128)(2,1)S(1)} %collective-permute-done.10), channel_id=1, source_target_pairs={{0,2},{2,0},{4,6},{6,4},{8,10},{10,8},{12,14},{14,12},{1,3},{3,1},... | collective-permute-start | bytes 548360 | tf_op jit(solution)/shard_map/ppermute | solution.py:153
  24.4 26.9 %collective-permute-start.17 = (bf16[42,2176]{1,0:T(8,128)(2,1)S(1)}, bf16[42,2176]{1,0:T(8,128)(2,1)S(1)}, u32[]{:S(2)}, u32[]{:S(2)}) collective-permute-start(bf16[42,2176]{1,0:T(8,128)(2,1)S(1)} %collective-permute-done.16), channel_id=1, source_target_pairs={{0,2},{2,0},{4,6},{6,4},{8,10},{10,8},{12,14},{14,12},{1,3},{3,1},... | collective-permute-start | bytes 548360 | tf_op jit(solution)/shard_map/ppermute | solution.py:153
  40.6 48.3 %collective-permute-start.6 = (bf16[2,2,84,768]{3,1,2,0:T(2,128)(2,1)}, bf16[2,2,84,768]{3,1,2,0:T(2,128)(2,1)}, u32[]{:S(2)}, u32[]{:S(2)}) collective-permute-start(bf16[2,2,84,768]{3,1,2,0:T(2,128)(2,1)} %copy.64), channel_id=1, source_target_pairs={{0,1},{1,0},{2,3},{3,2},{4,5},{5,4},{6,7},{7,6},{8,9},{9,8},{10,11... | collective-permute-start | bytes 1548296 | tf_op jit(solution)/shard_map/ppermute | solution.py:150
  50.8 41.1 %collective-permute-start.12 = (bf16[2,2,84,768]{3,1,2,0:T(2,128)(2,1)}, bf16[2,2,84,768]{3,1,2,0:T(2,128)(2,1)}, u32[]{:S(2)}, u32[]{:S(2)}) collective-permute-start(bf16[2,2,84,768]{3,1,2,0:T(2,128)(2,1)} %copy.68), channel_id=1, source_target_pairs={{0,1},{1,0},{2,3},{3,2},{4,5},{5,4},{6,7},{7,6},{8,9},{9,8},{10,11... | collective-permute-start | bytes 1548296 | tf_op jit(solution)/shard_map/ppermute | solution.py:150
  59.1 34.6 %collective-permute-start.18 = (bf16[2,2,84,768]{3,1,2,0:T(2,128)(2,1)S(1)}, bf16[2,2,84,768]{3,1,2,0:T(2,128)(2,1)}, u32[]{:S(2)}, u32[]{:S(2)}) collective-permute-start(bf16[2,2,84,768]{3,1,2,0:T(2,128)(2,1)S(1)} %copy.72), channel_id=1, source_target_pairs={{0,1},{1,0},{2,3},{3,2},{4,5},{5,4},{6,7},{7,6},{8,9},{9,8},{10,11... | collective-permute-start | bytes 1548296 | tf_op jit(solution)/shard_map/ppermute | solution.py:150
  83.9 31.2 %collective-permute-start.2 = (bf16[2,84,768]{2,1,0:T(8,128)(2,1)S(1)}, bf16[2,84,768]{2,1,0:T(8,128)(2,1)S(1)}, u32[]{:S(2)}, u32[]{:S(2)}) collective-permute-start(bf16[2,84,768]{2,1,0:T(8,128)(2,1)S(1)} %fusion.11.hidden_ref), channel_id=1, source_target_pairs={{0,1},{1,0},{2,3},{3,2},{4,5},{5,4},{6,7},{7,6},{8,9},{9,8},{10,11... | collective-permute-start | bytes 774152 | tf_op jit(solution)/shard_map/ppermute | solution.py:150
  90.3 15.5 %collective-permute-start.7 = (bf16[2,84,768]{2,1,0:T(8,128)(2,1)S(1)}, bf16[2,84,768]{2,1,0:T(8,128)(2,1)S(1)}, u32[]{:S(2)}, u32[]{:S(2)}) collective-permute-start(bf16[2,84,768]{2,1,0:T(8,128)(2,1)S(1)} %fusion.8.hidden_ref), channel_id=1, source_target_pairs={{0,1},{1,0},{2,3},{3,2},{4,5},{5,4},{6,7},{7,6},{8,9},{9,8},{10,11... | collective-permute-start | bytes 774152 | tf_op jit(solution)/shard_map/ppermute | solution.py:150
  93.2 27.0 %collective-permute-start.13 = (bf16[2,84,768]{2,1,0:T(8,128)(2,1)S(1)}, bf16[2,84,768]{2,1,0:T(8,128)(2,1)S(1)}, u32[]{:S(2)}, u32[]{:S(2)}) collective-permute-start(bf16[2,84,768]{2,1,0:T(8,128)(2,1)S(1)} %fusion.5.hidden_ref), channel_id=1, source_target_pairs={{0,1},{1,0},{2,3},{3,2},{4,5},{5,4},{6,7},{7,6},{8,9},{9,8},{10,11... | collective-permute-start | bytes 774152 | tf_op jit(solution)/shard_map/ppermute | solution.py:150
  95.1 29.8 %collective-permute-start.19 = (bf16[2,84,768]{2,1,0:T(8,128)(2,1)S(1)}, bf16[2,84,768]{2,1,0:T(8,128)(2,1)S(1)}, u32[]{:S(2)}, u32[]{:S(2)}) collective-permute-start(bf16[2,84,768]{2,1,0:T(8,128)(2,1)S(1)} %fusion.2.hidden_ref), channel_id=1, source_target_pairs={{0,1},{1,0},{2,3},{3,2},{4,5},{5,4},{6,7},{7,6},{8,9},{9,8},{10,11... | collective-permute-start | bytes 774152 | tf_op jit(solution)/shard_map/ppermute | solution.py:150
  110.4 19.6 %collective-permute-start.8 = (bf16[42,2048]{1,0:T(8,128)(2,1)S(1)}, bf16[42,2048]{1,0:T(8,128)(2,1)S(1)}, u32[]{:S(2)}, u32[]{:S(2)}) collective-permute-start(bf16[42,2048]{1,0:T(8,128)(2,1)S(1)} %slice.148), channel_id=1, source_target_pairs={{0,2},{2,0},{4,6},{6,4},{8,10},{10,8},{12,14},{14,12},{1,3},{3,1},... | collective-permute-start | bytes 516104 | tf_op jit(solution)/shard_map/ppermute | solution.py:153
  119.7 16.9 %collective-permute-start.3 = (bf16[42,2048]{1,0:T(8,128)(2,1)S(1)}, bf16[42,2048]{1,0:T(8,128)(2,1)S(1)}, u32[]{:S(2)}, u32[]{:S(2)}) collective-permute-start(bf16[42,2048]{1,0:T(8,128)(2,1)S(1)} %slice.149), channel_id=1, source_target_pairs={{0,2},{2,0},{4,6},{6,4},{8,10},{10,8},{12,14},{14,12},{1,3},{3,1},... | collective-permute-start | bytes 516104 | tf_op jit(solution)/shard_map/ppermute | solution.py:153
  124.8 9.1 %collective-permute-start.14 = (bf16[42,2048]{1,0:T(8,128)(2,1)S(1)}, bf16[42,2048]{1,0:T(8,128)(2,1)S(1)}, u32[]{:S(2)}, u32[]{:S(2)}) collective-permute-start(bf16[42,2048]{1,0:T(8,128)(2,1)S(1)} %slice.147), channel_id=1, source_target_pairs={{0,2},{2,0},{4,6},{6,4},{8,10},{10,8},{12,14},{14,12},{1,3},{3,1},... | collective-permute-start | bytes 516104 | tf_op jit(solution)/shard_map/ppermute | solution.py:153
  129.5 5.5 %collective-permute-start.20 = (bf16[42,2048]{1,0:T(8,128)(2,1)S(1)}, bf16[42,2048]{1,0:T(8,128)(2,1)S(1)}, u32[]{:S(2)}, u32[]{:S(2)}) collective-permute-start(bf16[42,2048]{1,0:T(8,128)(2,1)S(1)} %slice.146), channel_id=1, source_target_pairs={{0,2},{2,0},{4,6},{6,4},{8,10},{10,8},{12,14},{14,12},{1,3},{3,1},... | collective-permute-start | bytes 516104 | tf_op jit(solution)/shard_map/ppermute | solution.py:153
  130.1 12.5 %collective-permute-start.9 = (bf16[42,2048]{1,0:T(8,128)(2,1)S(1)}, bf16[42,2048]{1,0:T(8,128)(2,1)S(1)}, u32[]{:S(2)}, u32[]{:S(2)}) collective-permute-start(bf16[42,2048]{1,0:T(8,128)(2,1)S(1)} %fusion.14), channel_id=1, source_target_pairs={{0,4},{2,6},{4,0},{6,2},{8,12},{10,14},{12,8},{14,10},{1,5},{3,7},... | collective-permute-start | bytes 516104 | tf_op jit(solution)/shard_map/ppermute | solution.py:153
  134.0 17.2 %collective-permute-start.15 = (bf16[42,2048]{1,0:T(8,128)(2,1)S(1)}, bf16[42,2048]{1,0:T(8,128)(2,1)S(1)}, u32[]{:S(2)}, u32[]{:S(2)}) collective-permute-start(bf16[42,2048]{1,0:T(8,128)(2,1)S(1)} %fusion.13), channel_id=1, source_target_pairs={{0,8},{2,10},{4,12},{6,14},{8,0},{10,2},{12,4},{14,6},{1,9},{3,11}... | collective-permute-start | bytes 516104 | tf_op jit(solution)/shard_map/ppermute | solution.py:153
  135.1 16.1 %collective-permute-start.21 = (bf16[42,2048]{1,0:T(8,128)(2,1)S(1)}, bf16[42,2048]{1,0:T(8,128)(2,1)S(1)}, u32[]{:S(2)}, u32[]{:S(2)}) collective-permute-start(bf16[42,2048]{1,0:T(8,128)(2,1)S(1)} %fusion.12), channel_id=1, source_target_pairs={{0,12},{2,14},{4,8},{6,10},{8,4},{10,6},{12,0},{14,2},{1,13},{3,15... | collective-permute-start | bytes 516104 | tf_op jit(solution)/shard_map/ppermute | solution.py:153

commit v2 on v0

--- a/solution.py
+++ b/solution.py
@@ -1,7 +1,26 @@
+import functools
+
 import jax
 import jax.numpy as jnp
 from jax import lax
+from jax.experimental import pallas as pl
+from jax.experimental.pallas import tpu as pltpu
 from jax.sharding import PartitionSpec as P
+
+CORES = 2
+EXTRA = 128
+SMALL = 6 * 1024 * 1024
+VMEM_SPEC = pl.BlockSpec(memory_space=pltpu.VMEM)
+SMEM_SPEC = pl.BlockSpec(memory_space=pltpu.SMEM)
+ANY_SPEC = pl.BlockSpec(memory_space=pl.ANY)
+
+
+def in_hbm(value):
+    return pltpu.with_memory_space_constraint(value, pltpu.HBM)
+
+
+def in_vmem(value):
+    return pltpu.with_memory_space_constraint(value, pltpu.VMEM)
 
 
 def slot_targets(chosen_ids, total_experts, capacity):
@@ -13,7 +32,7 @@
     return chosen_ids * capacity + jnp.take_along_axis(before, chosen_ids, axis=1)
 
 
-def shards(tokens, route_ids, route_scores, w_gate, w_up, w_down):
+def general_shards(tokens, route_ids, route_scores, w_gate, w_up, w_down):
     groups = lax.axis_size("expert")
     local_experts = w_gate.shape[0]
     count_rows = route_ids.shape[0]
@@ -46,7 +65,296 @@
     return combined.astype(jnp.bfloat16)
 
 
+def prepare_kernel(tokens_ref, ids_ref, scores_ref, out_ref):
+    count, width = tokens_ref.shape
+    top = ids_ref.shape[1]
+    scores = scores_ref[...]
+    weights = scores / jnp.sum(scores, axis=1, keepdims=True)
+    lane = lax.broadcasted_iota(jnp.int32, (count, EXTRA), 1)
+    ids = ids_ref[...]
+    share = jnp.zeros((count, EXTRA), jnp.float32)
+    for k in range(top):
+        chosen = ids[:, k : k + 1]
+        match = (lane == chosen) | (lane == chosen + EXTRA // 2)
+        share = share + jnp.where(match, weights[:, k : k + 1], 0.0)
+    high = share.astype(jnp.bfloat16).astype(jnp.float32)
+    out_ref[:, :width] = tokens_ref[...]
+    out_ref[:, width:] = jnp.where(lane < EXTRA // 2, high, share - high).astype(jnp.bfloat16)
+
+
+def prepare(tokens, ids, scores):
+    count, width = tokens.shape
+    return pl.pallas_call(
+        prepare_kernel,
+        in_specs=[VMEM_SPEC] * 3,
+        out_specs=VMEM_SPEC,
+        out_shape=jax.ShapeDtypeStruct((count, width + EXTRA), jnp.bfloat16),
+        compiler_params=pltpu.CompilerParams(vmem_limit_bytes=SMALL),
+        name="prepare",
+    )(tokens, ids, scores)
+
+
+def project(rows_ref, held, out_ref, expert, which, start, size):
+    width, half = held.shape[1:]
+    place = (2 * expert + which) * half + start
+    out_ref[:, place : place + size] = jnp.dot(
+        rows_ref[:, :width], held[expert, :, start : start + size], preferred_element_type=jnp.float32
+    ).astype(out_ref.dtype)
+
+
+def gate_up_load_kernel(compute, side_ref, rows_ref, gate_ref, up_ref, *refs):
+    gate_held, up_held, sem = refs[-3:]
+    experts, _, half = gate_held.shape
+    tile = half // 2
+    base = side_ref[0] * half
+    work = []
+    for e in range(experts):
+        for which, source, held in ((0, gate_ref, gate_held), (1, up_ref, up_held)):
+            for start in range(0, half, tile):
+                copy = pltpu.make_async_copy(
+                    source.at[e, :, pl.ds(pl.multiple_of(base + start, 128), tile)],
+                    held.at[e, :, pl.ds(start, tile)],
+                    sem.at[len(work)],
+                )
+                copy.start()
+                work.append((copy, held, e, which, start))
+    for copy, held, e, which, start in work:
+        copy.wait()
+        if compute:
+            project(rows_ref, held, refs[-4], e, which, start, tile)
+
+
+def gate_up_load(side, rows, w_gate, w_up, after, dtype=None):
+    count = rows.shape[0]
+    experts, width, units = w_gate.shape
+    half = units // 2
+    compute = dtype is not None
+    held = pltpu.VMEM((experts, width, half), w_gate.dtype)
+    out = [jax.ShapeDtypeStruct((count, 2 * experts * half), dtype)] if compute else []
+    return pl.pallas_call(
+        functools.partial(gate_up_load_kernel, compute),
+        in_specs=[SMEM_SPEC, VMEM_SPEC if compute else ANY_SPEC] + [ANY_SPEC] * (2 + len(after)),
+        out_specs=[VMEM_SPEC] * (2 + len(out)),
+        out_shape=out + [held, held],
+        scratch_shapes=[pltpu.SemaphoreType.DMA((4 * experts,))],
+        compiler_params=pltpu.CompilerParams(vmem_limit_bytes=SMALL),
+        cost_estimate=pl.CostEstimate(
+            flops=4 * count * width * half * experts,
+            bytes_accessed=4 * experts * width * half,
+            transcendentals=0,
+        ),
+        name="gate_up_load",
+    )(side, rows, in_hbm(w_gate), in_hbm(w_up), *after)
+
+
+def gate_up_kernel(rows_ref, gate_held, up_held, *refs):
+    out_ref = refs[-1]
+    experts, _, half = gate_held.shape
+    tile = half // 3
+    for e in range(experts):
+        for which, held in ((0, gate_held), (1, up_held)):
+            for start in range(0, half, tile):
+                project(rows_ref, held, out_ref, e, which, start, tile)
+
+
+def gate_up(rows, gate_held, up_held, dtype, after):
+    count = rows.shape[0]
+    experts, width, half = gate_held.shape
+    return pl.pallas_call(
+        gate_up_kernel,
+        in_specs=[VMEM_SPEC] * 3 + [ANY_SPEC] * len(after),
+        out_specs=VMEM_SPEC,
+        out_shape=jax.ShapeDtypeStruct((count, 2 * experts * half), dtype),
+        compiler_params=pltpu.CompilerParams(vmem_limit_bytes=SMALL),
+        cost_estimate=pl.CostEstimate(
+            flops=4 * max(count, 256) * width * half * experts,
+            bytes_accessed=0,
+            transcendentals=0,
+        ),
+        name="gate_up",
+    )(rows, in_vmem(gate_held), in_vmem(up_held), *after)
+
+
+def hidden_kernel(experts, here_ref, rows_ref, kept_ref, received_ref, *refs):
+    out_ref = refs[-1]
+    count = rows_ref.shape[0]
+    half = kept_ref.shape[1] // (2 * experts)
+    width = rows_ref.shape[1] - EXTRA
+    share = rows_ref[:, width:].astype(jnp.float32)
+    lane = lax.broadcasted_iota(jnp.int32, (count, EXTRA), 1)
+
+    def full(index):
+        columns = slice(index * half, (index + 1) * half)
+        return kept_ref[:, columns] + received_ref[:, columns].astype(jnp.float32)
+
+    for e in range(experts):
+        expert = here_ref[0] * experts + e
+        match = (lane == expert) | (lane == expert + EXTRA // 2)
+        own = jnp.sum(jnp.where(match, share, 0.0), axis=1, keepdims=True)
+        gate, up = full(2 * e), full(2 * e + 1)
+        value = gate / (1.0 + jnp.exp(-gate)) * up * own
+        out_ref[:, e * half : (e + 1) * half] = value.astype(out_ref.dtype)
+
+
+def hidden_of(here, rows, kept, received, experts, after):
+    count = kept.shape[0]
+    half = kept.shape[1] // (2 * experts)
+    return pl.pallas_call(
+        functools.partial(hidden_kernel, experts),
+        in_specs=[SMEM_SPEC] + [VMEM_SPEC] * 3 + [ANY_SPEC] * len(after),
+        out_specs=VMEM_SPEC,
+        out_shape=jax.ShapeDtypeStruct((count, experts * half), jnp.bfloat16),
+        compiler_params=pltpu.CompilerParams(vmem_limit_bytes=SMALL),
+        cost_estimate=pl.CostEstimate(
+            flops=8 * count * half * experts,
+            bytes_accessed=0,
+            transcendentals=count * half * experts,
+        ),
+        name="hidden",
+    )(here, rows, kept, received, *after)
+
+
+def down_kernel(load, more, n_after, *refs):
+    refs = list(refs)
+    side_ref = refs.pop(0) if load else None
+    hidden_ref, weight_ref = refs.pop(0), refs.pop(0)
+    so_far = refs.pop(0) if more else None
+    refs = refs[n_after:]
+    out_ref = refs.pop(0)
+    held, sem = refs if load else (weight_ref, None)
+    experts, half, width = held.shape
+    tile = width // 4
+    copies = []
+    if load:
+        base = pl.multiple_of(side_ref[0] * half, 256)
+        for index in range(4):
+            for e in range(experts):
+                columns = pl.ds(index * tile, tile)
+                copy = pltpu.make_async_copy(
+                    weight_ref.at[e, pl.ds(base, half), columns],
+                    held.at[e, :, columns],
+                    sem.at[len(copies)],
+                )
+                copy.start()
+                copies.append(copy)
+    for index in range(4):
+        columns = slice(index * tile, (index + 1) * tile)
+        value = so_far[:, columns] if more else None
+        for e in range(experts):
+            if load:
+                copies[index * experts + e].wait()
+            product = jnp.dot(
+                hidden_ref[:, e * half : (e + 1) * half],
+                held[e, :, columns],
+                preferred_element_type=jnp.float32,
+            )
+            value = product if value is None else value + product
+        out_ref[:, columns] = value.astype(out_ref.dtype)
+
+
+def down(hidden, so_far, dtype, after, held=None, side=None, weight=None):
+    count = hidden.shape[0]
+    load = weight is not None
+    more = so_far is not None
+    experts, depth, width = (weight if load else held).shape
+    half = depth // 2 if load else depth
+    out = jax.ShapeDtypeStruct((count, width), dtype)
+    operands = [side, hidden, in_hbm(weight)] if load else [hidden, in_vmem(held)]
+    specs = [SMEM_SPEC, VMEM_SPEC, ANY_SPEC] if load else [VMEM_SPEC] * 2
+    if more:
+        operands.append(so_far)
+        specs.append(VMEM_SPEC)
+    operands += after
+    specs += [ANY_SPEC] * len(after)
+    return pl.pallas_call(
+        functools.partial(down_kernel, load, more, len(after)),
+        in_specs=specs,
+        out_specs=[VMEM_SPEC] * 2 if load else VMEM_SPEC,
+        out_shape=[out, pltpu.VMEM((experts, half, width), weight.dtype)] if load else out,
+        scratch_shapes=[pltpu.SemaphoreType.DMA((4 * experts,))] if load else [],
+        compiler_params=pltpu.CompilerParams(vmem_limit_bytes=SMALL),
+        cost_estimate=pl.CostEstimate(
+            flops=2 * max(count, 256) * width * half * experts,
+            bytes_accessed=2 * experts * width * half if load else 0,
+            transcendentals=0,
+        ),
+        name="down_load" if load else "down",
+    )(*operands)
+
+
+def pair_shards(tokens, route_ids, route_scores, w_gate, w_up, w_down):
+    groups = lax.axis_size("expert")
+    local_experts = w_gate.shape[0]
+    count, width = tokens.shape
+    chips = groups // CORES
+    here = lax.axis_index("expert").reshape(1)
+    mine = lax.axis_index("tensor").reshape(1)
+    other = 1 - mine
+    bf16, f32 = jnp.bfloat16, jnp.float32
+
+    def swap_tensor(value):
+        return lax.ppermute(value, "tensor", [(0, 1), (1, 0)])
+
+    def swap_expert(value, mask):
+        return lax.ppermute(value, "expert", [(i, i ^ mask) for i in range(groups)])
+
+    own = prepare(tokens, route_ids, route_scores)
+    steps = [0] + list(range(chips - 1, 0, -1))
+    chunks = []
+    for step in steps:
+        same = swap_expert(own, CORES * step) if step else own
+        chunks.append(jnp.concatenate([same, swap_expert(same, 1)], axis=0))
+    total = len(chunks)
+
+    gate_other, up_other = gate_up_load(other, own, w_gate, w_up, [])
+    theirs, received, kept, hidden, arrived, begun, outs = {}, {}, {}, {}, {}, {}, {}
+
+    def send_theirs(i, after):
+        theirs[i] = gate_up(chunks[i], gate_other, up_other, bf16, after)
+        received[i] = swap_tensor(theirs[i])
+        return [theirs[i]]
+
+    def send_hidden(i, after):
+        hidden[i] = hidden_of(here, chunks[i], kept[i], received[i], local_experts, after)
+        arrived[i] = swap_tensor(hidden[i])
+        return [hidden[i]]
+
+    after = send_theirs(0, [])
+    kept[0], gate_mine, up_mine = gate_up_load(mine, chunks[0], w_gate, w_up, after, f32)
+    after = [kept[0]]
+    for i in range(total):
+        if i + 1 < total:
+            after = send_theirs(i + 1, after)
+        after = send_hidden(i, after)
+        if i:
+            outs[i - 1] = down(arrived[i - 1], begun[i - 1], bf16, after, **late)
+            if i == 1:
+                outs[0], down_other = outs[0]
+                late = dict(held=down_other)
+            after = [outs[i - 1]]
+        early = dict(held=down_mine) if i else dict(side=mine, weight=w_down)
+        begun[i] = down(hidden[i], None, f32, after, **early)
+        if i == 0:
+            begun[0], down_mine = begun[0]
+            late = dict(side=other, weight=w_down)
+        after = [begun[i]]
+        if i + 1 < total:
+            kept[i + 1] = gate_up(chunks[i + 1], gate_mine, up_mine, f32, after)
+            after = [kept[i + 1]]
+    outs[total - 1] = down(arrived[total - 1], begun[total - 1], bf16, after, **late)
+    result = None
+    for i, step in enumerate(steps):
+        from_core = swap_expert(outs[i][count:], 1)
+        part = outs[i][:count].astype(f32) + from_core.astype(f32)
+        if step:
+            part = swap_expert(part.astype(bf16), CORES * step).astype(f32)
+        result = part if result is None else result + part
+    return result.astype(bf16)
+
+
 def solution(mesh):
+    groups = mesh.shape["expert"]
+    paired = mesh.shape["tensor"] == 2 and groups % CORES == 0 and groups & (groups - 1) == 0
     placed = (
         P(("replica", "expert"), "tensor"),
         P(("replica", "expert"), None),
@@ -56,7 +364,7 @@
         P("expert", None, "tensor"),
     )
     return jax.shard_map(
-        shards,
+        pair_shards if paired else general_shards,
         mesh=mesh,
         in_specs=placed,
         out_specs=P(("replica", "expert"), "tensor"),

time: 512 us -> 111 us (0.22)
  waiting for transfers between devices: 342 us -> 42.2 us
  blocking collectives: 69.5 us -> 0 us
  local copies, waits for them, and re-layouts: 48.5 us -> 2.67 us
  Pallas kernels: 0 us -> 39.8 us
  matrix products: 29 us -> 0 us
  starting transfers between devices: 5.05 us -> 24.9 us
  between operations: 13.6 us -> 0.24 us
    psum x1 -> x0, waiting for transfers between devices: 220 us -> none  [shards(): gate_full, up_full = lax.psum((gate_part, up_part), 'tensor')]
    all_to_all x1 -> x0, waiting for transfers between devices: 121 us -> none  [shards(): lax.all_to_all(produced, 'expert', split_axis=0, concat_axis=0, tiled=True)]
    all_to_all x1 -> x0, blocking collectives: 69.5 us -> none  [shards(): lax.all_to_all(outgoing, 'expert', split_axis=0, concat_axis=0, tiled=True)]
    ppermute x0 -> x22, waiting for transfers between devices: none -> 42.2 us  [the longest x8 23.5 us: swap_tensor(): return lax.ppermute(value, 'tensor', [(0, 1), (1, 0)])]
    pallas_call x0 -> x22, Pallas kernels: none -> 39.8 us  [the longest x7 15.1 us: gate_up(): pl.pallas_call(gate_up_kernel, in_specs=[VMEM_SPEC] * 3 + [ANY_SPEC] * le...]
    dot_general x3 -> x0, matrix products: 29 us -> none  [the longest x1 11 us: shards(): jnp.einsum('nech,ehd->necd', hidden, w_down, preferred_element_type=jnp.f...]
    ppermute x0 -> x22, starting transfers between devices: none -> 24.9 us  [the longest x14 13.2 us: swap_expert(): return lax.ppermute(value, 'expert', [(i, i ^ mask) for i in range(groups)])]
    gather x8 -> x0, local copies, waits for them, and re-layouts: 18.3 us -> none  [the longest x2 6.98 us: shards(): jnp.take(tokens, source_row, axis=0) * filled[:, None]]
  transfers between devices with their start and end apart: 2 -> 22, of which waited for: 2 -> 11; matrix products, arithmetic and copies ran while one was open for 0% -> 1% of each run, Pallas kernels for 0% -> 36%
where the time goes in v2:
time: 111 us
  waiting for transfers between devices  42.2 us (38%)
  Pallas kernels  39.8 us (36%)
  starting transfers between devices  24.9 us (22%)
  local copies, waits for them, and re-layouts  2.67 us (2%)
  other arithmetic  1.21 us (1%)
    ppermute x8, waiting for transfers between devices, swap_tensor(): return lax.ppermute(value, 'tensor', [(0, 1), (1, 0)])  23.5 us
    ppermute x14, waiting for transfers between devices, swap_expert(): return lax.ppermute(value, 'expert', [(i, i ^ mask) for i in range(groups)])  18.8 us
    pallas_call x7, Pallas kernels, gate_up(): pl.pallas_call(gate_up_kernel, in_specs=[VMEM_SPEC] * 3 + [ANY_SPEC] * le...  15.1 us
    pallas_call x8, Pallas kernels, down(): pl.pallas_call(functools.partial(down_kernel, load, more, len(after)), in...  13.4 us
    ppermute x14, starting transfers between devices, swap_expert(): return lax.ppermute(value, 'expert', [(i, i ^ mask) for i in range(groups)])  13.2 us
    ppermute x8, starting transfers between devices, swap_tensor(): return lax.ppermute(value, 'tensor', [(0, 1), (1, 0)])  11.8 us
    pallas_call x2, Pallas kernels, gate_up_load(): pl.pallas_call(functools.partial(gate_up_load_kernel, compute), in_specs=...  10.1 us
    unnamed x4, local copies, waits for them, and re-layouts  2.48 us
  transfers between devices with their start and end apart: 22, of which 11 were waited for; matrix products, arithmetic and copies ran while one was open for 1% of the time, Pallas kernels for 36%

profile of v2, /device:TPU:0, one launch (start us, length us, event | category | flops | bytes accessed | tf_op | source)
XLA Modules:
  0.0 111.1 jit_solution(1182611747501111370)
XLA Ops:
  3.3 4.7 %collective-permute-start.2 = (bf16[42,2176]{1,0:T(8,128)(2,1)S(1)}, bf16[42,2176]{1,0:T(8,128)(2,1)S(1)}, u32[]{:S(2)}, u32[]{:S(2)}) collective-permute-start(bf16[42,2176]{1,0:T(8,128)(2,1)S(1)} %prepare.1.rows_ref), channel_id=1, source_target_pairs={{0,12},{2,14},{4,8},{6,10},{8,4},{10,6},{12,0},{14,2},{1,13},{3,15... | collective-permute-start | bytes 548360 | tf_op jit(solution)/shard_map/ppermute | solution.py:299
  8.6 4.8 %gate_up_load.2 = (bf16[2,2048,768]{2,1,0:T(8,128)(2,1)S(1)}, bf16[2,2048,768]{2,1,0:T(8,128)(2,1)S(1)}) custom-call(s32[1]{0:T(128)S(6)} %sub.3.side_ref.refs_0_, bf16[42,2176]{1,0:T(8,128)(2,1)S(1)} %prepare.1.rows_ref, bf16[2,2048,1536]{2,1,0:T(8,128)(2,1)} %gate_ref.3, bf16[2,2048,1536]{2,1,0:T(8,128)(2,1)} %up_ref.3), custom_call_target="tpu_custom_call" | custom-call | flops 528482304 | bytes 12582912 | tf_op jit(solution)/shard_map/gate_up_load/pallas_call | solution.py:134
  14.1 2.2 %gate_up.7.refs_0_ = bf16[84,3072]{1,0:T(8,128)(2,1)S(1)} custom-call(bf16[84,2176]{1,0:T(8,128)(2,1)S(1)} %pad_maximum_fusion.rows_ref, bf16[2,2048,768]{2,1,0:T(8,128)(2,1)S(1)} %get-tuple-element.14.gate_held, bf16[2,2048,768]{2,1,0:T(8,128)(2,1)S(1)} %get-tuple-element.15.up_held), custom_call_target="tpu_custom_call" | custom-call | flops 3221225472 | tf_op jit(solution)/shard_map/gate_up/pallas_call | solution.py:163
  16.3 1.7 %collective-permute-start.1 = (bf16[84,3072]{1,0:T(8,128)(2,1)S(1)}, bf16[84,3072]{1,0:T(8,128)(2,1)S(1)}, u32[]{:S(2)}, u32[]{:S(2)}) collective-permute-start(bf16[84,3072]{1,0:T(8,128)(2,1)S(1)} %gate_up.7.refs_0_), channel_id=1, source_target_pairs={{0,1},{1,0},{2,3},{3,2},{4,5},{5,4},{6,7},{7,6},{8,9},{9,8},{10,11... | collective-permute-start | bytes 1548296 | tf_op jit(solution)/shard_map/ppermute | solution.py:296
  18.0 8.3 %collective-permute-done.6 = bf16[42,2176]{1,0:T(8,128)(2,1)S(1)} collective-permute-done((bf16[42,2176]{1,0:T(8,128)(2,1)S(1)}, bf16[42,2176]{1,0:T(8,128)(2,1)S(1)}, u32[]{:S(2)}, u32[]{:S(2)}) %collective-permute-start.6) | collective-permute-done | bytes 182816 | tf_op jit(solution)/shard_map/ppermute | solution.py:299
  26.8 5.3 %gate_up_load.3 = (f32[84,3072]{1,0:T(8,128)S(1)}, bf16[2,2048,768]{2,1,0:T(8,128)(2,1)S(1)}, bf16[2,2048,768]{2,1,0:T(8,128)(2,1)S(1)}) custom-call(s32[1]{0:T(128)} %bitcast.side_ref.refs_0_, bf16[84,2176]{1,0:T(8,128)(2,1)S(1)} %pad_maximum_fusion.rows_ref, bf16[2,2048,1536]{2,1,0:T(8,128)(2,1)} %gate_ref.3, bf16[2,2048,1536]{2,1,0:T(8,128)(2,1)} %up_ref.3, ...), custom_call_target="tpu_custom_call" | custom-call | flops 1056964608 | bytes 12582912 | tf_op jit(solution)/shard_map/gate_up_load/pallas_call | solution.py:134
  32.2 2.2 %gate_up.8.refs_0_ = bf16[84,3072]{1,0:T(8,128)(2,1)S(1)} custom-call(bf16[84,2176]{1,0:T(8,128)(2,1)S(1)} %pad_maximum_fusion.1.rows_ref, bf16[2,2048,768]{2,1,0:T(8,128)(2,1)S(1)} %get-tuple-element.14.gate_held, bf16[2,2048,768]{2,1,0:T(8,128)(2,1)S(1)} %get-tuple-element.15.up_held, f32[84,3072]{1,0:T(8,128)S(1)} %get-tuple-element.16.refs_0_.kept_ref), custom_call_target="tpu_custom_call" | custom-call | flops 3221225472 | tf_op jit(solution)/shard_map/gate_up/pallas_call | solution.py:163
  36.9 3.3 %down_load.2 = (f32[84,2048]{1,0:T(8,128)S(1)}, bf16[2,768,2048]{2,1,0:T(8,128)(2,1)S(1)}) custom-call(s32[1]{0:T(128)} %bitcast.side_ref.refs_0_, bf16[84,1536]{1,0:T(8,128)(2,1)S(1)} %hidden.4.refs_1_.refs_3_, bf16[2,1536,2048]{2,1,0:T(8,128)(2,1)} %refs_2_.3, bf16[84,1536]{1,0:T(8,128)(2,1)S(1)} %hidden.4.refs_1_.refs_3_), custom_call_target="tpu_custom_call" | custom-call | flops 1610612736 | bytes 6291456 | tf_op jit(solution)/shard_map/down_load/pallas_call | solution.py:269
  40.2 2.2 %gate_up.9.refs_0_.kept_ref = f32[84,3072]{1,0:T(8,128)S(1)} custom-call(bf16[84,2176]{1,0:T(8,128)(2,1)S(1)} %pad_maximum_fusion.1.rows_ref, bf16[2,2048,768]{2,1,0:T(8,128)(2,1)S(1)} %get-tuple-element.18.gate_held, bf16[2,2048,768]{2,1,0:T(8,128)(2,1)S(1)} %get-tuple-element.19.up_held, f32[84,2048]{1,0:T(8,128)S(1)} %get-tuple-element.17.refs_0_.refs_3_), custom_call_target="tpu_custom_call" | custom-call | flops 3221225472 | tf_op jit(solution)/shard_map/gate_up/pallas_call | solution.py:163
  42.4 2.1 %gate_up.10.refs_0_ = bf16[84,3072]{1,0:T(8,128)(2,1)S(1)} custom-call(bf16[84,2176]{1,0:T(8,128)(2,1)S(1)} %pad_maximum_fusion.2.rows_ref, bf16[2,2048,768]{2,1,0:T(8,128)(2,1)S(1)} %get-tuple-element.14.gate_held, bf16[2,2048,768]{2,1,0:T(8,128)(2,1)S(1)} %get-tuple-element.15.up_held, f32[84,3072]{1,0:T(8,128)S(1)} %gate_up.9.refs_0_.kept_ref), custom_call_target="tpu_custom_call" | custom-call | flops 3221225472 | tf_op jit(solution)/shard_map/gate_up/pallas_call | solution.py:163
  44.5 1.7 %collective-permute-start.10 = (bf16[84,3072]{1,0:T(8,128)(2,1)S(1)}, bf16[84,3072]{1,0:T(8,128)(2,1)S(1)}, u32[]{:S(2)}, u32[]{:S(2)}) collective-permute-start(bf16[84,3072]{1,0:T(8,128)(2,1)S(1)} %gate_up.10.refs_0_), channel_id=1, source_target_pairs={{0,1},{1,0},{2,3},{3,2},{4,5},{5,4},{6,7},{7,6},{8,9},{9,8},{10,11... | collective-permute-start | bytes 1548296 | tf_op jit(solution)/shard_map/ppermute | solution.py:296
  46.3 3.3 %collective-permute-done.5.received_ref = bf16[84,3072]{1,0:T(8,128)(2,1)S(1)} collective-permute-done((bf16[84,3072]{1,0:T(8,128)(2,1)S(1)}, bf16[84,3072]{1,0:T(8,128)(2,1)S(1)}, u32[]{:S(2)}, u32[]{:S(2)}) %collective-permute-start.5) | collective-permute-done | bytes 516128 | tf_op jit(solution)/shard_map/ppermute | solution.py:296
  51.4 4.0 %collective-permute-done.4.refs_1_ = bf16[84,1536]{1,0:T(8,128)(2,1)S(1)} collective-permute-done((bf16[84,1536]{1,0:T(8,128)(2,1)S(1)}, bf16[84,1536]{1,0:T(8,128)(2,1)S(1)}, u32[]{:S(2)}, u32[]{:S(2)}) %collective-permute-start.4) | collective-permute-done | bytes 258080 | tf_op jit(solution)/shard_map/ppermute | solution.py:296
  55.4 3.2 %down_load.3 = (bf16[84,2048]{1,0:T(8,128)(2,1)S(1)}, bf16[2,768,2048]{2,1,0:T(8,128)(2,1)S(1)}) custom-call(s32[1]{0:T(128)S(6)} %sub.3.side_ref.refs_0_, bf16[84,1536]{1,0:T(8,128)(2,1)S(1)} %collective-permute-done.4.refs_1_, bf16[2,1536,2048]{2,1,0:T(8,128)(2,1)} %refs_2_.3, f32[84,2048]{1,0:T(8,128)S(1)} %get-tuple-element.17.refs_0_.refs_3_, ...), custom_call_target="tpu_custom_call" | custom-call | flops 1610612736 | bytes 6291456 | tf_op jit(solution)/shard_map/down_load/pallas_call | solution.py:269
  59.8 2.1 %gate_up.11.refs_0_.kept_ref = f32[84,3072]{1,0:T(8,128)S(1)} custom-call(bf16[84,2176]{1,0:T(8,128)(2,1)S(1)} %pad_maximum_fusion.2.rows_ref, bf16[2,2048,768]{2,1,0:T(8,128)(2,1)S(1)} %get-tuple-element.18.gate_held, bf16[2,2048,768]{2,1,0:T(8,128)(2,1)S(1)} %get-tuple-element.19.up_held, f32[84,2048]{1,0:T(8,128)S(1)} %down.6.refs_0_.refs_2_), custom_call_target="tpu_custom_call" | custom-call | flops 3221225472 | tf_op jit(solution)/shard_map/gate_up/pallas_call | solution.py:163
  61.9 2.2 %gate_up.12.refs_0_ = bf16[84,3072]{1,0:T(8,128)(2,1)S(1)} custom-call(bf16[84,2176]{1,0:T(8,128)(2,1)S(1)} %pad_maximum_fusion.3.rows_ref, bf16[2,2048,768]{2,1,0:T(8,128)(2,1)S(1)} %get-tuple-element.14.gate_held, bf16[2,2048,768]{2,1,0:T(8,128)(2,1)S(1)} %get-tuple-element.15.up_held, f32[84,3072]{1,0:T(8,128)S(1)} %gate_up.11.refs_0_.kept_ref), custom_call_target="tpu_custom_call" | custom-call | flops 3221225472 | tf_op jit(solution)/shard_map/gate_up/pallas_call | solution.py:163
  67.2 5.5 %collective-permute-done.9.refs_0_ = bf16[84,1536]{1,0:T(8,128)(2,1)S(1)} collective-permute-done((bf16[84,1536]{1,0:T(8,128)(2,1)S(1)}, bf16[84,1536]{1,0:T(8,128)(2,1)S(1)}, u32[]{:S(2)}, u32[]{:S(2)}) %collective-permute-start.9) | collective-permute-done | bytes 258080 | tf_op jit(solution)/shard_map/ppermute | solution.py:296
  76.7 2.2 %gate_up.13.kept_ref.refs_0_ = f32[84,3072]{1,0:T(8,128)S(1)} custom-call(bf16[84,2176]{1,0:T(8,128)(2,1)S(1)} %pad_maximum_fusion.3.rows_ref, bf16[2,2048,768]{2,1,0:T(8,128)(2,1)S(1)} %get-tuple-element.18.gate_held, bf16[2,2048,768]{2,1,0:T(8,128)(2,1)S(1)} %get-tuple-element.19.up_held, f32[84,2048]{1,0:T(8,128)S(1)} %down.8.refs_0_.refs_2_), custom_call_target="tpu_custom_call" | custom-call | flops 3221225472 | tf_op jit(solution)/shard_map/gate_up/pallas_call | solution.py:163
  79.0 2.5 %collective-permute-start.14 = (bf16[42,2048]{1,0:T(8,128)(2,1)S(1)}, bf16[42,2048]{1,0:T(8,128)(2,1)S(1)}, u32[]{:S(2)}, u32[]{:S(2)}) collective-permute-start(bf16[42,2048]{1,0:T(8,128)(2,1)S(1)} %add_convert_fusion.3), channel_id=1, source_target_pairs={{0,12},{2,14},{4,8},{6,10},{8,4},{10,6},{12,0},{14,2},{1,13},{3,15... | collective-permute-start | bytes 516104 | tf_op jit(solution)/shard_map/ppermute | solution.py:299
  81.5 2.9 %collective-permute-done.16.received_ref = bf16[84,3072]{1,0:T(8,128)(2,1)S(1)} collective-permute-done((bf16[84,3072]{1,0:T(8,128)(2,1)S(1)}, bf16[84,3072]{1,0:T(8,128)(2,1)S(1)}, u32[]{:S(2)}, u32[]{:S(2)}) %collective-permute-start.16) | collective-permute-done | bytes 516128 | tf_op jit(solution)/shard_map/ppermute | solution.py:296
  86.1 4.0 %collective-permute-done.15.refs_0_ = bf16[84,1536]{1,0:T(8,128)(2,1)S(1)} collective-permute-done((bf16[84,1536]{1,0:T(8,128)(2,1)S(1)}, bf16[84,1536]{1,0:T(8,128)(2,1)S(1)}, u32[]{:S(2)}, u32[]{:S(2)}) %collective-permute-start.15) | collective-permute-done | bytes 258080 | tf_op jit(solution)/shard_map/ppermute | solution.py:296
  92.6 2.4 %collective-permute-done.19.refs_0_ = bf16[84,1536]{1,0:T(8,128)(2,1)S(1)} collective-permute-done((bf16[84,1536]{1,0:T(8,128)(2,1)S(1)}, bf16[84,1536]{1,0:T(8,128)(2,1)S(1)}, u32[]{:S(2)}, u32[]{:S(2)}) %collective-permute-start.19) | collective-permute-done | bytes 258080 | tf_op jit(solution)/shard_map/ppermute | solution.py:296
  96.3 3.8 %collective-permute-start.18 = (bf16[42,2048]{1,0:T(8,128)(2,1)S(1)}, bf16[42,2048]{1,0:T(8,128)(2,1)S(1)}, u32[]{:S(2)}, u32[]{:S(2)}) collective-permute-start(bf16[42,2048]{1,0:T(8,128)(2,1)S(1)} %add_convert_fusion.2), channel_id=1, source_target_pairs={{0,8},{2,10},{4,12},{6,14},{8,0},{10,2},{12,4},{14,6},{1,9},{3,11}... | collective-permute-start | bytes 516104 | tf_op jit(solution)/shard_map/ppermute | solution.py:299
  100.5 9.5 %collective-permute-done.18 = bf16[42,2048]{1,0:T(8,128)(2,1)S(1)} collective-permute-done((bf16[42,2048]{1,0:T(8,128)(2,1)S(1)}, bf16[42,2048]{1,0:T(8,128)(2,1)S(1)}, u32[]{:S(2)}, u32[]{:S(2)}) %collective-permute-start.18) | collective-permute-done | bytes 172064 | tf_op jit(solution)/shard_map/ppermute | solution.py:299
  (58 shorter events, 24.8 us)
Async XLA Ops:
  1.6 0.9 copy-start
  2.8 10.7 %collective-permute-start = (bf16[42,2176]{1,0:T(8,128)(2,1)S(1)}, bf16[42,2176]{1,0:T(8,128)(2,1)S(1)}, u32[]{:S(2)}, u32[]{:S(2)}) collective-permute-start(bf16[42,2176]{1,0:T(8,128)(2,1)S(1)} %prepare.1.rows_ref), channel_id=1, source_target_pairs={{0,2},{2,0},{4,6},{6,4},{8,10},{10,8},{12,14},{14,12},{1,3},{3,1},... | collective-permute-start | bytes 548360 | tf_op jit(solution)/shard_map/ppermute | solution.py:299
  3.3 10.8 %collective-permute-start.2 = (bf16[42,2176]{1,0:T(8,128)(2,1)S(1)}, bf16[42,2176]{1,0:T(8,128)(2,1)S(1)}, u32[]{:S(2)}, u32[]{:S(2)}) collective-permute-start(bf16[42,2176]{1,0:T(8,128)(2,1)S(1)} %prepare.1.rows_ref), channel_id=1, source_target_pairs={{0,12},{2,14},{4,8},{6,10},{8,4},{10,6},{12,0},{14,2},{1,13},{3,15... | collective-permute-start | bytes 548360 | tf_op jit(solution)/shard_map/ppermute | solution.py:299
  8.0 18.4 %collective-permute-start.6 = (bf16[42,2176]{1,0:T(8,128)(2,1)S(1)}, bf16[42,2176]{1,0:T(8,128)(2,1)S(1)}, u32[]{:S(2)}, u32[]{:S(2)}) collective-permute-start(bf16[42,2176]{1,0:T(8,128)(2,1)S(1)} %prepare.1.rows_ref), channel_id=1, source_target_pairs={{0,8},{2,10},{4,12},{6,14},{8,0},{10,2},{12,4},{14,6},{1,9},{3,11}... | collective-permute-start | bytes 548360 | tf_op jit(solution)/shard_map/ppermute | solution.py:299
  8.0 18.4 %collective-permute-start.11 = (bf16[42,2176]{1,0:T(8,128)(2,1)S(1)}, bf16[42,2176]{1,0:T(8,128)(2,1)S(1)}, u32[]{:S(2)}, u32[]{:S(2)}) collective-permute-start(bf16[42,2176]{1,0:T(8,128)(2,1)S(1)} %prepare.1.rows_ref), channel_id=1, source_target_pairs={{0,4},{2,6},{4,0},{6,2},{8,12},{10,14},{12,8},{14,10},{1,5},{3,7},... | collective-permute-start | bytes 548360 | tf_op jit(solution)/shard_map/ppermute | solution.py:299
  14.1 18.0 %collective-permute-start.3 = (bf16[42,2176]{1,0:T(8,128)(2,1)S(1)}, bf16[42,2176]{1,0:T(8,128)(2,1)S(1)}, u32[]{:S(2)}, u32[]{:S(2)}) collective-permute-start(bf16[42,2176]{1,0:T(8,128)(2,1)S(1)} %collective-permute-done.2), channel_id=1, source_target_pairs={{0,2},{2,0},{4,6},{6,4},{8,10},{10,8},{12,14},{14,12},{1,3},{3,1},... | collective-permute-start | bytes 548360 | tf_op jit(solution)/shard_map/ppermute | solution.py:299
  16.3 19.8 %collective-permute-start.1 = (bf16[84,3072]{1,0:T(8,128)(2,1)S(1)}, bf16[84,3072]{1,0:T(8,128)(2,1)S(1)}, u32[]{:S(2)}, u32[]{:S(2)}) collective-permute-start(bf16[84,3072]{1,0:T(8,128)(2,1)S(1)} %gate_up.7.refs_0_), channel_id=1, source_target_pairs={{0,1},{1,0},{2,3},{3,2},{4,5},{5,4},{6,7},{7,6},{8,9},{9,8},{10,11... | collective-permute-start | bytes 1548296 | tf_op jit(solution)/shard_map/ppermute | solution.py:296
  26.3 9.6 %collective-permute-start.7 = (bf16[42,2176]{1,0:T(8,128)(2,1)S(1)}, bf16[42,2176]{1,0:T(8,128)(2,1)S(1)}, u32[]{:S(2)}, u32[]{:S(2)}) collective-permute-start(bf16[42,2176]{1,0:T(8,128)(2,1)S(1)} %collective-permute-done.6), channel_id=1, source_target_pairs={{0,2},{2,0},{4,6},{6,4},{8,10},{10,8},{12,14},{14,12},{1,3},{3,1},... | collective-permute-start | bytes 548360 | tf_op jit(solution)/shard_map/ppermute | solution.py:299
  26.3 9.7 %collective-permute-start.12 = (bf16[42,2176]{1,0:T(8,128)(2,1)S(1)}, bf16[42,2176]{1,0:T(8,128)(2,1)S(1)}, u32[]{:S(2)}, u32[]{:S(2)}) collective-permute-start(bf16[42,2176]{1,0:T(8,128)(2,1)S(1)} %collective-permute-done.11), channel_id=1, source_target_pairs={{0,2},{2,0},{4,6},{6,4},{8,10},{10,8},{12,14},{14,12},{1,3},{3,1},... | collective-permute-start | bytes 548360 | tf_op jit(solution)/shard_map/ppermute | solution.py:299
  34.4 15.2 %collective-permute-start.5 = (bf16[84,3072]{1,0:T(8,128)(2,1)S(1)}, bf16[84,3072]{1,0:T(8,128)(2,1)S(1)}, u32[]{:S(2)}, u32[]{:S(2)}) collective-permute-start(bf16[84,3072]{1,0:T(8,128)(2,1)S(1)} %gate_up.8.refs_0_), channel_id=1, source_target_pairs={{0,1},{1,0},{2,3},{3,2},{4,5},{5,4},{6,7},{7,6},{8,9},{9,8},{10,11... | collective-permute-start | bytes 1548296 | tf_op jit(solution)/shard_map/ppermute | solution.py:296
  36.3 19.0 %collective-permute-start.4 = (bf16[84,1536]{1,0:T(8,128)(2,1)S(1)}, bf16[84,1536]{1,0:T(8,128)(2,1)S(1)}, u32[]{:S(2)}, u32[]{:S(2)}) collective-permute-start(bf16[84,1536]{1,0:T(8,128)(2,1)S(1)} %hidden.4.refs_1_.refs_3_), channel_id=1, source_target_pairs={{0,1},{1,0},{2,3},{3,2},{4,5},{5,4},{6,7},{7,6},{8,9},{9,8},{10,11... | collective-permute-start | bytes 774152 | tf_op jit(solution)/shard_map/ppermute | solution.py:296
  44.5 22.4 %collective-permute-start.10 = (bf16[84,3072]{1,0:T(8,128)(2,1)S(1)}, bf16[84,3072]{1,0:T(8,128)(2,1)S(1)}, u32[]{:S(2)}, u32[]{:S(2)}) collective-permute-start(bf16[84,3072]{1,0:T(8,128)(2,1)S(1)} %gate_up.10.refs_0_), channel_id=1, source_target_pairs={{0,1},{1,0},{2,3},{3,2},{4,5},{5,4},{6,7},{7,6},{8,9},{9,8},{10,11... | collective-permute-start | bytes 1548296 | tf_op jit(solution)/shard_map/ppermute | solution.py:296
  49.8 22.9 %collective-permute-start.9 = (bf16[84,1536]{1,0:T(8,128)(2,1)S(1)}, bf16[84,1536]{1,0:T(8,128)(2,1)S(1)}, u32[]{:S(2)}, u32[]{:S(2)}) collective-permute-start(bf16[84,1536]{1,0:T(8,128)(2,1)S(1)} %hidden.5.refs_4_.refs_0_), channel_id=1, source_target_pairs={{0,1},{1,0},{2,3},{3,2},{4,5},{5,4},{6,7},{7,6},{8,9},{9,8},{10,11... | collective-permute-start | bytes 774152 | tf_op jit(solution)/shard_map/ppermute | solution.py:296
  64.1 20.2 %collective-permute-start.16 = (bf16[84,3072]{1,0:T(8,128)(2,1)S(1)}, bf16[84,3072]{1,0:T(8,128)(2,1)S(1)}, u32[]{:S(2)}, u32[]{:S(2)}) collective-permute-start(bf16[84,3072]{1,0:T(8,128)(2,1)S(1)} %gate_up.12.refs_0_), channel_id=1, source_target_pairs={{0,1},{1,0},{2,3},{3,2},{4,5},{5,4},{6,7},{7,6},{8,9},{9,8},{10,11... | collective-permute-start | bytes 1548296 | tf_op jit(solution)/shard_map/ppermute | solution.py:296
  65.7 34.9 %collective-permute-start.8 = (bf16[42,2048]{1,0:T(8,128)(2,1)S(1)}, bf16[42,2048]{1,0:T(8,128)(2,1)S(1)}, u32[]{:S(2)}, u32[]{:S(2)}) collective-permute-start(bf16[42,2048]{1,0:T(8,128)(2,1)S(1)} %slice.25), channel_id=1, source_target_pairs={{0,2},{2,0},{4,6},{6,4},{8,10},{10,8},{12,14},{14,12},{1,3},{3,1},... | collective-permute-start | bytes 516104 | tf_op jit(solution)/shard_map/ppermute | solution.py:299
  75.2 15.0 %collective-permute-start.15 = (bf16[84,1536]{1,0:T(8,128)(2,1)S(1)}, bf16[84,1536]{1,0:T(8,128)(2,1)S(1)}, u32[]{:S(2)}, u32[]{:S(2)}) collective-permute-start(bf16[84,1536]{1,0:T(8,128)(2,1)S(1)} %hidden.6.refs_3_.refs_0_), channel_id=1, source_target_pairs={{0,1},{1,0},{2,3},{3,2},{4,5},{5,4},{6,7},{7,6},{8,9},{9,8},{10,11... | collective-permute-start | bytes 774152 | tf_op jit(solution)/shard_map/ppermute | solution.py:296
  76.7 2.2 %collective-permute-start.13 = (bf16[42,2048]{1,0:T(8,128)(2,1)S(1)}, bf16[42,2048]{1,0:T(8,128)(2,1)S(1)}, u32[]{:S(2)}, u32[]{:S(2)}) collective-permute-start(bf16[42,2048]{1,0:T(8,128)(2,1)S(1)} %slice.33), channel_id=1, source_target_pairs={{0,2},{2,0},{4,6},{6,4},{8,10},{10,8},{12,14},{14,12},{1,3},{3,1},... | collective-permute-start | bytes 516104 | tf_op jit(solution)/shard_map/ppermute | solution.py:299
  79.0 21.6 %collective-permute-start.14 = (bf16[42,2048]{1,0:T(8,128)(2,1)S(1)}, bf16[42,2048]{1,0:T(8,128)(2,1)S(1)}, u32[]{:S(2)}, u32[]{:S(2)}) collective-permute-start(bf16[42,2048]{1,0:T(8,128)(2,1)S(1)} %add_convert_fusion.3), channel_id=1, source_target_pairs={{0,12},{2,14},{4,8},{6,10},{8,4},{10,6},{12,0},{14,2},{1,13},{3,15... | collective-permute-start | bytes 516104 | tf_op jit(solution)/shard_map/ppermute | solution.py:299
  84.6 10.4 %collective-permute-start.19 = (bf16[84,1536]{1,0:T(8,128)(2,1)S(1)}, bf16[84,1536]{1,0:T(8,128)(2,1)S(1)}, u32[]{:S(2)}, u32[]{:S(2)}) collective-permute-start(bf16[84,1536]{1,0:T(8,128)(2,1)S(1)} %hidden.7.refs_3_.refs_0_), channel_id=1, source_target_pairs={{0,1},{1,0},{2,3},{3,2},{4,5},{5,4},{6,7},{7,6},{8,9},{9,8},{10,11... | collective-permute-start | bytes 774152 | tf_op jit(solution)/shard_map/ppermute | solution.py:296
  91.3 4.9 %collective-permute-start.17 = (bf16[42,2048]{1,0:T(8,128)(2,1)S(1)}, bf16[42,2048]{1,0:T(8,128)(2,1)S(1)}, u32[]{:S(2)}, u32[]{:S(2)}) collective-permute-start(bf16[42,2048]{1,0:T(8,128)(2,1)S(1)} %slice.35), channel_id=1, source_target_pairs={{0,2},{2,0},{4,6},{6,4},{8,10},{10,8},{12,14},{14,12},{1,3},{3,1},... | collective-permute-start | bytes 516104 | tf_op jit(solution)/shard_map/ppermute | solution.py:299
  96.2 4.0 %collective-permute-start.20 = (bf16[42,2048]{1,0:T(8,128)(2,1)S(1)}, bf16[42,2048]{1,0:T(8,128)(2,1)S(1)}, u32[]{:S(2)}, u32[]{:S(2)}) collective-permute-start(bf16[42,2048]{1,0:T(8,128)(2,1)S(1)} %slice.37), channel_id=1, source_target_pairs={{0,2},{2,0},{4,6},{6,4},{8,10},{10,8},{12,14},{14,12},{1,3},{3,1},... | collective-permute-start | bytes 516104 | tf_op jit(solution)/shard_map/ppermute | solution.py:299
  96.3 13.7 %collective-permute-start.18 = (bf16[42,2048]{1,0:T(8,128)(2,1)S(1)}, bf16[42,2048]{1,0:T(8,128)(2,1)S(1)}, u32[]{:S(2)}, u32[]{:S(2)}) collective-permute-start(bf16[42,2048]{1,0:T(8,128)(2,1)S(1)} %add_convert_fusion.2), channel_id=1, source_target_pairs={{0,8},{2,10},{4,12},{6,14},{8,0},{10,2},{12,4},{14,6},{1,9},{3,11}... | collective-permute-start | bytes 516104 | tf_op jit(solution)/shard_map/ppermute | solution.py:299
  100.2 10.1 %collective-permute-start.21 = (bf16[42,2048]{1,0:T(8,128)(2,1)S(1)}, bf16[42,2048]{1,0:T(8,128)(2,1)S(1)}, u32[]{:S(2)}, u32[]{:S(2)}) collective-permute-start(bf16[42,2048]{1,0:T(8,128)(2,1)S(1)} %add_convert_fusion.1), channel_id=1, source_target_pairs={{0,4},{2,6},{4,0},{6,2},{8,12},{10,14},{12,8},{14,10},{1,5},{3,7},... | collective-permute-start | bytes 516104 | tf_op jit(solution)/shard_map/ppermute | solution.py:299

commit v3 on v2

--- a/solution.py
+++ b/solution.py
@@ -67,19 +67,18 @@
 
 def prepare_kernel(tokens_ref, ids_ref, scores_ref, out_ref):
     count, width = tokens_ref.shape
-    top = ids_ref.shape[1]
+    top = ids_ref.shape[0]
     scores = scores_ref[...]
-    weights = scores / jnp.sum(scores, axis=1, keepdims=True)
-    lane = lax.broadcasted_iota(jnp.int32, (count, EXTRA), 1)
-    ids = ids_ref[...]
-    share = jnp.zeros((count, EXTRA), jnp.float32)
+    weights = scores / jnp.sum(scores, axis=0, keepdims=True)
+    place = lax.broadcasted_iota(jnp.int32, (EXTRA, count), 0)
+    share = jnp.zeros((EXTRA, count), jnp.float32)
     for k in range(top):
-        chosen = ids[:, k : k + 1]
-        match = (lane == chosen) | (lane == chosen + EXTRA // 2)
-        share = share + jnp.where(match, weights[:, k : k + 1], 0.0)
+        chosen = ids_ref[k : k + 1, :]
+        match = (place == chosen) | (place == chosen + EXTRA // 2)
+        share = share + jnp.where(match, weights[k : k + 1, :], 0.0)
     high = share.astype(jnp.bfloat16).astype(jnp.float32)
     out_ref[:, :width] = tokens_ref[...]
-    out_ref[:, width:] = jnp.where(lane < EXTRA // 2, high, share - high).astype(jnp.bfloat16)
+    out_ref[:, width:] = jnp.where(place < EXTRA // 2, high, share - high).T.astype(jnp.bfloat16)
 
 
 def prepare(tokens, ids, scores):
@@ -91,7 +90,7 @@
         out_shape=jax.ShapeDtypeStruct((count, width + EXTRA), jnp.bfloat16),
         compiler_params=pltpu.CompilerParams(vmem_limit_bytes=SMALL),
         name="prepare",
-    )(tokens, ids, scores)
+    )(in_hbm(tokens), in_hbm(ids.T), in_hbm(scores.T))
 
 
 def project(rows_ref, held, out_ref, expert, which, start, size):
@@ -147,24 +146,50 @@
     )(side, rows, in_hbm(w_gate), in_hbm(w_up), *after)
 
 
-def gate_up_kernel(rows_ref, gate_held, up_held, *refs):
-    out_ref = refs[-1]
+def down_copies(side_ref, weight_ref, held, sem):
+    experts, half, width = held.shape
+    base = pl.multiple_of(side_ref[0] * half, 256)
+    return [
+        pltpu.make_async_copy(weight_ref.at[e, pl.ds(base, half), :], held.at[e], sem.at[e])
+        for e in range(experts)
+    ]
+
+
+def gate_up_kernel(load, rows_ref, gate_held, up_held, *refs):
     experts, _, half = gate_held.shape
     tile = half // 3
+    copies = []
+    if load:
+        out_ref, held, sem = refs[-3:]
+        copies = down_copies(refs[0], refs[1], held, sem)
+    else:
+        out_ref = refs[-1]
+    for copy in copies:
+        copy.start()
     for e in range(experts):
         for which, held in ((0, gate_held), (1, up_held)):
             for start in range(0, half, tile):
                 project(rows_ref, held, out_ref, e, which, start, tile)
-
-
-def gate_up(rows, gate_held, up_held, dtype, after):
+    for copy in copies:
+        copy.wait()
+
+
+def gate_up(rows, gate_held, up_held, dtype, after, side=None, w_down=None):
     count = rows.shape[0]
     experts, width, half = gate_held.shape
+    load = w_down is not None
+    out = jax.ShapeDtypeStruct((count, 2 * experts * half), dtype)
+    operands = [rows, in_vmem(gate_held), in_vmem(up_held)]
+    specs = [VMEM_SPEC] * 3
+    if load:
+        operands += [side, in_hbm(w_down)]
+        specs += [SMEM_SPEC, ANY_SPEC]
     return pl.pallas_call(
-        gate_up_kernel,
-        in_specs=[VMEM_SPEC] * 3 + [ANY_SPEC] * len(after),
-        out_specs=VMEM_SPEC,
-        out_shape=jax.ShapeDtypeStruct((count, 2 * experts * half), dtype),
+        functools.partial(gate_up_kernel, load),
+        in_specs=specs + [ANY_SPEC] * len(after),
+        out_specs=[VMEM_SPEC] * 2 if load else VMEM_SPEC,
+        out_shape=[out, pltpu.VMEM((experts, half, w_down.shape[2]), w_down.dtype)] if load else out,
+        scratch_shapes=[pltpu.SemaphoreType.DMA((experts,))] if load else [],
         compiler_params=pltpu.CompilerParams(vmem_limit_bytes=SMALL),
         cost_estimate=pl.CostEstimate(
             flops=4 * max(count, 256) * width * half * experts,
@@ -172,7 +197,7 @@
             transcendentals=0,
         ),
         name="gate_up",
-    )(rows, in_vmem(gate_held), in_vmem(up_held), *after)
+    )(*operands, *after)
 
 
 def hidden_kernel(experts, here_ref, rows_ref, kept_ref, received_ref, *refs):
@@ -214,78 +239,46 @@
     )(here, rows, kept, received, *after)
 
 
-def down_kernel(load, more, n_after, *refs):
-    refs = list(refs)
-    side_ref = refs.pop(0) if load else None
-    hidden_ref, weight_ref = refs.pop(0), refs.pop(0)
-    so_far = refs.pop(0) if more else None
-    refs = refs[n_after:]
-    out_ref = refs.pop(0)
-    held, sem = refs if load else (weight_ref, None)
+def down_kernel(more, hidden_ref, held, *refs):
+    out_ref = refs[-1]
     experts, half, width = held.shape
     tile = width // 4
-    copies = []
-    if load:
-        base = pl.multiple_of(side_ref[0] * half, 256)
-        for index in range(4):
-            for e in range(experts):
-                columns = pl.ds(index * tile, tile)
-                copy = pltpu.make_async_copy(
-                    weight_ref.at[e, pl.ds(base, half), columns],
-                    held.at[e, :, columns],
-                    sem.at[len(copies)],
-                )
-                copy.start()
-                copies.append(copy)
     for index in range(4):
         columns = slice(index * tile, (index + 1) * tile)
-        value = so_far[:, columns] if more else None
+        value = refs[0][:, columns] if more else None
         for e in range(experts):
-            if load:
-                copies[index * experts + e].wait()
             product = jnp.dot(
                 hidden_ref[:, e * half : (e + 1) * half],
                 held[e, :, columns],
                 preferred_element_type=jnp.float32,
             )
             value = product if value is None else value + product
-        out_ref[:, columns] = value.astype(out_ref.dtype)
-
-
-def down(hidden, so_far, dtype, after, held=None, side=None, weight=None):
+        out_ref[:, columns] = value
+
+
+def down(hidden, held, so_far, after):
     count = hidden.shape[0]
-    load = weight is not None
-    more = so_far is not None
-    experts, depth, width = (weight if load else held).shape
-    half = depth // 2 if load else depth
-    out = jax.ShapeDtypeStruct((count, width), dtype)
-    operands = [side, hidden, in_hbm(weight)] if load else [hidden, in_vmem(held)]
-    specs = [SMEM_SPEC, VMEM_SPEC, ANY_SPEC] if load else [VMEM_SPEC] * 2
-    if more:
-        operands.append(so_far)
-        specs.append(VMEM_SPEC)
-    operands += after
-    specs += [ANY_SPEC] * len(after)
+    experts, half, width = held.shape
+    extra = [] if so_far is None else [so_far]
     return pl.pallas_call(
-        functools.partial(down_kernel, load, more, len(after)),
-        in_specs=specs,
-        out_specs=[VMEM_SPEC] * 2 if load else VMEM_SPEC,
-        out_shape=[out, pltpu.VMEM((experts, half, width), weight.dtype)] if load else out,
-        scratch_shapes=[pltpu.SemaphoreType.DMA((4 * experts,))] if load else [],
+        functools.partial(down_kernel, len(extra)),
+        in_specs=[VMEM_SPEC] * (2 + len(extra)) + [ANY_SPEC] * len(after),
+        out_specs=VMEM_SPEC,
+        out_shape=jax.ShapeDtypeStruct((count, width), jnp.float32),
         compiler_params=pltpu.CompilerParams(vmem_limit_bytes=SMALL),
         cost_estimate=pl.CostEstimate(
             flops=2 * max(count, 256) * width * half * experts,
-            bytes_accessed=2 * experts * width * half if load else 0,
+            bytes_accessed=0,
             transcendentals=0,
         ),
-        name="down_load" if load else "down",
-    )(*operands)
+        name="down",
+    )(hidden, in_vmem(held), *extra, *after)
 
 
 def pair_shards(tokens, route_ids, route_scores, w_gate, w_up, w_down):
     groups = lax.axis_size("expert")
     local_experts = w_gate.shape[0]
-    count, width = tokens.shape
+    count = tokens.shape[0]
     chips = groups // CORES
     here = lax.axis_index("expert").reshape(1)
     mine = lax.axis_index("tensor").reshape(1)
@@ -298,63 +291,136 @@
     def swap_expert(value, mask):
         return lax.ppermute(value, "expert", [(i, i ^ mask) for i in range(groups)])
 
+    def later(value, than):
+        return lax.optimization_barrier((value, than))[0]
+
+    near, far = CORES, [CORES * step for step in range(chips - 1, 1, -1)]
+    fills = [-count % 8] + [-(CORES * count) % 8] * len(far) + [-count % 8]
+    first = (count - sum(fills[:2])) // 8 * 8
+    if CORES * count - first - sum(fills) < 8:
+        fills = [0] * len(fills)
+    begins = [first + sum(fills[:i]) for i in range(len(fills) + 1)]
+    last = len(fills) + 1
+
     own = prepare(tokens, route_ids, route_scores)
-    steps = [0] + list(range(chips - 1, 0, -1))
-    chunks = []
-    for step in steps:
-        same = swap_expert(own, CORES * step) if step else own
-        chunks.append(jnp.concatenate([same, swap_expert(same, 1)], axis=0))
-    total = len(chunks)
-
-    gate_other, up_other = gate_up_load(other, own, w_gate, w_up, [])
-    theirs, received, kept, hidden, arrived, begun, outs = {}, {}, {}, {}, {}, {}, {}
-
-    def send_theirs(i, after):
-        theirs[i] = gate_up(chunks[i], gate_other, up_other, bf16, after)
+    near_same = swap_expert(own, near)
+    came = [swap_expert(own, mask) for mask in far[:1]]
+    theirs, received, kept, hidden, arrived, begun, outs, chunks = {}, {}, {}, {}, {}, {}, {}, {}
+    parts, back, after = {}, [], []
+
+    def local(begin, end):
+        if end <= count:
+            return [own[begin:end]]
+        if begin >= count:
+            return [partner[begin - count : end - count]]
+        return [own[begin:], partner[: end - count]]
+
+    def bring(i, rows):
+        chunks[i] = jnp.concatenate(rows + local(begins[i - 1], begins[i]), axis=0)
+
+    def bring_far(i):
+        rows = later(came[i - 2], after[0])
+        bring(i, [rows, swap_expert(rows, 1)])
+
+    def send_theirs(i, **load):
+        theirs[i] = gate_up(chunks[i], gate_other, up_other, bf16, after, **load)
+        more = []
+        if load:
+            theirs[i], *more = theirs[i]
         received[i] = swap_tensor(theirs[i])
-        return [theirs[i]]
-
-    def send_hidden(i, after):
+        after[:] = [theirs[i]]
+        return more
+
+    def keep(i, **load):
+        kept[i] = gate_up(chunks[i], gate_mine, up_mine, f32, after, **load)
+        more = []
+        if load:
+            kept[i], *more = kept[i]
+        after[:] = [kept[i]]
+        return more
+
+    def send_hidden(i):
         hidden[i] = hidden_of(here, chunks[i], kept[i], received[i], local_experts, after)
         arrived[i] = swap_tensor(hidden[i])
-        return [hidden[i]]
-
-    after = send_theirs(0, [])
+        after[:] = [hidden[i]]
+
+    def begin_down(i):
+        begun[i] = down(hidden[i], down_mine, None, after)
+        after[:] = [begun[i]]
+
+    def end_down(i):
+        out = outs[i] = down(arrived[i], down_other, begun[i], after)
+        after[:] = [out]
+        if i in (1, last - 1):
+            back.append(swap_expert(out[:count].astype(bf16), near + (i != 1)))
+        elif 1 < i < last:
+            from_core = swap_expert(out[count : CORES * count].astype(bf16), 1)
+            parts[i] = (out[:count] + from_core.astype(f32)).astype(bf16)
+            back.append(swap_expert(parts[i], far[i - 2]))
+
+    chunks[0] = own[:first]
+    theirs[0], gate_other, up_other = gate_up_load(other, chunks[0], w_gate, w_up, [here, mine], bf16)
+    received[0] = swap_tensor(theirs[0])
+    after[:] = [theirs[0]]
+    bring(1, [near_same])
+    send_theirs(1)
+    waiting = later(own, theirs[1])
+    partner = swap_expert(waiting, 1)
+    came += [swap_expert(waiting, mask) for mask in far[1:]]
     kept[0], gate_mine, up_mine = gate_up_load(mine, chunks[0], w_gate, w_up, after, f32)
-    after = [kept[0]]
-    for i in range(total):
-        if i + 1 < total:
-            after = send_theirs(i + 1, after)
-        after = send_hidden(i, after)
-        if i:
-            outs[i - 1] = down(arrived[i - 1], begun[i - 1], bf16, after, **late)
-            if i == 1:
-                outs[0], down_other = outs[0]
-                late = dict(held=down_other)
-            after = [outs[i - 1]]
-        early = dict(held=down_mine) if i else dict(side=mine, weight=w_down)
-        begun[i] = down(hidden[i], None, f32, after, **early)
-        if i == 0:
-            begun[0], down_mine = begun[0]
-            late = dict(side=other, weight=w_down)
-        after = [begun[i]]
-        if i + 1 < total:
-            kept[i + 1] = gate_up(chunks[i + 1], gate_mine, up_mine, f32, after)
-            after = [kept[i + 1]]
-    outs[total - 1] = down(arrived[total - 1], begun[total - 1], bf16, after, **late)
-    result = None
-    for i, step in enumerate(steps):
-        from_core = swap_expert(outs[i][count:], 1)
-        part = outs[i][:count].astype(f32) + from_core.astype(f32)
-        if step:
-            part = swap_expert(part.astype(bf16), CORES * step).astype(f32)
-        result = part if result is None else result + part
+    after[:] = [kept[0]]
+    send_hidden(0)
+    if far:
+        bring_far(2)
+    keep(1)
+    send_hidden(1)
+    near_other = swap_expert(later(own, hidden[1]), near + 1)
+    if not far:
+        bring(2, [near_other])
+    (down_mine,) = send_theirs(2, side=mine, w_down=w_down)
+    if len(far) > 1:
+        bring_far(3)
+    elif far:
+        bring(3, [near_other])
+    else:
+        chunks[3] = partner[begins[-1] - count :]
+    (down_other,) = keep(2, side=other, w_down=w_down)
+    begin_down(0)
+    send_theirs(3)
+    begin_down(1)
+    for i in range(2, last + 1):
+        send_hidden(i)
+        if i + 2 <= last:
+            if i + 2 == last:
+                chunks[last] = partner[begins[-1] - count :]
+            elif i + 2 == last - 1:
+                bring(i + 2, [later(near_other, hidden[i])])
+            else:
+                bring_far(i + 2)
+            send_theirs(i + 2)
+        for early in (0, 1) if i == 2 else (i - 1,):
+            end_down(early)
+        begin_down(i)
+        if i < last:
+            keep(i + 1)
+        if i - 1 in parts:
+            after.append(parts[i - 1])
+    end_down(last)
+
+    pieces = [outs[0]]
+    for i in range(1, last):
+        pieces.append(outs[i][count if i in (1, last - 1) else CORES * count :])
+    pieces = jnp.concatenate(pieces + [outs[last]], axis=0)
+    from_core = swap_expert(pieces[count:].astype(bf16), 1)
+    result = pieces[:count]
+    for value in back + [from_core]:
+        result = result + value.astype(f32)
     return result.astype(bf16)
 
 
 def solution(mesh):
     groups = mesh.shape["expert"]
-    paired = mesh.shape["tensor"] == 2 and groups % CORES == 0 and groups & (groups - 1) == 0
+    paired = mesh.shape["tensor"] == 2 and groups > CORES and groups & (groups - 1) == 0
     placed = (
         P(("replica", "expert"), "tensor"),
         P(("replica", "expert"), None),

time: 111 us -> 95.9 us (0.86)
  the two profiles are of different devices: /device:TPU:0 before, /device:TPU:25 now
where the time goes in v3:
time: 95.9 us; the launch traced here: 95.8 us
  Pallas kernels  50.9 us (53%)
  starting transfers between devices  26 us (27%)
  waiting for transfers between devices  16.9 us (18%)
  other arithmetic  1.3 us (1%)
    pallas_call x10, Pallas kernels, gate_up(): pl.pallas_call(functools.partial(gate_up_kernel, load), in_specs=specs +...  23.8 us
    ppermute x14, starting transfers between devices, swap_expert(): return lax.ppermute(value, 'expert', [(i, i ^ mask) for i in range(groups)])  16.6 us
    pallas_call x12, Pallas kernels, down(): pl.pallas_call(functools.partial(down_kernel, len(extra)), in_specs=[VMEM...  14.5 us
    ppermute x12, waiting for transfers between devices, swap_tensor(): return lax.ppermute(value, 'tensor', [(0, 1), (1, 0)])  11.3 us
    pallas_call x2, Pallas kernels, gate_up_load(): pl.pallas_call(functools.partial(gate_up_load_kernel, compute), in_specs=...  10.4 us
    ppermute x12, starting transfers between devices, swap_tensor(): return lax.ppermute(value, 'tensor', [(0, 1), (1, 0)])  9.48 us
    ppermute x14, waiting for transfers between devices, swap_expert(): return lax.ppermute(value, 'expert', [(i, i ^ mask) for i in range(groups)])  5.63 us
  transfers between devices with their start and end apart: 26, of which 6 were waited for; matrix products, arithmetic and copies ran while one was open for 1% of the time, Pallas kernels for 52%

profile of v3, /device:TPU:25, one launch (start us, length us, event | category | flops | bytes accessed | tf_op | source)
XLA Modules:
  0.0 95.8 jit_solution(15324183278449974806)
XLA Ops:
  2.5 5.2 %gate_up_load.2 = (bf16[32,3072]{1,0:T(8,128)(2,1)S(1)}, bf16[2,2048,768]{2,1,0:T(8,128)(2,1)S(1)}, bf16[2,2048,768]{2,1,0:T(8,128)(2,1)S(1)}) custom-call(s32[1]{0:T(128)S(6)} %sub.3.side_ref.refs_0_, bf16[32,2176]{1,0:T(8,128)(2,1)S(1)} %slice.74.rows_ref, bf16[2,2048,1536]{2,1,0:T(8,128)(2,1)} %gate_ref.3, bf16[2,2048,1536]{2,1,0:T(8,128)(2,1)} %up_ref.3, ...), custom_call_target="tpu_custom_call" | custom-call | flops 402653184 | bytes 12582912 | tf_op jit(solution)/shard_map/gate_up_load/pallas_call | solution.py:133
  9.0 2.3 %gate_up.10.refs_0_ = bf16[48,3072]{1,0:T(8,128)(2,1)S(1)} custom-call(bf16[48,2176]{1,0:T(8,128)(2,1)S(1)} %pad_maximum_fusion.2.rows_ref, bf16[2,2048,768]{2,1,0:T(8,128)(2,1)S(1)} %get-tuple-element.20.gate_held, bf16[2,2048,768]{2,1,0:T(8,128)(2,1)S(1)} %get-tuple-element.21.up_held, bf16[32,3072]{1,0:T(8,128)(2,1)S(1)} %get-tuple-element.22.refs_0_), custom_call_target="tpu_custom_call" | custom-call | flops 3221225472 | tf_op jit(solution)/shard_map/gate_up/pallas_call | solution.py:187
  11.4 4.3 %collective-permute-start.10 = (bf16[42,2176]{1,0:T(8,128)(2,1)S(1)}, bf16[42,2176]{1,0:T(8,128)(2,1)S(1)}, u32[]{:S(2)}, u32[]{:S(2)}) collective-permute-start(bf16[42,2176]{1,0:T(8,128)(2,1)S(1)} %prepare.1), channel_id=1, source_target_pairs={{0,2},{2,0},{4,6},{6,4},{8,10},{10,8},{12,14},{14,12},{1,3},{3,1},... | collective-permute-start | bytes 548360 | tf_op jit(solution)/shard_map/ppermute | solution.py:292
  16.9 5.2 %gate_up_load.3 = (f32[32,3072]{1,0:T(8,128)S(1)}, bf16[2,2048,768]{2,1,0:T(8,128)(2,1)S(1)}, bf16[2,2048,768]{2,1,0:T(8,128)(2,1)S(1)}) custom-call(s32[1]{0:T(128)} %bitcast.3.refs_1_.side_ref.refs_0_, bf16[32,2176]{1,0:T(8,128)(2,1)S(1)} %slice.74.rows_ref, bf16[2,2048,1536]{2,1,0:T(8,128)(2,1)} %gate_ref.3, bf16[2,2048,1536]{2,1,0:T(8,128)(2,1)} %up_ref.3, ...), custom_call_target="tpu_custom_call" | custom-call | flops 402653184 | bytes 12582912 | tf_op jit(solution)/shard_map/gate_up_load/pallas_call | solution.py:133
  23.3 2.3 %gate_up.11.kept_ref.refs_0_ = f32[48,3072]{1,0:T(8,128)S(1)} custom-call(bf16[48,2176]{1,0:T(8,128)(2,1)S(1)} %pad_maximum_fusion.2.rows_ref, bf16[2,2048,768]{2,1,0:T(8,128)(2,1)S(1)} %get-tuple-element.25.gate_held, bf16[2,2048,768]{2,1,0:T(8,128)(2,1)S(1)} %get-tuple-element.26.up_held, bf16[32,1536]{1,0:T(8,128)(2,1)S(1)} %hidden.6.refs_0_.hidden_ref), custom_call_target="tpu_custom_call" | custom-call | flops 3221225472 | tf_op jit(solution)/shard_map/gate_up/pallas_call | solution.py:187
  27.2 2.9 %gate_up.12 = (bf16[88,3072]{1,0:T(8,128)(2,1)S(1)}, bf16[2,768,2048]{2,1,0:T(8,128)(2,1)S(1)}) custom-call(bf16[88,2176]{1,0:T(8,128)(2,1)S(1)} %pad_maximum_fusion.rows_ref, bf16[2,2048,768]{2,1,0:T(8,128)(2,1)S(1)} %get-tuple-element.20.gate_held, bf16[2,2048,768]{2,1,0:T(8,128)(2,1)S(1)} %get-tuple-element.21.up_held, s32[1]{0:T(128)} %bitcast.3.refs_1_.side_ref.refs_0_, ...), custom_call_target="tpu_custom_call" | custom-call | flops 3221225472 | tf_op jit(solution)/shard_map/gate_up/pallas_call | solution.py:187
  31.0 2.9 %gate_up.13 = (f32[88,3072]{1,0:T(8,128)S(1)}, bf16[2,768,2048]{2,1,0:T(8,128)(2,1)S(1)}) custom-call(bf16[88,2176]{1,0:T(8,128)(2,1)S(1)} %pad_maximum_fusion.rows_ref, bf16[2,2048,768]{2,1,0:T(8,128)(2,1)S(1)} %get-tuple-element.25.gate_held, bf16[2,2048,768]{2,1,0:T(8,128)(2,1)S(1)} %get-tuple-element.26.up_held, s32[1]{0:T(128)S(6)} %sub.3.side_ref.refs_0_, ...), custom_call_target="tpu_custom_call" | custom-call | flops 3221225472 | tf_op jit(solution)/shard_map/gate_up/pallas_call | solution.py:187
  34.0 1.4 %down.12.refs_0_ = f32[32,2048]{1,0:T(8,128)S(1)} custom-call(bf16[32,1536]{1,0:T(8,128)(2,1)S(1)} %hidden.6.refs_0_.hidden_ref, bf16[2,768,2048]{2,1,0:T(8,128)(2,1)S(1)} %get-tuple-element.29.held, f32[88,3072]{1,0:T(8,128)S(1)} %get-tuple-element.30.refs_0_.kept_ref), custom_call_target="tpu_custom_call" | custom-call | flops 1610612736 | tf_op jit(solution)/shard_map/down/pallas_call | solution.py:263
  35.5 2.1 %gate_up.14.refs_0_ = bf16[88,3072]{1,0:T(8,128)(2,1)S(1)} custom-call(bf16[88,2176]{1,0:T(8,128)(2,1)S(1)} %pad_maximum_fusion.1.rows_ref, bf16[2,2048,768]{2,1,0:T(8,128)(2,1)S(1)} %get-tuple-element.20.gate_held, bf16[2,2048,768]{2,1,0:T(8,128)(2,1)S(1)} %get-tuple-element.21.up_held, f32[32,2048]{1,0:T(8,128)S(1)} %down.12.refs_0_), custom_call_target="tpu_custom_call" | custom-call | flops 3221225472 | tf_op jit(solution)/shard_map/gate_up/pallas_call | solution.py:187
  40.1 3.7 %collective-permute-done.7.received_ref = bf16[88,3072]{1,0:T(8,128)(2,1)S(1)} collective-permute-done((bf16[88,3072]{1,0:T(8,128)(2,1)S(1)}, bf16[88,3072]{1,0:T(8,128)(2,1)S(1)}, u32[]{:S(2)}, u32[]{:S(2)}) %collective-permute-start.7) | collective-permute-done | bytes 540704 | tf_op jit(solution)/shard_map/ppermute | solution.py:289
  44.4 2.3 %gate_up.15.refs_1_ = bf16[48,3072]{1,0:T(8,128)(2,1)S(1)} custom-call(bf16[48,2176]{1,0:T(8,128)(2,1)S(1)} %pad_maximum_fusion.3.rows_ref, bf16[2,2048,768]{2,1,0:T(8,128)(2,1)S(1)} %get-tuple-element.20.gate_held, bf16[2,2048,768]{2,1,0:T(8,128)(2,1)S(1)} %get-tuple-element.21.up_held, bf16[88,1536]{1,0:T(8,128)(2,1)S(1)} %hidden.8.refs_0_.hidden_ref), custom_call_target="tpu_custom_call" | custom-call | flops 3221225472 | tf_op jit(solution)/shard_map/gate_up/pallas_call | solution.py:187
  51.7 2.2 %gate_up.16.kept_ref.refs_0_ = f32[88,3072]{1,0:T(8,128)S(1)} custom-call(bf16[88,2176]{1,0:T(8,128)(2,1)S(1)} %pad_maximum_fusion.1.rows_ref, bf16[2,2048,768]{2,1,0:T(8,128)(2,1)S(1)} %get-tuple-element.25.gate_held, bf16[2,2048,768]{2,1,0:T(8,128)(2,1)S(1)} %get-tuple-element.26.up_held, f32[88,2048]{1,0:T(8,128)S(1)} %down.16.refs_0_), custom_call_target="tpu_custom_call" | custom-call | flops 3221225472 | tf_op jit(solution)/shard_map/gate_up/pallas_call | solution.py:187
  53.8 1.5 %collective-permute-done.13.received_ref = bf16[88,3072]{1,0:T(8,128)(2,1)S(1)} collective-permute-done((bf16[88,3072]{1,0:T(8,128)(2,1)S(1)}, bf16[88,3072]{1,0:T(8,128)(2,1)S(1)}, u32[]{:S(2)}, u32[]{:S(2)}) %collective-permute-start.13) | collective-permute-done | bytes 540704 | tf_op jit(solution)/shard_map/ppermute | solution.py:289
  56.0 2.2 %gate_up.17.refs_1_ = bf16[32,3072]{1,0:T(8,128)(2,1)S(1)} custom-call(bf16[32,2176]{1,0:T(8,128)(2,1)S(1)} %slice.80.rows_ref, bf16[2,2048,768]{2,1,0:T(8,128)(2,1)S(1)} %get-tuple-element.20.gate_held, bf16[2,2048,768]{2,1,0:T(8,128)(2,1)S(1)} %get-tuple-element.21.up_held, bf16[88,1536]{1,0:T(8,128)(2,1)S(1)} %hidden.9.refs_0_.hidden_ref), custom_call_target="tpu_custom_call" | custom-call | flops 3221225472 | tf_op jit(solution)/shard_map/gate_up/pallas_call | solution.py:187
  59.4 1.7 %collective-permute-done.12.hidden_ref = bf16[88,1536]{1,0:T(8,128)(2,1)S(1)} collective-permute-done((bf16[88,1536]{1,0:T(8,128)(2,1)S(1)}, bf16[88,1536]{1,0:T(8,128)(2,1)S(1)}, u32[]{:S(2)}, u32[]{:S(2)}) %collective-permute-start.12) | collective-permute-done | bytes 270368 | tf_op jit(solution)/shard_map/ppermute | solution.py:289
  62.4 1.4 %down.18.refs_0_ = f32[88,2048]{1,0:T(8,128)S(1)} custom-call(bf16[88,1536]{1,0:T(8,128)(2,1)S(1)} %hidden.9.refs_0_.hidden_ref, bf16[2,768,2048]{2,1,0:T(8,128)(2,1)S(1)} %get-tuple-element.29.held, f32[88,2048]{1,0:T(8,128)S(1)} %down.17.refs_0_), custom_call_target="tpu_custom_call" | custom-call | flops 1610612736 | tf_op jit(solution)/shard_map/down/pallas_call | solution.py:263
  63.7 1.9 %collective-permute-start.15 = (bf16[42,2048]{1,0:T(8,128)(2,1)S(1)}, bf16[42,2048]{1,0:T(8,128)(2,1)S(1)}, u32[]{:S(2)}, u32[]{:S(2)}) collective-permute-start(bf16[42,2048]{1,0:T(8,128)(2,1)S(1)} %slice.98), channel_id=1, source_target_pairs={{0,2},{2,0},{4,6},{6,4},{8,10},{10,8},{12,14},{14,12},{1,3},{3,1},... | collective-permute-start | bytes 516104 | tf_op jit(solution)/shard_map/ppermute | solution.py:292
  65.6 2.3 %gate_up.18.kept_ref.refs_0_ = f32[48,3072]{1,0:T(8,128)S(1)} custom-call(bf16[48,2176]{1,0:T(8,128)(2,1)S(1)} %pad_maximum_fusion.3.rows_ref, bf16[2,2048,768]{2,1,0:T(8,128)(2,1)S(1)} %get-tuple-element.25.gate_held, bf16[2,2048,768]{2,1,0:T(8,128)(2,1)S(1)} %get-tuple-element.26.up_held, f32[88,2048]{1,0:T(8,128)S(1)} %down.18.refs_0_), custom_call_target="tpu_custom_call" | custom-call | flops 3221225472 | tf_op jit(solution)/shard_map/gate_up/pallas_call | solution.py:187
  67.9 1.9 %collective-permute-start.16 = (bf16[42,2048]{1,0:T(8,128)(2,1)S(1)}, bf16[42,2048]{1,0:T(8,128)(2,1)S(1)}, u32[]{:S(2)}, u32[]{:S(2)}) collective-permute-start(bf16[42,2048]{1,0:T(8,128)(2,1)S(1)} %fusion.1.refs_1_), channel_id=1, source_target_pairs={{0,12},{2,14},{4,8},{6,10},{8,4},{10,6},{12,0},{14,2},{1,13},{3,15... | collective-permute-start | bytes 516104 | tf_op jit(solution)/shard_map/ppermute | solution.py:292
  70.4 2.9 %collective-permute-done.17.hidden_ref = bf16[88,1536]{1,0:T(8,128)(2,1)S(1)} collective-permute-done((bf16[88,1536]{1,0:T(8,128)(2,1)S(1)}, bf16[88,1536]{1,0:T(8,128)(2,1)S(1)}, u32[]{:S(2)}, u32[]{:S(2)}) %collective-permute-start.17) | collective-permute-done | bytes 270368 | tf_op jit(solution)/shard_map/ppermute | solution.py:289
  75.8 1.8 %collective-permute-start.19 = (bf16[42,2048]{1,0:T(8,128)(2,1)S(1)}, bf16[42,2048]{1,0:T(8,128)(2,1)S(1)}, u32[]{:S(2)}, u32[]{:S(2)}) collective-permute-start(bf16[42,2048]{1,0:T(8,128)(2,1)S(1)} %slice.86), channel_id=1, source_target_pairs={{0,2},{2,0},{4,6},{6,4},{8,10},{10,8},{12,14},{14,12},{1,3},{3,1},... | collective-permute-start | bytes 516104 | tf_op jit(solution)/shard_map/ppermute | solution.py:292
  77.6 2.2 %gate_up.19.kept_ref.refs_0_ = f32[32,3072]{1,0:T(8,128)S(1)} custom-call(bf16[32,2176]{1,0:T(8,128)(2,1)S(1)} %slice.80.rows_ref, bf16[2,2048,768]{2,1,0:T(8,128)(2,1)S(1)} %get-tuple-element.25.gate_held, bf16[2,2048,768]{2,1,0:T(8,128)(2,1)S(1)} %get-tuple-element.26.up_held, f32[48,2048]{1,0:T(8,128)S(1)} %down.20.refs_0_), custom_call_target="tpu_custom_call" | custom-call | flops 3221225472 | tf_op jit(solution)/shard_map/gate_up/pallas_call | solution.py:187
  79.9 2.6 %collective-permute-start.20 = (bf16[42,2048]{1,0:T(8,128)(2,1)S(1)}, bf16[42,2048]{1,0:T(8,128)(2,1)S(1)}, u32[]{:S(2)}, u32[]{:S(2)}) collective-permute-start(bf16[42,2048]{1,0:T(8,128)(2,1)S(1)} %fusion.refs_1_), channel_id=1, source_target_pairs={{0,8},{2,10},{4,12},{6,14},{8,0},{10,2},{12,4},{14,6},{1,9},{3,11}... | collective-permute-start | bytes 516104 | tf_op jit(solution)/shard_map/ppermute | solution.py:292
  89.3 5.6 %collective-permute-done.23 = bf16[42,2048]{1,0:T(8,128)(2,1)S(1)} collective-permute-done((bf16[42,2048]{1,0:T(8,128)(2,1)S(1)}, bf16[42,2048]{1,0:T(8,128)(2,1)S(1)}, u32[]{:S(2)}, u32[]{:S(2)}) %collective-permute-start.23) | collective-permute-done | bytes 172064 | tf_op jit(solution)/shard_map/ppermute | solution.py:292
  (86 shorter events, 30.3 us)
Async XLA Ops:
  1.1 7.9 %collective-permute-start = (bf16[42,2176]{1,0:T(8,128)(2,1)S(1)}, bf16[42,2176]{1,0:T(8,128)(2,1)S(1)}, u32[]{:S(2)}, u32[]{:S(2)}) collective-permute-start(bf16[42,2176]{1,0:T(8,128)(2,1)S(1)} %prepare.1), channel_id=1, source_target_pairs={{0,4},{2,6},{4,0},{6,2},{8,12},{10,14},{12,8},{14,10},{1,5},{3,7},... | collective-permute-start | bytes 548360 | tf_op jit(solution)/shard_map/ppermute | solution.py:292
  1.4 21.2 %collective-permute-start.3 = (bf16[42,2176]{1,0:T(8,128)(2,1)S(1)}, bf16[42,2176]{1,0:T(8,128)(2,1)S(1)}, u32[]{:S(2)}, u32[]{:S(2)}) collective-permute-start(bf16[42,2176]{1,0:T(8,128)(2,1)S(1)} %prepare.1), channel_id=1, source_target_pairs={{0,12},{2,14},{4,8},{6,10},{8,4},{10,6},{12,0},{14,2},{1,13},{3,15... | collective-permute-start | bytes 548360 | tf_op jit(solution)/shard_map/ppermute | solution.py:292
  7.7 14.5 %collective-permute-start.1 = (bf16[32,3072]{1,0:T(8,128)(2,1)S(1)}, bf16[32,3072]{1,0:T(8,128)(2,1)S(1)}, u32[]{:S(2)}, u32[]{:S(2)}) collective-permute-start(bf16[32,3072]{1,0:T(8,128)(2,1)S(1)} %get-tuple-element.22.refs_0_), channel_id=1, source_target_pairs={{0,1},{1,0},{2,3},{3,2},{4,5},{5,4},{6,7},{7,6},{8,9},{9,8},{10,11... | collective-permute-start | bytes 589832 | tf_op jit(solution)/shard_map/ppermute | solution.py:289
  11.4 14.2 %collective-permute-start.10 = (bf16[42,2176]{1,0:T(8,128)(2,1)S(1)}, bf16[42,2176]{1,0:T(8,128)(2,1)S(1)}, u32[]{:S(2)}, u32[]{:S(2)}) collective-permute-start(bf16[42,2176]{1,0:T(8,128)(2,1)S(1)} %prepare.1), channel_id=1, source_target_pairs={{0,2},{2,0},{4,6},{6,4},{8,10},{10,8},{12,14},{14,12},{1,3},{3,1},... | collective-permute-start | bytes 548360 | tf_op jit(solution)/shard_map/ppermute | solution.py:292
  15.7 14.8 %collective-permute-start.8 = (bf16[42,2176]{1,0:T(8,128)(2,1)S(1)}, bf16[42,2176]{1,0:T(8,128)(2,1)S(1)}, u32[]{:S(2)}, u32[]{:S(2)}) collective-permute-start(bf16[42,2176]{1,0:T(8,128)(2,1)S(1)} %prepare.1), channel_id=1, source_target_pairs={{0,8},{2,10},{4,12},{6,14},{8,0},{10,2},{12,4},{14,6},{1,9},{3,11}... | collective-permute-start | bytes 548360 | tf_op jit(solution)/shard_map/ppermute | solution.py:292
  15.7 10.1 %collective-permute-start.5 = (bf16[48,3072]{1,0:T(8,128)(2,1)S(1)}, bf16[48,3072]{1,0:T(8,128)(2,1)S(1)}, u32[]{:S(2)}, u32[]{:S(2)}) collective-permute-start(bf16[48,3072]{1,0:T(8,128)(2,1)S(1)} %gate_up.10.refs_0_), channel_id=1, source_target_pairs={{0,1},{1,0},{2,3},{3,2},{4,5},{5,4},{6,7},{7,6},{8,9},{9,8},{10,11... | collective-permute-start | bytes 884744 | tf_op jit(solution)/shard_map/ppermute | solution.py:289
  22.2 25.8 %collective-permute-start.2 = (bf16[32,1536]{1,0:T(8,128)(2,1)S(1)}, bf16[32,1536]{1,0:T(8,128)(2,1)S(1)}, u32[]{:S(2)}, u32[]{:S(2)}) collective-permute-start(bf16[32,1536]{1,0:T(8,128)(2,1)S(1)} %hidden.6.refs_0_.hidden_ref), channel_id=1, source_target_pairs={{0,1},{1,0},{2,3},{3,2},{4,5},{5,4},{6,7},{7,6},{8,9},{9,8},{10,11... | collective-permute-start | bytes 294920 | tf_op jit(solution)/shard_map/ppermute | solution.py:289
  26.0 23.2 %collective-permute-start.11 = (bf16[48,1536]{1,0:T(8,128)(2,1)S(1)}, bf16[48,1536]{1,0:T(8,128)(2,1)S(1)}, u32[]{:S(2)}, u32[]{:S(2)}) collective-permute-start(bf16[48,1536]{1,0:T(8,128)(2,1)S(1)} %hidden.7.refs_2_.hidden_ref), channel_id=1, source_target_pairs={{0,1},{1,0},{2,3},{3,2},{4,5},{5,4},{6,7},{7,6},{8,9},{9,8},{10,11... | collective-permute-start | bytes 442376 | tf_op jit(solution)/shard_map/ppermute | solution.py:289
  30.1 13.7 %collective-permute-start.7 = (bf16[88,3072]{1,0:T(8,128)(2,1)S(1)}, bf16[88,3072]{1,0:T(8,128)(2,1)S(1)}, u32[]{:S(2)}, u32[]{:S(2)}) collective-permute-start(bf16[88,3072]{1,0:T(8,128)(2,1)S(1)} %get-tuple-element.27.refs_2_), channel_id=1, source_target_pairs={{0,1},{1,0},{2,3},{3,2},{4,5},{5,4},{6,7},{7,6},{8,9},{9,8},{10,11... | collective-permute-start | bytes 1622024 | tf_op jit(solution)/shard_map/ppermute | solution.py:289
  30.5 4.9 %collective-permute-start.9 = (bf16[42,2176]{1,0:T(8,128)(2,1)S(1)}, bf16[42,2176]{1,0:T(8,128)(2,1)S(1)}, u32[]{:S(2)}, u32[]{:S(2)}) collective-permute-start(bf16[42,2176]{1,0:T(8,128)(2,1)S(1)} %collective-permute-done.8), channel_id=1, source_target_pairs={{0,2},{2,0},{4,6},{6,4},{8,10},{10,8},{12,14},{14,12},{1,3},{3,1},... | collective-permute-start | bytes 548360 | tf_op jit(solution)/shard_map/ppermute | solution.py:292
  33.9 10.4 %collective-permute-start.6 = (bf16[42,2176]{1,0:T(8,128)(2,1)S(1)}, bf16[42,2176]{1,0:T(8,128)(2,1)S(1)}, u32[]{:S(2)}, u32[]{:S(2)}) collective-permute-start(bf16[42,2176]{1,0:T(8,128)(2,1)S(1)} %prepare.1), channel_id=1, source_target_pairs={{0,6},{2,4},{4,2},{6,0},{8,14},{10,12},{12,10},{14,8},{1,7},{3,5},... | collective-permute-start | bytes 548360 | tf_op jit(solution)/shard_map/ppermute | solution.py:292
  37.6 17.8 %collective-permute-start.13 = (bf16[88,3072]{1,0:T(8,128)(2,1)S(1)}, bf16[88,3072]{1,0:T(8,128)(2,1)S(1)}, u32[]{:S(2)}, u32[]{:S(2)}) collective-permute-start(bf16[88,3072]{1,0:T(8,128)(2,1)S(1)} %gate_up.14.refs_0_), channel_id=1, source_target_pairs={{0,1},{1,0},{2,3},{3,2},{4,5},{5,4},{6,7},{7,6},{8,9},{9,8},{10,11... | collective-permute-start | bytes 1622024 | tf_op jit(solution)/shard_map/ppermute | solution.py:289
  44.1 17.1 %collective-permute-start.12 = (bf16[88,1536]{1,0:T(8,128)(2,1)S(1)}, bf16[88,1536]{1,0:T(8,128)(2,1)S(1)}, u32[]{:S(2)}, u32[]{:S(2)}) collective-permute-start(bf16[88,1536]{1,0:T(8,128)(2,1)S(1)} %hidden.8.refs_0_.hidden_ref), channel_id=1, source_target_pairs={{0,1},{1,0},{2,3},{3,2},{4,5},{5,4},{6,7},{7,6},{8,9},{9,8},{10,11... | collective-permute-start | bytes 811016 | tf_op jit(solution)/shard_map/ppermute | solution.py:289
  46.7 23.2 %collective-permute-start.18 = (bf16[48,3072]{1,0:T(8,128)(2,1)S(1)}, bf16[48,3072]{1,0:T(8,128)(2,1)S(1)}, u32[]{:S(2)}, u32[]{:S(2)}) collective-permute-start(bf16[48,3072]{1,0:T(8,128)(2,1)S(1)} %gate_up.15.refs_1_), channel_id=1, source_target_pairs={{0,1},{1,0},{2,3},{3,2},{4,5},{5,4},{6,7},{7,6},{8,9},{9,8},{10,11... | collective-permute-start | bytes 884744 | tf_op jit(solution)/shard_map/ppermute | solution.py:289
  50.4 38.9 %collective-permute-start.14 = (bf16[42,2048]{1,0:T(8,128)(2,1)S(1)}, bf16[42,2048]{1,0:T(8,128)(2,1)S(1)}, u32[]{:S(2)}, u32[]{:S(2)}) collective-permute-start(bf16[42,2048]{1,0:T(8,128)(2,1)S(1)} %slice.99), channel_id=1, source_target_pairs={{0,4},{2,6},{4,0},{6,2},{8,12},{10,14},{12,8},{14,10},{1,5},{3,7},... | collective-permute-start | bytes 516104 | tf_op jit(solution)/shard_map/ppermute | solution.py:292
  55.6 17.6 %collective-permute-start.17 = (bf16[88,1536]{1,0:T(8,128)(2,1)S(1)}, bf16[88,1536]{1,0:T(8,128)(2,1)S(1)}, u32[]{:S(2)}, u32[]{:S(2)}) collective-permute-start(bf16[88,1536]{1,0:T(8,128)(2,1)S(1)} %hidden.9.refs_0_.hidden_ref), channel_id=1, source_target_pairs={{0,1},{1,0},{2,3},{3,2},{4,5},{5,4},{6,7},{7,6},{8,9},{9,8},{10,11... | collective-permute-start | bytes 811016 | tf_op jit(solution)/shard_map/ppermute | solution.py:289
  58.2 24.3 %collective-permute-start.22 = (bf16[32,3072]{1,0:T(8,128)(2,1)S(1)}, bf16[32,3072]{1,0:T(8,128)(2,1)S(1)}, u32[]{:S(2)}, u32[]{:S(2)}) collective-permute-start(bf16[32,3072]{1,0:T(8,128)(2,1)S(1)} %gate_up.17.refs_1_), channel_id=1, source_target_pairs={{0,1},{1,0},{2,3},{3,2},{4,5},{5,4},{6,7},{7,6},{8,9},{9,8},{10,11... | collective-permute-start | bytes 589832 | tf_op jit(solution)/shard_map/ppermute | solution.py:289
  63.7 4.2 %collective-permute-start.15 = (bf16[42,2048]{1,0:T(8,128)(2,1)S(1)}, bf16[42,2048]{1,0:T(8,128)(2,1)S(1)}, u32[]{:S(2)}, u32[]{:S(2)}) collective-permute-start(bf16[42,2048]{1,0:T(8,128)(2,1)S(1)} %slice.98), channel_id=1, source_target_pairs={{0,2},{2,0},{4,6},{6,4},{8,10},{10,8},{12,14},{14,12},{1,3},{3,1},... | collective-permute-start | bytes 516104 | tf_op jit(solution)/shard_map/ppermute | solution.py:292
  67.9 21.4 %collective-permute-start.16 = (bf16[42,2048]{1,0:T(8,128)(2,1)S(1)}, bf16[42,2048]{1,0:T(8,128)(2,1)S(1)}, u32[]{:S(2)}, u32[]{:S(2)}) collective-permute-start(bf16[42,2048]{1,0:T(8,128)(2,1)S(1)} %fusion.1.refs_1_), channel_id=1, source_target_pairs={{0,12},{2,14},{4,8},{6,10},{8,4},{10,6},{12,0},{14,2},{1,13},{3,15... | collective-permute-start | bytes 516104 | tf_op jit(solution)/shard_map/ppermute | solution.py:292
  70.0 12.9 %collective-permute-start.21 = (bf16[48,1536]{1,0:T(8,128)(2,1)S(1)}, bf16[48,1536]{1,0:T(8,128)(2,1)S(1)}, u32[]{:S(2)}, u32[]{:S(2)}) collective-permute-start(bf16[48,1536]{1,0:T(8,128)(2,1)S(1)} %hidden.10.refs_1_.hidden_ref), channel_id=1, source_target_pairs={{0,1},{1,0},{2,3},{3,2},{4,5},{5,4},{6,7},{7,6},{8,9},{9,8},{10,11... | collective-permute-start | bytes 442376 | tf_op jit(solution)/shard_map/ppermute | solution.py:289
  79.9 15.0 %collective-permute-start.20 = (bf16[42,2048]{1,0:T(8,128)(2,1)S(1)}, bf16[42,2048]{1,0:T(8,128)(2,1)S(1)}, u32[]{:S(2)}, u32[]{:S(2)}) collective-permute-start(bf16[42,2048]{1,0:T(8,128)(2,1)S(1)} %fusion.refs_1_), channel_id=1, source_target_pairs={{0,8},{2,10},{4,12},{6,14},{8,0},{10,2},{12,4},{14,6},{1,9},{3,11}... | collective-permute-start | bytes 516104 | tf_op jit(solution)/shard_map/ppermute | solution.py:292
  82.7 4.2 %collective-permute-start.24 = (bf16[32,1536]{1,0:T(8,128)(2,1)S(1)}, bf16[32,1536]{1,0:T(8,128)(2,1)S(1)}, u32[]{:S(2)}, u32[]{:S(2)}) collective-permute-start(bf16[32,1536]{1,0:T(8,128)(2,1)S(1)} %hidden.11.refs_1_.hidden_ref), channel_id=1, source_target_pairs={{0,1},{1,0},{2,3},{3,2},{4,5},{5,4},{6,7},{7,6},{8,9},{9,8},{10,11... | collective-permute-start | bytes 294920 | tf_op jit(solution)/shard_map/ppermute | solution.py:289
  84.2 10.7 %collective-permute-start.23 = (bf16[42,2048]{1,0:T(8,128)(2,1)S(1)}, bf16[42,2048]{1,0:T(8,128)(2,1)S(1)}, u32[]{:S(2)}, u32[]{:S(2)}) collective-permute-start(bf16[42,2048]{1,0:T(8,128)(2,1)S(1)} %bitcast.5), channel_id=1, source_target_pairs={{0,6},{2,4},{4,2},{6,0},{8,14},{10,12},{12,10},{14,8},{1,7},{3,5},... | collective-permute-start | bytes 516104 | tf_op jit(solution)/shard_map/ppermute | solution.py:292
  88.1 6.8 %collective-permute-start.25 = (bf16[42,2048]{1,0:T(8,128)(2,1)S(1)}, bf16[42,2048]{1,0:T(8,128)(2,1)S(1)}, u32[]{:S(2)}, u32[]{:S(2)}) collective-permute-start(bf16[42,2048]{1,0:T(8,128)(2,1)S(1)} %pad_maximum_fusion.4), channel_id=1, source_target_pairs={{0,2},{2,0},{4,6},{6,4},{8,10},{10,8},{12,14},{14,12},{1,3},{3,1},... | collective-permute-start | bytes 516104 | tf_op jit(solution)/shard_map/ppermute | solution.py:292
  (4 other events, 13.2 us)

commit v4 on v3

--- a/solution.py
+++ b/solution.py
@@ -256,7 +256,7 @@
         out_ref[:, columns] = value
 
 
-def down(hidden, held, so_far, after):
+def down(hidden, held, so_far, after, weight=1):
     count = hidden.shape[0]
     experts, half, width = held.shape
     extra = [] if so_far is None else [so_far]
@@ -267,7 +267,7 @@
         out_shape=jax.ShapeDtypeStruct((count, width), jnp.float32),
         compiler_params=pltpu.CompilerParams(vmem_limit_bytes=SMALL),
         cost_estimate=pl.CostEstimate(
-            flops=2 * max(count, 256) * width * half * experts,
+            flops=weight * 2 * max(count, 256) * width * half * experts,
             bytes_accessed=0,
             transcendentals=0,
         ),
@@ -304,7 +304,7 @@
 
     own = prepare(tokens, route_ids, route_scores)
     near_same = swap_expert(own, near)
-    came = [swap_expert(own, mask) for mask in far[:1]]
+    came = [swap_expert(own, mask) for mask in far]
     theirs, received, kept, hidden, arrived, begun, outs, chunks = {}, {}, {}, {}, {}, {}, {}, {}
     parts, back, after = {}, [], []
 
@@ -345,7 +345,7 @@
         after[:] = [hidden[i]]
 
     def begin_down(i):
-        begun[i] = down(hidden[i], down_mine, None, after)
+        begun[i] = down(hidden[i], down_mine, None, after, 3 if i == last - 1 else 1)
         after[:] = [begun[i]]
 
     def end_down(i):
@@ -364,11 +364,9 @@
     after[:] = [theirs[0]]
     bring(1, [near_same])
     send_theirs(1)
-    waiting = later(own, theirs[1])
-    partner = swap_expert(waiting, 1)
-    came += [swap_expert(waiting, mask) for mask in far[1:]]
     kept[0], gate_mine, up_mine = gate_up_load(mine, chunks[0], w_gate, w_up, after, f32)
     after[:] = [kept[0]]
+    partner = swap_expert(later(own, kept[0]), 1)
     send_hidden(0)
     if far:
         bring_far(2)
@@ -398,10 +396,12 @@
             else:
                 bring_far(i + 2)
             send_theirs(i + 2)
+        if i == last - 1:
+            keep(last)
         for early in (0, 1) if i == 2 else (i - 1,):
             end_down(early)
         begin_down(i)
-        if i < last:
+        if i + 1 < last:
             keep(i + 1)
         if i - 1 in parts:
             after.append(parts[i - 1])

time: 95.9 us -> 94.1 us (0.981)
  the two profiles are of different devices: /device:TPU:25 before, /device:TPU:0 now
where the time goes in v4:
time: 94.1 us; the launch traced here: 94 us
  Pallas kernels  50.8 us (54%)
  starting transfers between devices  32.7 us (35%)
  waiting for transfers between devices  8.48 us (9%)
  other arithmetic  1.29 us (1%)
    pallas_call x10, Pallas kernels, gate_up(): pl.pallas_call(functools.partial(gate_up_kernel, load), in_specs=specs +...  23.9 us
    ppermute x14, starting transfers between devices, swap_expert(): return lax.ppermute(value, 'expert', [(i, i ^ mask) for i in range(groups)])  18.6 us
    pallas_call x12, Pallas kernels, down(): pl.pallas_call(functools.partial(down_kernel, len(extra)), in_specs=[VMEM...  14.4 us
    ppermute x12, starting transfers between devices, swap_tensor(): return lax.ppermute(value, 'tensor', [(0, 1), (1, 0)])  14.1 us
    pallas_call x2, Pallas kernels, gate_up_load(): pl.pallas_call(functools.partial(gate_up_load_kernel, compute), in_specs=...  10.4 us
    ppermute x14, waiting for transfers between devices, swap_expert(): return lax.ppermute(value, 'expert', [(i, i ^ mask) for i in range(groups)])  5.14 us
    ppermute x12, waiting for transfers between devices, swap_tensor(): return lax.ppermute(value, 'tensor', [(0, 1), (1, 0)])  3.34 us
  transfers between devices with their start and end apart: 26, of which 4 were waited for; matrix products, arithmetic and copies ran while one was open for 1% of the time, Pallas kernels for 53%

profile of v4, /device:TPU:0, one launch (start us, length us, event | category | flops | bytes accessed | tf_op | source)
XLA Modules:
  0.0 94.0 jit_solution(14003606249757562127)
XLA Ops:
  1.1 3.1 %collective-permute-start = (bf16[42,2176]{1,0:T(8,128)(2,1)S(1)}, bf16[42,2176]{1,0:T(8,128)(2,1)S(1)}, u32[]{:S(2)}, u32[]{:S(2)}) collective-permute-start(bf16[42,2176]{1,0:T(8,128)(2,1)S(1)} %prepare.1), channel_id=1, source_target_pairs={{0,4},{2,6},{4,0},{6,2},{8,12},{10,14},{12,8},{14,10},{1,5},{3,7},... | collective-permute-start | bytes 548360 | tf_op jit(solution)/shard_map/ppermute | solution.py:292
  4.2 2.6 %collective-permute-start.8 = (bf16[42,2176]{1,0:T(8,128)(2,1)S(1)}, bf16[42,2176]{1,0:T(8,128)(2,1)S(1)}, u32[]{:S(2)}, u32[]{:S(2)}) collective-permute-start(bf16[42,2176]{1,0:T(8,128)(2,1)S(1)} %prepare.1), channel_id=1, source_target_pairs={{0,8},{2,10},{4,12},{6,14},{8,0},{10,2},{12,4},{14,6},{1,9},{3,11}... | collective-permute-start | bytes 548360 | tf_op jit(solution)/shard_map/ppermute | solution.py:292
  6.8 5.2 %gate_up_load.2 = (bf16[32,3072]{1,0:T(8,128)(2,1)S(1)}, bf16[2,2048,768]{2,1,0:T(8,128)(2,1)S(1)}, bf16[2,2048,768]{2,1,0:T(8,128)(2,1)S(1)}) custom-call(s32[1]{0:T(128)S(6)} %sub.3.side_ref.refs_0_, bf16[32,2176]{1,0:T(8,128)(2,1)S(1)} %slice.74.rows_ref, bf16[2,2048,1536]{2,1,0:T(8,128)(2,1)} %gate_ref.3, bf16[2,2048,1536]{2,1,0:T(8,128)(2,1)} %up_ref.3, ...), custom_call_target="tpu_custom_call" | custom-call | flops 402653184 | bytes 12582912 | tf_op jit(solution)/shard_map/gate_up_load/pallas_call | solution.py:133
  12.1 1.8 %collective-permute-start.1 = (bf16[32,3072]{1,0:T(8,128)(2,1)S(1)}, bf16[32,3072]{1,0:T(8,128)(2,1)S(1)}, u32[]{:S(2)}, u32[]{:S(2)}) collective-permute-start(bf16[32,3072]{1,0:T(8,128)(2,1)S(1)} %get-tuple-element.22.refs_0_), channel_id=1, source_target_pairs={{0,1},{1,0},{2,3},{3,2},{4,5},{5,4},{6,7},{7,6},{8,9},{9,8},{10,11... | collective-permute-start | bytes 589832 | tf_op jit(solution)/shard_map/ppermute | solution.py:289
  13.9 2.3 %gate_up.10.refs_0_ = bf16[48,3072]{1,0:T(8,128)(2,1)S(1)} custom-call(bf16[48,2176]{1,0:T(8,128)(2,1)S(1)} %pad_maximum_fusion.2.rows_ref, bf16[2,2048,768]{2,1,0:T(8,128)(2,1)S(1)} %get-tuple-element.20.gate_held, bf16[2,2048,768]{2,1,0:T(8,128)(2,1)S(1)} %get-tuple-element.21.up_held, bf16[32,3072]{1,0:T(8,128)(2,1)S(1)} %get-tuple-element.22.refs_0_), custom_call_target="tpu_custom_call" | custom-call | flops 3221225472 | tf_op jit(solution)/shard_map/gate_up/pallas_call | solution.py:187
  17.2 5.2 %gate_up_load.3 = (f32[32,3072]{1,0:T(8,128)S(1)}, bf16[2,2048,768]{2,1,0:T(8,128)(2,1)S(1)}, bf16[2,2048,768]{2,1,0:T(8,128)(2,1)S(1)}) custom-call(s32[1]{0:T(128)} %bitcast.3.refs_1_.side_ref.refs_0_, bf16[32,2176]{1,0:T(8,128)(2,1)S(1)} %slice.74.rows_ref, bf16[2,2048,1536]{2,1,0:T(8,128)(2,1)} %gate_ref.3, bf16[2,2048,1536]{2,1,0:T(8,128)(2,1)} %up_ref.3, ...), custom_call_target="tpu_custom_call" | custom-call | flops 402653184 | bytes 12582912 | tf_op jit(solution)/shard_map/gate_up_load/pallas_call | solution.py:133
  24.0 2.3 %gate_up.11.kept_ref.refs_0_ = f32[48,3072]{1,0:T(8,128)S(1)} custom-call(bf16[48,2176]{1,0:T(8,128)(2,1)S(1)} %pad_maximum_fusion.2.rows_ref, bf16[2,2048,768]{2,1,0:T(8,128)(2,1)S(1)} %get-tuple-element.25.gate_held, bf16[2,2048,768]{2,1,0:T(8,128)(2,1)S(1)} %get-tuple-element.26.up_held, bf16[32,1536]{1,0:T(8,128)(2,1)S(1)} %hidden.6.refs_0_.hidden_ref), custom_call_target="tpu_custom_call" | custom-call | flops 3221225472 | tf_op jit(solution)/shard_map/gate_up/pallas_call | solution.py:187
  27.6 2.9 %gate_up.12 = (bf16[88,3072]{1,0:T(8,128)(2,1)S(1)}, bf16[2,768,2048]{2,1,0:T(8,128)(2,1)S(1)}) custom-call(bf16[88,2176]{1,0:T(8,128)(2,1)S(1)} %pad_maximum_fusion.rows_ref, bf16[2,2048,768]{2,1,0:T(8,128)(2,1)S(1)} %get-tuple-element.20.gate_held, bf16[2,2048,768]{2,1,0:T(8,128)(2,1)S(1)} %get-tuple-element.21.up_held, s32[1]{0:T(128)} %bitcast.3.refs_1_.side_ref.refs_0_, ...), custom_call_target="tpu_custom_call" | custom-call | flops 3221225472 | tf_op jit(solution)/shard_map/gate_up/pallas_call | solution.py:187
  31.7 2.9 %gate_up.13 = (f32[88,3072]{1,0:T(8,128)S(1)}, bf16[2,768,2048]{2,1,0:T(8,128)(2,1)S(1)}) custom-call(bf16[88,2176]{1,0:T(8,128)(2,1)S(1)} %pad_maximum_fusion.rows_ref, bf16[2,2048,768]{2,1,0:T(8,128)(2,1)S(1)} %get-tuple-element.25.gate_held, bf16[2,2048,768]{2,1,0:T(8,128)(2,1)S(1)} %get-tuple-element.26.up_held, s32[1]{0:T(128)S(6)} %sub.3.side_ref.refs_0_, ...), custom_call_target="tpu_custom_call" | custom-call | flops 3221225472 | tf_op jit(solution)/shard_map/gate_up/pallas_call | solution.py:187
  34.6 2.0 %collective-permute-start.6 = (bf16[42,2176]{1,0:T(8,128)(2,1)S(1)}, bf16[42,2176]{1,0:T(8,128)(2,1)S(1)}, u32[]{:S(2)}, u32[]{:S(2)}) collective-permute-start(bf16[42,2176]{1,0:T(8,128)(2,1)S(1)} %prepare.1), channel_id=1, source_target_pairs={{0,6},{2,4},{4,2},{6,0},{8,14},{10,12},{12,10},{14,8},{1,7},{3,5},... | collective-permute-start | bytes 548360 | tf_op jit(solution)/shard_map/ppermute | solution.py:292
  38.0 2.2 %gate_up.14.refs_0_ = bf16[88,3072]{1,0:T(8,128)(2,1)S(1)} custom-call(bf16[88,2176]{1,0:T(8,128)(2,1)S(1)} %pad_maximum_fusion.1.rows_ref, bf16[2,2048,768]{2,1,0:T(8,128)(2,1)S(1)} %get-tuple-element.20.gate_held, bf16[2,2048,768]{2,1,0:T(8,128)(2,1)S(1)} %get-tuple-element.21.up_held, f32[32,2048]{1,0:T(8,128)S(1)} %down.12.refs_0_), custom_call_target="tpu_custom_call" | custom-call | flops 3221225472 | tf_op jit(solution)/shard_map/gate_up/pallas_call | solution.py:187
  40.2 1.6 %collective-permute-start.13 = (bf16[88,3072]{1,0:T(8,128)(2,1)S(1)}, bf16[88,3072]{1,0:T(8,128)(2,1)S(1)}, u32[]{:S(2)}, u32[]{:S(2)}) collective-permute-start(bf16[88,3072]{1,0:T(8,128)(2,1)S(1)} %gate_up.14.refs_0_), channel_id=1, source_target_pairs={{0,1},{1,0},{2,3},{3,2},{4,5},{5,4},{6,7},{7,6},{8,9},{9,8},{10,11... | collective-permute-start | bytes 1622024 | tf_op jit(solution)/shard_map/ppermute | solution.py:289
  43.0 2.7 %collective-permute-done.7.received_ref = bf16[88,3072]{1,0:T(8,128)(2,1)S(1)} collective-permute-done((bf16[88,3072]{1,0:T(8,128)(2,1)S(1)}, bf16[88,3072]{1,0:T(8,128)(2,1)S(1)}, u32[]{:S(2)}, u32[]{:S(2)}) %collective-permute-start.7) | collective-permute-done | bytes 540704 | tf_op jit(solution)/shard_map/ppermute | solution.py:289
  47.2 2.3 %gate_up.15.refs_1_ = bf16[48,3072]{1,0:T(8,128)(2,1)S(1)} custom-call(bf16[48,2176]{1,0:T(8,128)(2,1)S(1)} %pad_maximum_fusion.3.rows_ref, bf16[2,2048,768]{2,1,0:T(8,128)(2,1)S(1)} %get-tuple-element.20.gate_held, bf16[2,2048,768]{2,1,0:T(8,128)(2,1)S(1)} %get-tuple-element.21.up_held, bf16[88,1536]{1,0:T(8,128)(2,1)S(1)} %hidden.8.refs_0_.hidden_ref), custom_call_target="tpu_custom_call" | custom-call | flops 3221225472 | tf_op jit(solution)/shard_map/gate_up/pallas_call | solution.py:187
  52.9 2.4 %collective-permute-start.14 = (bf16[42,2048]{1,0:T(8,128)(2,1)S(1)}, bf16[42,2048]{1,0:T(8,128)(2,1)S(1)}, u32[]{:S(2)}, u32[]{:S(2)}) collective-permute-start(bf16[42,2048]{1,0:T(8,128)(2,1)S(1)} %slice.99), channel_id=1, source_target_pairs={{0,4},{2,6},{4,0},{6,2},{8,12},{10,14},{12,8},{14,10},{1,5},{3,7},... | collective-permute-start | bytes 516104 | tf_op jit(solution)/shard_map/ppermute | solution.py:292
  56.5 2.2 %gate_up.16.kept_ref.refs_0_ = f32[88,3072]{1,0:T(8,128)S(1)} custom-call(bf16[88,2176]{1,0:T(8,128)(2,1)S(1)} %pad_maximum_fusion.1.rows_ref, bf16[2,2048,768]{2,1,0:T(8,128)(2,1)S(1)} %get-tuple-element.25.gate_held, bf16[2,2048,768]{2,1,0:T(8,128)(2,1)S(1)} %get-tuple-element.26.up_held, f32[88,2048]{1,0:T(8,128)S(1)} %down.16.refs_0_), custom_call_target="tpu_custom_call" | custom-call | flops 3221225472 | tf_op jit(solution)/shard_map/gate_up/pallas_call | solution.py:187
  59.5 2.2 %gate_up.17.refs_1_ = bf16[32,3072]{1,0:T(8,128)(2,1)S(1)} custom-call(bf16[32,2176]{1,0:T(8,128)(2,1)S(1)} %slice.80.rows_ref, bf16[2,2048,768]{2,1,0:T(8,128)(2,1)S(1)} %get-tuple-element.20.gate_held, bf16[2,2048,768]{2,1,0:T(8,128)(2,1)S(1)} %get-tuple-element.21.up_held, bf16[88,1536]{1,0:T(8,128)(2,1)S(1)} %hidden.9.refs_0_.hidden_ref), custom_call_target="tpu_custom_call" | custom-call | flops 3221225472 | tf_op jit(solution)/shard_map/gate_up/pallas_call | solution.py:187
  61.8 1.5 %collective-permute-start.22 = (bf16[32,3072]{1,0:T(8,128)(2,1)S(1)}, bf16[32,3072]{1,0:T(8,128)(2,1)S(1)}, u32[]{:S(2)}, u32[]{:S(2)}) collective-permute-start(bf16[32,3072]{1,0:T(8,128)(2,1)S(1)} %gate_up.17.refs_1_), channel_id=1, source_target_pairs={{0,1},{1,0},{2,3},{3,2},{4,5},{5,4},{6,7},{7,6},{8,9},{9,8},{10,11... | collective-permute-start | bytes 589832 | tf_op jit(solution)/shard_map/ppermute | solution.py:289
  66.0 2.3 %gate_up.18.kept_ref.refs_0_ = f32[48,3072]{1,0:T(8,128)S(1)} custom-call(bf16[48,2176]{1,0:T(8,128)(2,1)S(1)} %pad_maximum_fusion.3.rows_ref, bf16[2,2048,768]{2,1,0:T(8,128)(2,1)S(1)} %get-tuple-element.25.gate_held, bf16[2,2048,768]{2,1,0:T(8,128)(2,1)S(1)} %get-tuple-element.26.up_held, f32[88,2048]{1,0:T(8,128)S(1)} %down.18.refs_0_), custom_call_target="tpu_custom_call" | custom-call | flops 3221225472 | tf_op jit(solution)/shard_map/gate_up/pallas_call | solution.py:187
  68.4 3.1 %collective-permute-start.16 = (bf16[42,2048]{1,0:T(8,128)(2,1)S(1)}, bf16[42,2048]{1,0:T(8,128)(2,1)S(1)}, u32[]{:S(2)}, u32[]{:S(2)}) collective-permute-start(bf16[42,2048]{1,0:T(8,128)(2,1)S(1)} %fusion.1.refs_1_), channel_id=1, source_target_pairs={{0,12},{2,14},{4,8},{6,10},{8,4},{10,6},{12,0},{14,2},{1,13},{3,15... | collective-permute-start | bytes 516104 | tf_op jit(solution)/shard_map/ppermute | solution.py:292
  71.6 1.6 %collective-permute-start.21 = (bf16[48,1536]{1,0:T(8,128)(2,1)S(1)}, bf16[48,1536]{1,0:T(8,128)(2,1)S(1)}, u32[]{:S(2)}, u32[]{:S(2)}) collective-permute-start(bf16[48,1536]{1,0:T(8,128)(2,1)S(1)} %hidden.10.refs_0_.hidden_ref), channel_id=1, source_target_pairs={{0,1},{1,0},{2,3},{3,2},{4,5},{5,4},{6,7},{7,6},{8,9},{9,8},{10,11... | collective-permute-start | bytes 442376 | tf_op jit(solution)/shard_map/ppermute | solution.py:289
  73.2 2.2 %gate_up.19.refs_1_.kept_ref = f32[32,3072]{1,0:T(8,128)S(1)} custom-call(bf16[32,2176]{1,0:T(8,128)(2,1)S(1)} %slice.80.rows_ref, bf16[2,2048,768]{2,1,0:T(8,128)(2,1)S(1)} %get-tuple-element.25.gate_held, bf16[2,2048,768]{2,1,0:T(8,128)(2,1)S(1)} %get-tuple-element.26.up_held, bf16[48,1536]{1,0:T(8,128)(2,1)S(1)} %hidden.10.refs_0_.hidden_ref), custom_call_target="tpu_custom_call" | custom-call | flops 3221225472 | tf_op jit(solution)/shard_map/gate_up/pallas_call | solution.py:187
  78.2 3.2 %collective-permute-start.20 = (bf16[42,2048]{1,0:T(8,128)(2,1)S(1)}, bf16[42,2048]{1,0:T(8,128)(2,1)S(1)}, u32[]{:S(2)}, u32[]{:S(2)}) collective-permute-start(bf16[42,2048]{1,0:T(8,128)(2,1)S(1)} %fusion.refs_1_), channel_id=1, source_target_pairs={{0,8},{2,10},{4,12},{6,14},{8,0},{10,2},{12,4},{14,6},{1,9},{3,11}... | collective-permute-start | bytes 516104 | tf_op jit(solution)/shard_map/ppermute | solution.py:292
  88.2 4.9 %collective-permute-done.23 = bf16[42,2048]{1,0:T(8,128)(2,1)S(1)} collective-permute-done((bf16[42,2048]{1,0:T(8,128)(2,1)S(1)}, bf16[42,2048]{1,0:T(8,128)(2,1)S(1)}, u32[]{:S(2)}, u32[]{:S(2)}) %collective-permute-start.23) | collective-permute-done | bytes 172064 | tf_op jit(solution)/shard_map/ppermute | solution.py:292
  (86 shorter events, 28.8 us)
Async XLA Ops:
  1.1 12.7 %collective-permute-start = (bf16[42,2176]{1,0:T(8,128)(2,1)S(1)}, bf16[42,2176]{1,0:T(8,128)(2,1)S(1)}, u32[]{:S(2)}, u32[]{:S(2)}) collective-permute-start(bf16[42,2176]{1,0:T(8,128)(2,1)S(1)} %prepare.1), channel_id=1, source_target_pairs={{0,4},{2,6},{4,0},{6,2},{8,12},{10,14},{12,8},{14,10},{1,5},{3,7},... | collective-permute-start | bytes 548360 | tf_op jit(solution)/shard_map/ppermute | solution.py:292
  4.2 27.5 %collective-permute-start.8 = (bf16[42,2176]{1,0:T(8,128)(2,1)S(1)}, bf16[42,2176]{1,0:T(8,128)(2,1)S(1)}, u32[]{:S(2)}, u32[]{:S(2)}) collective-permute-start(bf16[42,2176]{1,0:T(8,128)(2,1)S(1)} %prepare.1), channel_id=1, source_target_pairs={{0,8},{2,10},{4,12},{6,14},{8,0},{10,2},{12,4},{14,6},{1,9},{3,11}... | collective-permute-start | bytes 548360 | tf_op jit(solution)/shard_map/ppermute | solution.py:292
  6.8 17.0 %collective-permute-start.3 = (bf16[42,2176]{1,0:T(8,128)(2,1)S(1)}, bf16[42,2176]{1,0:T(8,128)(2,1)S(1)}, u32[]{:S(2)}, u32[]{:S(2)}) collective-permute-start(bf16[42,2176]{1,0:T(8,128)(2,1)S(1)} %prepare.1), channel_id=1, source_target_pairs={{0,12},{2,14},{4,8},{6,10},{8,4},{10,6},{12,0},{14,2},{1,13},{3,15... | collective-permute-start | bytes 548360 | tf_op jit(solution)/shard_map/ppermute | solution.py:292
  12.1 10.4 %collective-permute-start.1 = (bf16[32,3072]{1,0:T(8,128)(2,1)S(1)}, bf16[32,3072]{1,0:T(8,128)(2,1)S(1)}, u32[]{:S(2)}, u32[]{:S(2)}) collective-permute-start(bf16[32,3072]{1,0:T(8,128)(2,1)S(1)} %get-tuple-element.22.refs_0_), channel_id=1, source_target_pairs={{0,1},{1,0},{2,3},{3,2},{4,5},{5,4},{6,7},{7,6},{8,9},{9,8},{10,11... | collective-permute-start | bytes 589832 | tf_op jit(solution)/shard_map/ppermute | solution.py:289
  16.2 10.3 %collective-permute-start.5 = (bf16[48,3072]{1,0:T(8,128)(2,1)S(1)}, bf16[48,3072]{1,0:T(8,128)(2,1)S(1)}, u32[]{:S(2)}, u32[]{:S(2)}) collective-permute-start(bf16[48,3072]{1,0:T(8,128)(2,1)S(1)} %gate_up.10.refs_0_), channel_id=1, source_target_pairs={{0,1},{1,0},{2,3},{3,2},{4,5},{5,4},{6,7},{7,6},{8,9},{9,8},{10,11... | collective-permute-start | bytes 884744 | tf_op jit(solution)/shard_map/ppermute | solution.py:289
  22.4 3.9 %collective-permute-start.10 = (bf16[42,2176]{1,0:T(8,128)(2,1)S(1)}, bf16[42,2176]{1,0:T(8,128)(2,1)S(1)}, u32[]{:S(2)}, u32[]{:S(2)}) collective-permute-start(bf16[42,2176]{1,0:T(8,128)(2,1)S(1)} %prepare.1), channel_id=1, source_target_pairs={{0,2},{2,0},{4,6},{6,4},{8,10},{10,8},{12,14},{14,12},{1,3},{3,1},... | collective-permute-start | bytes 548360 | tf_op jit(solution)/shard_map/ppermute | solution.py:292
  22.6 27.9 %collective-permute-start.2 = (bf16[32,1536]{1,0:T(8,128)(2,1)S(1)}, bf16[32,1536]{1,0:T(8,128)(2,1)S(1)}, u32[]{:S(2)}, u32[]{:S(2)}) collective-permute-start(bf16[32,1536]{1,0:T(8,128)(2,1)S(1)} %hidden.6.refs_0_.hidden_ref), channel_id=1, source_target_pairs={{0,1},{1,0},{2,3},{3,2},{4,5},{5,4},{6,7},{7,6},{8,9},{9,8},{10,11... | collective-permute-start | bytes 294920 | tf_op jit(solution)/shard_map/ppermute | solution.py:289
  23.8 2.6 %collective-permute-start.4 = (bf16[42,2176]{1,0:T(8,128)(2,1)S(1)}, bf16[42,2176]{1,0:T(8,128)(2,1)S(1)}, u32[]{:S(2)}, u32[]{:S(2)}) collective-permute-start(bf16[42,2176]{1,0:T(8,128)(2,1)S(1)} %collective-permute-done.3), channel_id=1, source_target_pairs={{0,2},{2,0},{4,6},{6,4},{8,10},{10,8},{12,14},{14,12},{1,3},{3,1},... | collective-permute-start | bytes 548360 | tf_op jit(solution)/shard_map/ppermute | solution.py:292
  26.6 25.0 %collective-permute-start.11 = (bf16[48,1536]{1,0:T(8,128)(2,1)S(1)}, bf16[48,1536]{1,0:T(8,128)(2,1)S(1)}, u32[]{:S(2)}, u32[]{:S(2)}) collective-permute-start(bf16[48,1536]{1,0:T(8,128)(2,1)S(1)} %hidden.7.refs_2_.hidden_ref), channel_id=1, source_target_pairs={{0,1},{1,0},{2,3},{3,2},{4,5},{5,4},{6,7},{7,6},{8,9},{9,8},{10,11... | collective-permute-start | bytes 442376 | tf_op jit(solution)/shard_map/ppermute | solution.py:289
  30.5 15.2 %collective-permute-start.7 = (bf16[88,3072]{1,0:T(8,128)(2,1)S(1)}, bf16[88,3072]{1,0:T(8,128)(2,1)S(1)}, u32[]{:S(2)}, u32[]{:S(2)}) collective-permute-start(bf16[88,3072]{1,0:T(8,128)(2,1)S(1)} %get-tuple-element.27.refs_2_), channel_id=1, source_target_pairs={{0,1},{1,0},{2,3},{3,2},{4,5},{5,4},{6,7},{7,6},{8,9},{9,8},{10,11... | collective-permute-start | bytes 1622024 | tf_op jit(solution)/shard_map/ppermute | solution.py:289
  31.7 6.2 %collective-permute-start.9 = (bf16[42,2176]{1,0:T(8,128)(2,1)S(1)}, bf16[42,2176]{1,0:T(8,128)(2,1)S(1)}, u32[]{:S(2)}, u32[]{:S(2)}) collective-permute-start(bf16[42,2176]{1,0:T(8,128)(2,1)S(1)} %collective-permute-done.8), channel_id=1, source_target_pairs={{0,2},{2,0},{4,6},{6,4},{8,10},{10,8},{12,14},{14,12},{1,3},{3,1},... | collective-permute-start | bytes 548360 | tf_op jit(solution)/shard_map/ppermute | solution.py:292
  34.6 12.5 %collective-permute-start.6 = (bf16[42,2176]{1,0:T(8,128)(2,1)S(1)}, bf16[42,2176]{1,0:T(8,128)(2,1)S(1)}, u32[]{:S(2)}, u32[]{:S(2)}) collective-permute-start(bf16[42,2176]{1,0:T(8,128)(2,1)S(1)} %prepare.1), channel_id=1, source_target_pairs={{0,6},{2,4},{4,2},{6,0},{8,14},{10,12},{12,10},{14,8},{1,7},{3,5},... | collective-permute-start | bytes 548360 | tf_op jit(solution)/shard_map/ppermute | solution.py:292
  40.2 18.4 %collective-permute-start.13 = (bf16[88,3072]{1,0:T(8,128)(2,1)S(1)}, bf16[88,3072]{1,0:T(8,128)(2,1)S(1)}, u32[]{:S(2)}, u32[]{:S(2)}) collective-permute-start(bf16[88,3072]{1,0:T(8,128)(2,1)S(1)} %gate_up.14.refs_0_), channel_id=1, source_target_pairs={{0,1},{1,0},{2,3},{3,2},{4,5},{5,4},{6,7},{7,6},{8,9},{9,8},{10,11... | collective-permute-start | bytes 1622024 | tf_op jit(solution)/shard_map/ppermute | solution.py:289
  45.9 17.4 %collective-permute-start.12 = (bf16[88,1536]{1,0:T(8,128)(2,1)S(1)}, bf16[88,1536]{1,0:T(8,128)(2,1)S(1)}, u32[]{:S(2)}, u32[]{:S(2)}) collective-permute-start(bf16[88,1536]{1,0:T(8,128)(2,1)S(1)} %hidden.8.refs_0_.hidden_ref), channel_id=1, source_target_pairs={{0,1},{1,0},{2,3},{3,2},{4,5},{5,4},{6,7},{7,6},{8,9},{9,8},{10,11... | collective-permute-start | bytes 811016 | tf_op jit(solution)/shard_map/ppermute | solution.py:289
  49.5 21.9 %collective-permute-start.18 = (bf16[48,3072]{1,0:T(8,128)(2,1)S(1)}, bf16[48,3072]{1,0:T(8,128)(2,1)S(1)}, u32[]{:S(2)}, u32[]{:S(2)}) collective-permute-start(bf16[48,3072]{1,0:T(8,128)(2,1)S(1)} %gate_up.15.refs_1_), channel_id=1, source_target_pairs={{0,1},{1,0},{2,3},{3,2},{4,5},{5,4},{6,7},{7,6},{8,9},{9,8},{10,11... | collective-permute-start | bytes 884744 | tf_op jit(solution)/shard_map/ppermute | solution.py:289
  52.9 35.3 %collective-permute-start.14 = (bf16[42,2048]{1,0:T(8,128)(2,1)S(1)}, bf16[42,2048]{1,0:T(8,128)(2,1)S(1)}, u32[]{:S(2)}, u32[]{:S(2)}) collective-permute-start(bf16[42,2048]{1,0:T(8,128)(2,1)S(1)} %slice.99), channel_id=1, source_target_pairs={{0,4},{2,6},{4,0},{6,2},{8,12},{10,14},{12,8},{14,10},{1,5},{3,7},... | collective-permute-start | bytes 516104 | tf_op jit(solution)/shard_map/ppermute | solution.py:292
  58.9 16.5 %collective-permute-start.17 = (bf16[88,1536]{1,0:T(8,128)(2,1)S(1)}, bf16[88,1536]{1,0:T(8,128)(2,1)S(1)}, u32[]{:S(2)}, u32[]{:S(2)}) collective-permute-start(bf16[88,1536]{1,0:T(8,128)(2,1)S(1)} %hidden.9.refs_0_.hidden_ref), channel_id=1, source_target_pairs={{0,1},{1,0},{2,3},{3,2},{4,5},{5,4},{6,7},{7,6},{8,9},{9,8},{10,11... | collective-permute-start | bytes 811016 | tf_op jit(solution)/shard_map/ppermute | solution.py:289
  61.8 19.7 %collective-permute-start.22 = (bf16[32,3072]{1,0:T(8,128)(2,1)S(1)}, bf16[32,3072]{1,0:T(8,128)(2,1)S(1)}, u32[]{:S(2)}, u32[]{:S(2)}) collective-permute-start(bf16[32,3072]{1,0:T(8,128)(2,1)S(1)} %gate_up.17.refs_1_), channel_id=1, source_target_pairs={{0,1},{1,0},{2,3},{3,2},{4,5},{5,4},{6,7},{7,6},{8,9},{9,8},{10,11... | collective-permute-start | bytes 589832 | tf_op jit(solution)/shard_map/ppermute | solution.py:289
  68.4 19.8 %collective-permute-start.16 = (bf16[42,2048]{1,0:T(8,128)(2,1)S(1)}, bf16[42,2048]{1,0:T(8,128)(2,1)S(1)}, u32[]{:S(2)}, u32[]{:S(2)}) collective-permute-start(bf16[42,2048]{1,0:T(8,128)(2,1)S(1)} %fusion.1.refs_1_), channel_id=1, source_target_pairs={{0,12},{2,14},{4,8},{6,10},{8,4},{10,6},{12,0},{14,2},{1,13},{3,15... | collective-permute-start | bytes 516104 | tf_op jit(solution)/shard_map/ppermute | solution.py:292
  71.6 10.5 %collective-permute-start.21 = (bf16[48,1536]{1,0:T(8,128)(2,1)S(1)}, bf16[48,1536]{1,0:T(8,128)(2,1)S(1)}, u32[]{:S(2)}, u32[]{:S(2)}) collective-permute-start(bf16[48,1536]{1,0:T(8,128)(2,1)S(1)} %hidden.10.refs_0_.hidden_ref), channel_id=1, source_target_pairs={{0,1},{1,0},{2,3},{3,2},{4,5},{5,4},{6,7},{7,6},{8,9},{9,8},{10,11... | collective-permute-start | bytes 442376 | tf_op jit(solution)/shard_map/ppermute | solution.py:289
  78.2 14.9 %collective-permute-start.20 = (bf16[42,2048]{1,0:T(8,128)(2,1)S(1)}, bf16[42,2048]{1,0:T(8,128)(2,1)S(1)}, u32[]{:S(2)}, u32[]{:S(2)}) collective-permute-start(bf16[42,2048]{1,0:T(8,128)(2,1)S(1)} %fusion.refs_1_), channel_id=1, source_target_pairs={{0,8},{2,10},{4,12},{6,14},{8,0},{10,2},{12,4},{14,6},{1,9},{3,11}... | collective-permute-start | bytes 516104 | tf_op jit(solution)/shard_map/ppermute | solution.py:292
  81.5 4.8 %collective-permute-start.24 = (bf16[32,1536]{1,0:T(8,128)(2,1)S(1)}, bf16[32,1536]{1,0:T(8,128)(2,1)S(1)}, u32[]{:S(2)}, u32[]{:S(2)}) collective-permute-start(bf16[32,1536]{1,0:T(8,128)(2,1)S(1)} %hidden.11.refs_1_.hidden_ref), channel_id=1, source_target_pairs={{0,1},{1,0},{2,3},{3,2},{4,5},{5,4},{6,7},{7,6},{8,9},{9,8},{10,11... | collective-permute-start | bytes 294920 | tf_op jit(solution)/shard_map/ppermute | solution.py:289
  83.4 9.7 %collective-permute-start.23 = (bf16[42,2048]{1,0:T(8,128)(2,1)S(1)}, bf16[42,2048]{1,0:T(8,128)(2,1)S(1)}, u32[]{:S(2)}, u32[]{:S(2)}) collective-permute-start(bf16[42,2048]{1,0:T(8,128)(2,1)S(1)} %bitcast.5), channel_id=1, source_target_pairs={{0,6},{2,4},{4,2},{6,0},{8,14},{10,12},{12,10},{14,8},{1,7},{3,5},... | collective-permute-start | bytes 516104 | tf_op jit(solution)/shard_map/ppermute | solution.py:292
  87.6 5.5 %collective-permute-start.25 = (bf16[42,2048]{1,0:T(8,128)(2,1)S(1)}, bf16[42,2048]{1,0:T(8,128)(2,1)S(1)}, u32[]{:S(2)}, u32[]{:S(2)}) collective-permute-start(bf16[42,2048]{1,0:T(8,128)(2,1)S(1)} %pad_maximum_fusion.4), channel_id=1, source_target_pairs={{0,2},{2,0},{4,6},{6,4},{8,10},{10,8},{12,14},{14,12},{1,3},{3,1},... | collective-permute-start | bytes 516104 | tf_op jit(solution)/shard_map/ppermute | solution.py:292
  (4 other events, 11.4 us)

commit v5 on v4

--- a/solution.py
+++ b/solution.py
@@ -157,7 +157,7 @@
 
 def gate_up_kernel(load, rows_ref, gate_held, up_held, *refs):
     experts, _, half = gate_held.shape
-    tile = half // 3
+    tile = half // 2
     copies = []
     if load:
         out_ref, held, sem = refs[-3:]
@@ -294,7 +294,7 @@
     def later(value, than):
         return lax.optimization_barrier((value, than))[0]
 
-    near, far = CORES, [CORES * step for step in range(chips - 1, 1, -1)]
+    near, far = CORES, [CORES * step for step in range(2, chips)]
     fills = [-count % 8] + [-(CORES * count) % 8] * len(far) + [-count % 8]
     first = (count - sum(fills[:2])) // 8 * 8
     if CORES * count - first - sum(fills) < 8:

time: 94.1 us -> 93.7 us (level)
  waiting for transfers between devices: 8.48 us -> 19.4 us
  starting transfers between devices: 32.7 us -> 22.8 us
  Pallas kernels: 50.8 us -> 49.2 us
    ppermute x12, waiting for transfers between devices: 3.34 us -> 13 us  [swap_tensor(): return lax.ppermute(value, 'tensor', [(0, 1), (1, 0)])]
    ppermute x14, starting transfers between devices: 18.6 us -> 10.1 us  [swap_expert(): return lax.ppermute(value, 'expert', [(i, i ^ mask) for i in range(groups)])]
    ppermute x12, starting transfers between devices: 14.1 us -> 12.7 us  [swap_tensor(): return lax.ppermute(value, 'tensor', [(0, 1), (1, 0)])]
    ppermute x14, waiting for transfers between devices: 5.14 us -> 6.39 us  [swap_expert(): return lax.ppermute(value, 'expert', [(i, i ^ mask) for i in range(groups)])]
    pallas_call x10, Pallas kernels: 23.9 us -> 22.7 us  [gate_up(): pl.pallas_call(functools.partial(gate_up_kernel, load), in_specs=specs +...]
  transfers between devices with their start and end apart: 26 -> 26, of which waited for: 4 -> 10; matrix products, arithmetic and copies ran while one was open for 1% -> 1% of each run, Pallas kernels for 53% -> 51%
where the time goes in v5:
time: 93.7 us; the launch traced here: 93.5 us
  Pallas kernels  49.2 us (53%)
  starting transfers between devices  22.8 us (24%)
  waiting for transfers between devices  19.4 us (21%)
  other arithmetic  1.29 us (1%)
    pallas_call x10, Pallas kernels, gate_up(): pl.pallas_call(functools.partial(gate_up_kernel, load), in_specs=specs +...  22.7 us
    pallas_call x12, Pallas kernels, down(): pl.pallas_call(functools.partial(down_kernel, len(extra)), in_specs=[VMEM...  14 us
    ppermute x12, waiting for transfers between devices, swap_tensor(): return lax.ppermute(value, 'tensor', [(0, 1), (1, 0)])  13 us
    ppermute x12, starting transfers between devices, swap_tensor(): return lax.ppermute(value, 'tensor', [(0, 1), (1, 0)])  12.7 us
    pallas_call x2, Pallas kernels, gate_up_load(): pl.pallas_call(functools.partial(gate_up_load_kernel, compute), in_specs=...  10.4 us
    ppermute x14, starting transfers between devices, swap_expert(): return lax.ppermute(value, 'expert', [(i, i ^ mask) for i in range(groups)])  10.1 us
    ppermute x14, waiting for transfers between devices, swap_expert(): return lax.ppermute(value, 'expert', [(i, i ^ mask) for i in range(groups)])  6.39 us
  transfers between devices with their start and end apart: 26, of which 10 were waited for; matrix products, arithmetic and copies ran while one was open for 1% of the time, Pallas kernels for 51%

profile of v5, /device:TPU:0, one launch (start us, length us, event | category | flops | bytes accessed | tf_op | source)
XLA Modules:
  0.0 93.5 jit_solution(16105766017951639040)
XLA Ops:
  1.1 3.1 %collective-permute-start = (bf16[42,2176]{1,0:T(8,128)(2,1)S(1)}, bf16[42,2176]{1,0:T(8,128)(2,1)S(1)}, u32[]{:S(2)}, u32[]{:S(2)}) collective-permute-start(bf16[42,2176]{1,0:T(8,128)(2,1)S(1)} %prepare.1), channel_id=1, source_target_pairs={{0,4},{2,6},{4,0},{6,2},{8,12},{10,14},{12,8},{14,10},{1,5},{3,7},... | collective-permute-start | bytes 548360 | tf_op jit(solution)/shard_map/ppermute | solution.py:292
  4.2 2.5 %collective-permute-start.8 = (bf16[42,2176]{1,0:T(8,128)(2,1)S(1)}, bf16[42,2176]{1,0:T(8,128)(2,1)S(1)}, u32[]{:S(2)}, u32[]{:S(2)}) collective-permute-start(bf16[42,2176]{1,0:T(8,128)(2,1)S(1)} %prepare.1), channel_id=1, source_target_pairs={{0,12},{2,14},{4,8},{6,10},{8,4},{10,6},{12,0},{14,2},{1,13},{3,15... | collective-permute-start | bytes 548360 | tf_op jit(solution)/shard_map/ppermute | solution.py:292
  6.8 5.2 %gate_up_load.2 = (bf16[32,3072]{1,0:T(8,128)(2,1)S(1)}, bf16[2,2048,768]{2,1,0:T(8,128)(2,1)S(1)}, bf16[2,2048,768]{2,1,0:T(8,128)(2,1)S(1)}) custom-call(s32[1]{0:T(128)S(6)} %sub.3.side_ref.refs_0_, bf16[32,2176]{1,0:T(8,128)(2,1)S(1)} %slice.74.rows_ref, bf16[2,2048,1536]{2,1,0:T(8,128)(2,1)} %gate_ref.3, bf16[2,2048,1536]{2,1,0:T(8,128)(2,1)} %up_ref.3, ...), custom_call_target="tpu_custom_call" | custom-call | flops 402653184 | bytes 12582912 | tf_op jit(solution)/shard_map/gate_up_load/pallas_call | solution.py:133
  12.1 1.6 %collective-permute-start.1 = (bf16[32,3072]{1,0:T(8,128)(2,1)S(1)}, bf16[32,3072]{1,0:T(8,128)(2,1)S(1)}, u32[]{:S(2)}, u32[]{:S(2)}) collective-permute-start(bf16[32,3072]{1,0:T(8,128)(2,1)S(1)} %get-tuple-element.22.refs_0_), channel_id=1, source_target_pairs={{0,1},{1,0},{2,3},{3,2},{4,5},{5,4},{6,7},{7,6},{8,9},{9,8},{10,11... | collective-permute-start | bytes 589832 | tf_op jit(solution)/shard_map/ppermute | solution.py:289
  13.7 2.0 %gate_up.10.refs_0_ = bf16[48,3072]{1,0:T(8,128)(2,1)S(1)} custom-call(bf16[48,2176]{1,0:T(8,128)(2,1)S(1)} %pad_maximum_fusion.2.rows_ref, bf16[2,2048,768]{2,1,0:T(8,128)(2,1)S(1)} %get-tuple-element.20.gate_held, bf16[2,2048,768]{2,1,0:T(8,128)(2,1)S(1)} %get-tuple-element.21.up_held, bf16[32,3072]{1,0:T(8,128)(2,1)S(1)} %get-tuple-element.22.refs_0_), custom_call_target="tpu_custom_call" | custom-call | flops 3221225472 | tf_op jit(solution)/shard_map/gate_up/pallas_call | solution.py:187
  16.3 5.2 %gate_up_load.3 = (f32[32,3072]{1,0:T(8,128)S(1)}, bf16[2,2048,768]{2,1,0:T(8,128)(2,1)S(1)}, bf16[2,2048,768]{2,1,0:T(8,128)(2,1)S(1)}) custom-call(s32[1]{0:T(128)} %bitcast.3.refs_1_.side_ref.refs_0_, bf16[32,2176]{1,0:T(8,128)(2,1)S(1)} %slice.74.rows_ref, bf16[2,2048,1536]{2,1,0:T(8,128)(2,1)} %gate_ref.3, bf16[2,2048,1536]{2,1,0:T(8,128)(2,1)} %up_ref.3, ...), custom_call_target="tpu_custom_call" | custom-call | flops 402653184 | bytes 12582912 | tf_op jit(solution)/shard_map/gate_up_load/pallas_call | solution.py:133
  21.7 1.6 %collective-permute-start.2 = (bf16[32,1536]{1,0:T(8,128)(2,1)S(1)}, bf16[32,1536]{1,0:T(8,128)(2,1)S(1)}, u32[]{:S(2)}, u32[]{:S(2)}) collective-permute-start(bf16[32,1536]{1,0:T(8,128)(2,1)S(1)} %hidden.6.refs_0_.hidden_ref), channel_id=1, source_target_pairs={{0,1},{1,0},{2,3},{3,2},{4,5},{5,4},{6,7},{7,6},{8,9},{9,8},{10,11... | collective-permute-start | bytes 294920 | tf_op jit(solution)/shard_map/ppermute | solution.py:289
  23.3 1.9 %collective-permute-done.3 = bf16[42,2176]{1,0:T(8,128)(2,1)S(1)} collective-permute-done((bf16[42,2176]{1,0:T(8,128)(2,1)S(1)}, bf16[42,2176]{1,0:T(8,128)(2,1)S(1)}, u32[]{:S(2)}, u32[]{:S(2)}) %collective-permute-start.3) | collective-permute-done | bytes 182816 | tf_op jit(solution)/shard_map/ppermute | solution.py:292
  25.1 2.0 %gate_up.11.kept_ref.refs_0_ = f32[48,3072]{1,0:T(8,128)S(1)} custom-call(bf16[48,2176]{1,0:T(8,128)(2,1)S(1)} %pad_maximum_fusion.2.rows_ref, bf16[2,2048,768]{2,1,0:T(8,128)(2,1)S(1)} %get-tuple-element.25.gate_held, bf16[2,2048,768]{2,1,0:T(8,128)(2,1)S(1)} %get-tuple-element.26.up_held, bf16[32,1536]{1,0:T(8,128)(2,1)S(1)} %hidden.6.refs_0_.hidden_ref), custom_call_target="tpu_custom_call" | custom-call | flops 3221225472 | tf_op jit(solution)/shard_map/gate_up/pallas_call | solution.py:187
  27.5 1.6 %collective-permute-start.11 = (bf16[48,1536]{1,0:T(8,128)(2,1)S(1)}, bf16[48,1536]{1,0:T(8,128)(2,1)S(1)}, u32[]{:S(2)}, u32[]{:S(2)}) collective-permute-start(bf16[48,1536]{1,0:T(8,128)(2,1)S(1)} %hidden.7.refs_2_.hidden_ref), channel_id=1, source_target_pairs={{0,1},{1,0},{2,3},{3,2},{4,5},{5,4},{6,7},{7,6},{8,9},{9,8},{10,11... | collective-permute-start | bytes 442376 | tf_op jit(solution)/shard_map/ppermute | solution.py:289
  29.0 2.9 %gate_up.12 = (bf16[88,3072]{1,0:T(8,128)(2,1)S(1)}, bf16[2,768,2048]{2,1,0:T(8,128)(2,1)S(1)}) custom-call(bf16[88,2176]{1,0:T(8,128)(2,1)S(1)} %pad_maximum_fusion.rows_ref, bf16[2,2048,768]{2,1,0:T(8,128)(2,1)S(1)} %get-tuple-element.20.gate_held, bf16[2,2048,768]{2,1,0:T(8,128)(2,1)S(1)} %get-tuple-element.21.up_held, s32[1]{0:T(128)} %bitcast.3.refs_1_.side_ref.refs_0_, ...), custom_call_target="tpu_custom_call" | custom-call | flops 3221225472 | tf_op jit(solution)/shard_map/gate_up/pallas_call | solution.py:187
  32.5 2.9 %gate_up.13 = (f32[88,3072]{1,0:T(8,128)S(1)}, bf16[2,768,2048]{2,1,0:T(8,128)(2,1)S(1)}) custom-call(bf16[88,2176]{1,0:T(8,128)(2,1)S(1)} %pad_maximum_fusion.rows_ref, bf16[2,2048,768]{2,1,0:T(8,128)(2,1)S(1)} %get-tuple-element.25.gate_held, bf16[2,2048,768]{2,1,0:T(8,128)(2,1)S(1)} %get-tuple-element.26.up_held, s32[1]{0:T(128)S(6)} %sub.3.side_ref.refs_0_, ...), custom_call_target="tpu_custom_call" | custom-call | flops 3221225472 | tf_op jit(solution)/shard_map/gate_up/pallas_call | solution.py:187
  37.0 2.3 %gate_up.14.refs_0_ = bf16[88,3072]{1,0:T(8,128)(2,1)S(1)} custom-call(bf16[88,2176]{1,0:T(8,128)(2,1)S(1)} %pad_maximum_fusion.1.rows_ref, bf16[2,2048,768]{2,1,0:T(8,128)(2,1)S(1)} %get-tuple-element.20.gate_held, bf16[2,2048,768]{2,1,0:T(8,128)(2,1)S(1)} %get-tuple-element.21.up_held, f32[32,2048]{1,0:T(8,128)S(1)} %down.12.refs_0_), custom_call_target="tpu_custom_call" | custom-call | flops 3221225472 | tf_op jit(solution)/shard_map/gate_up/pallas_call | solution.py:187
  41.9 5.2 %collective-permute-done.7.received_ref = bf16[88,3072]{1,0:T(8,128)(2,1)S(1)} collective-permute-done((bf16[88,3072]{1,0:T(8,128)(2,1)S(1)}, bf16[88,3072]{1,0:T(8,128)(2,1)S(1)}, u32[]{:S(2)}, u32[]{:S(2)}) %collective-permute-start.7) | collective-permute-done | bytes 540704 | tf_op jit(solution)/shard_map/ppermute | solution.py:289
  48.0 2.1 %gate_up.15.refs_1_ = bf16[48,3072]{1,0:T(8,128)(2,1)S(1)} custom-call(bf16[48,2176]{1,0:T(8,128)(2,1)S(1)} %pad_maximum_fusion.3.rows_ref, bf16[2,2048,768]{2,1,0:T(8,128)(2,1)S(1)} %get-tuple-element.20.gate_held, bf16[2,2048,768]{2,1,0:T(8,128)(2,1)S(1)} %get-tuple-element.21.up_held, bf16[88,1536]{1,0:T(8,128)(2,1)S(1)} %hidden.8.refs_0_.hidden_ref), custom_call_target="tpu_custom_call" | custom-call | flops 3221225472 | tf_op jit(solution)/shard_map/gate_up/pallas_call | solution.py:187
  50.1 1.6 %collective-permute-start.18 = (bf16[48,3072]{1,0:T(8,128)(2,1)S(1)}, bf16[48,3072]{1,0:T(8,128)(2,1)S(1)}, u32[]{:S(2)}, u32[]{:S(2)}) collective-permute-start(bf16[48,3072]{1,0:T(8,128)(2,1)S(1)} %gate_up.15.refs_1_), channel_id=1, source_target_pairs={{0,1},{1,0},{2,3},{3,2},{4,5},{5,4},{6,7},{7,6},{8,9},{9,8},{10,11... | collective-permute-start | bytes 884744 | tf_op jit(solution)/shard_map/ppermute | solution.py:289
  55.3 2.3 %gate_up.16.kept_ref.refs_0_ = f32[88,3072]{1,0:T(8,128)S(1)} custom-call(bf16[88,2176]{1,0:T(8,128)(2,1)S(1)} %pad_maximum_fusion.1.rows_ref, bf16[2,2048,768]{2,1,0:T(8,128)(2,1)S(1)} %get-tuple-element.25.gate_held, bf16[2,2048,768]{2,1,0:T(8,128)(2,1)S(1)} %get-tuple-element.26.up_held, f32[88,2048]{1,0:T(8,128)S(1)} %down.16.refs_0_), custom_call_target="tpu_custom_call" | custom-call | flops 3221225472 | tf_op jit(solution)/shard_map/gate_up/pallas_call | solution.py:187
  59.5 2.1 %gate_up.17.refs_1_ = bf16[32,3072]{1,0:T(8,128)(2,1)S(1)} custom-call(bf16[32,2176]{1,0:T(8,128)(2,1)S(1)} %slice.80.rows_ref, bf16[2,2048,768]{2,1,0:T(8,128)(2,1)S(1)} %get-tuple-element.20.gate_held, bf16[2,2048,768]{2,1,0:T(8,128)(2,1)S(1)} %get-tuple-element.21.up_held, bf16[88,1536]{1,0:T(8,128)(2,1)S(1)} %hidden.9.refs_0_.hidden_ref), custom_call_target="tpu_custom_call" | custom-call | flops 3221225472 | tf_op jit(solution)/shard_map/gate_up/pallas_call | solution.py:187
  61.7 1.6 %collective-permute-start.22 = (bf16[32,3072]{1,0:T(8,128)(2,1)S(1)}, bf16[32,3072]{1,0:T(8,128)(2,1)S(1)}, u32[]{:S(2)}, u32[]{:S(2)}) collective-permute-start(bf16[32,3072]{1,0:T(8,128)(2,1)S(1)} %gate_up.17.refs_1_), channel_id=1, source_target_pairs={{0,1},{1,0},{2,3},{3,2},{4,5},{5,4},{6,7},{7,6},{8,9},{9,8},{10,11... | collective-permute-start | bytes 589832 | tf_op jit(solution)/shard_map/ppermute | solution.py:289
  66.9 2.1 %gate_up.18.kept_ref.refs_0_ = f32[48,3072]{1,0:T(8,128)S(1)} custom-call(bf16[48,2176]{1,0:T(8,128)(2,1)S(1)} %pad_maximum_fusion.3.rows_ref, bf16[2,2048,768]{2,1,0:T(8,128)(2,1)S(1)} %get-tuple-element.25.gate_held, bf16[2,2048,768]{2,1,0:T(8,128)(2,1)S(1)} %get-tuple-element.26.up_held, f32[88,2048]{1,0:T(8,128)S(1)} %down.18.refs_0_), custom_call_target="tpu_custom_call" | custom-call | flops 3221225472 | tf_op jit(solution)/shard_map/gate_up/pallas_call | solution.py:187
  71.5 1.9 %gate_up.19.refs_1_.kept_ref = f32[32,3072]{1,0:T(8,128)S(1)} custom-call(bf16[32,2176]{1,0:T(8,128)(2,1)S(1)} %slice.80.rows_ref, bf16[2,2048,768]{2,1,0:T(8,128)(2,1)S(1)} %get-tuple-element.25.gate_held, bf16[2,2048,768]{2,1,0:T(8,128)(2,1)S(1)} %get-tuple-element.26.up_held, bf16[48,1536]{1,0:T(8,128)(2,1)S(1)} %hidden.10.refs_0_.hidden_ref), custom_call_target="tpu_custom_call" | custom-call | flops 3221225472 | tf_op jit(solution)/shard_map/gate_up/pallas_call | solution.py:187
  73.5 3.1 %collective-permute-done.17.hidden_ref = bf16[88,1536]{1,0:T(8,128)(2,1)S(1)} collective-permute-done((bf16[88,1536]{1,0:T(8,128)(2,1)S(1)}, bf16[88,1536]{1,0:T(8,128)(2,1)S(1)}, u32[]{:S(2)}, u32[]{:S(2)}) %collective-permute-start.17) | collective-permute-done | bytes 270368 | tf_op jit(solution)/shard_map/ppermute | solution.py:289
  79.4 2.7 %collective-permute-start.20 = (bf16[42,2048]{1,0:T(8,128)(2,1)S(1)}, bf16[42,2048]{1,0:T(8,128)(2,1)S(1)}, u32[]{:S(2)}, u32[]{:S(2)}) collective-permute-start(bf16[42,2048]{1,0:T(8,128)(2,1)S(1)} %fusion.refs_1_), channel_id=1, source_target_pairs={{0,12},{2,14},{4,8},{6,10},{8,4},{10,6},{12,0},{14,2},{1,13},{3,15... | collective-permute-start | bytes 516104 | tf_op jit(solution)/shard_map/ppermute | solution.py:292
  88.4 4.3 %collective-permute-done.23 = bf16[42,2048]{1,0:T(8,128)(2,1)S(1)} collective-permute-done((bf16[42,2048]{1,0:T(8,128)(2,1)S(1)}, bf16[42,2048]{1,0:T(8,128)(2,1)S(1)}, u32[]{:S(2)}, u32[]{:S(2)}) %collective-permute-start.23) | collective-permute-done | bytes 172064 | tf_op jit(solution)/shard_map/ppermute | solution.py:292
  (86 shorter events, 29.4 us)
Async XLA Ops:
  1.1 12.5 %collective-permute-start = (bf16[42,2176]{1,0:T(8,128)(2,1)S(1)}, bf16[42,2176]{1,0:T(8,128)(2,1)S(1)}, u32[]{:S(2)}, u32[]{:S(2)}) collective-permute-start(bf16[42,2176]{1,0:T(8,128)(2,1)S(1)} %prepare.1), channel_id=1, source_target_pairs={{0,4},{2,6},{4,0},{6,2},{8,12},{10,14},{12,8},{14,10},{1,5},{3,7},... | collective-permute-start | bytes 548360 | tf_op jit(solution)/shard_map/ppermute | solution.py:292
  4.2 28.3 %collective-permute-start.8 = (bf16[42,2176]{1,0:T(8,128)(2,1)S(1)}, bf16[42,2176]{1,0:T(8,128)(2,1)S(1)}, u32[]{:S(2)}, u32[]{:S(2)}) collective-permute-start(bf16[42,2176]{1,0:T(8,128)(2,1)S(1)} %prepare.1), channel_id=1, source_target_pairs={{0,12},{2,14},{4,8},{6,10},{8,4},{10,6},{12,0},{14,2},{1,13},{3,15... | collective-permute-start | bytes 548360 | tf_op jit(solution)/shard_map/ppermute | solution.py:292
  6.7 18.4 %collective-permute-start.3 = (bf16[42,2176]{1,0:T(8,128)(2,1)S(1)}, bf16[42,2176]{1,0:T(8,128)(2,1)S(1)}, u32[]{:S(2)}, u32[]{:S(2)}) collective-permute-start(bf16[42,2176]{1,0:T(8,128)(2,1)S(1)} %prepare.1), channel_id=1, source_target_pairs={{0,8},{2,10},{4,12},{6,14},{8,0},{10,2},{12,4},{14,6},{1,9},{3,11}... | collective-permute-start | bytes 548360 | tf_op jit(solution)/shard_map/ppermute | solution.py:292
  12.1 9.5 %collective-permute-start.1 = (bf16[32,3072]{1,0:T(8,128)(2,1)S(1)}, bf16[32,3072]{1,0:T(8,128)(2,1)S(1)}, u32[]{:S(2)}, u32[]{:S(2)}) collective-permute-start(bf16[32,3072]{1,0:T(8,128)(2,1)S(1)} %get-tuple-element.22.refs_0_), channel_id=1, source_target_pairs={{0,1},{1,0},{2,3},{3,2},{4,5},{5,4},{6,7},{7,6},{8,9},{9,8},{10,11... | collective-permute-start | bytes 589832 | tf_op jit(solution)/shard_map/ppermute | solution.py:289
  15.7 11.6 %collective-permute-start.5 = (bf16[48,3072]{1,0:T(8,128)(2,1)S(1)}, bf16[48,3072]{1,0:T(8,128)(2,1)S(1)}, u32[]{:S(2)}, u32[]{:S(2)}) collective-permute-start(bf16[48,3072]{1,0:T(8,128)(2,1)S(1)} %gate_up.10.refs_0_), channel_id=1, source_target_pairs={{0,1},{1,0},{2,3},{3,2},{4,5},{5,4},{6,7},{7,6},{8,9},{9,8},{10,11... | collective-permute-start | bytes 884744 | tf_op jit(solution)/shard_map/ppermute | solution.py:289
  21.5 5.6 %collective-permute-start.10 = (bf16[42,2176]{1,0:T(8,128)(2,1)S(1)}, bf16[42,2176]{1,0:T(8,128)(2,1)S(1)}, u32[]{:S(2)}, u32[]{:S(2)}) collective-permute-start(bf16[42,2176]{1,0:T(8,128)(2,1)S(1)} %prepare.1), channel_id=1, source_target_pairs={{0,2},{2,0},{4,6},{6,4},{8,10},{10,8},{12,14},{14,12},{1,3},{3,1},... | collective-permute-start | bytes 548360 | tf_op jit(solution)/shard_map/ppermute | solution.py:292
  21.7 29.9 %collective-permute-start.2 = (bf16[32,1536]{1,0:T(8,128)(2,1)S(1)}, bf16[32,1536]{1,0:T(8,128)(2,1)S(1)}, u32[]{:S(2)}, u32[]{:S(2)}) collective-permute-start(bf16[32,1536]{1,0:T(8,128)(2,1)S(1)} %hidden.6.refs_0_.hidden_ref), channel_id=1, source_target_pairs={{0,1},{1,0},{2,3},{3,2},{4,5},{5,4},{6,7},{7,6},{8,9},{9,8},{10,11... | collective-permute-start | bytes 294920 | tf_op jit(solution)/shard_map/ppermute | solution.py:289
  27.5 25.4 %collective-permute-start.11 = (bf16[48,1536]{1,0:T(8,128)(2,1)S(1)}, bf16[48,1536]{1,0:T(8,128)(2,1)S(1)}, u32[]{:S(2)}, u32[]{:S(2)}) collective-permute-start(bf16[48,1536]{1,0:T(8,128)(2,1)S(1)} %hidden.7.refs_2_.hidden_ref), channel_id=1, source_target_pairs={{0,1},{1,0},{2,3},{3,2},{4,5},{5,4},{6,7},{7,6},{8,9},{9,8},{10,11... | collective-permute-start | bytes 442376 | tf_op jit(solution)/shard_map/ppermute | solution.py:289
  31.9 15.2 %collective-permute-start.7 = (bf16[88,3072]{1,0:T(8,128)(2,1)S(1)}, bf16[88,3072]{1,0:T(8,128)(2,1)S(1)}, u32[]{:S(2)}, u32[]{:S(2)}) collective-permute-start(bf16[88,3072]{1,0:T(8,128)(2,1)S(1)} %get-tuple-element.27.refs_2_), channel_id=1, source_target_pairs={{0,1},{1,0},{2,3},{3,2},{4,5},{5,4},{6,7},{7,6},{8,9},{9,8},{10,11... | collective-permute-start | bytes 1622024 | tf_op jit(solution)/shard_map/ppermute | solution.py:289
  32.5 4.4 %collective-permute-start.9 = (bf16[42,2176]{1,0:T(8,128)(2,1)S(1)}, bf16[42,2176]{1,0:T(8,128)(2,1)S(1)}, u32[]{:S(2)}, u32[]{:S(2)}) collective-permute-start(bf16[42,2176]{1,0:T(8,128)(2,1)S(1)} %collective-permute-done.8), channel_id=1, source_target_pairs={{0,2},{2,0},{4,6},{6,4},{8,10},{10,8},{12,14},{14,12},{1,3},{3,1},... | collective-permute-start | bytes 548360 | tf_op jit(solution)/shard_map/ppermute | solution.py:292
  35.4 12.5 %collective-permute-start.6 = (bf16[42,2176]{1,0:T(8,128)(2,1)S(1)}, bf16[42,2176]{1,0:T(8,128)(2,1)S(1)}, u32[]{:S(2)}, u32[]{:S(2)}) collective-permute-start(bf16[42,2176]{1,0:T(8,128)(2,1)S(1)} %prepare.1), channel_id=1, source_target_pairs={{0,6},{2,4},{4,2},{6,0},{8,14},{10,12},{12,10},{14,8},{1,7},{3,5},... | collective-permute-start | bytes 548360 | tf_op jit(solution)/shard_map/ppermute | solution.py:292
  39.4 19.3 %collective-permute-start.13 = (bf16[88,3072]{1,0:T(8,128)(2,1)S(1)}, bf16[88,3072]{1,0:T(8,128)(2,1)S(1)}, u32[]{:S(2)}, u32[]{:S(2)}) collective-permute-start(bf16[88,3072]{1,0:T(8,128)(2,1)S(1)} %gate_up.14.refs_0_), channel_id=1, source_target_pairs={{0,1},{1,0},{2,3},{3,2},{4,5},{5,4},{6,7},{7,6},{8,9},{9,8},{10,11... | collective-permute-start | bytes 1622024 | tf_op jit(solution)/shard_map/ppermute | solution.py:289
  47.4 17.1 %collective-permute-start.12 = (bf16[88,1536]{1,0:T(8,128)(2,1)S(1)}, bf16[88,1536]{1,0:T(8,128)(2,1)S(1)}, u32[]{:S(2)}, u32[]{:S(2)}) collective-permute-start(bf16[88,1536]{1,0:T(8,128)(2,1)S(1)} %hidden.8.refs_0_.hidden_ref), channel_id=1, source_target_pairs={{0,1},{1,0},{2,3},{3,2},{4,5},{5,4},{6,7},{7,6},{8,9},{9,8},{10,11... | collective-permute-start | bytes 811016 | tf_op jit(solution)/shard_map/ppermute | solution.py:289
  50.1 20.7 %collective-permute-start.18 = (bf16[48,3072]{1,0:T(8,128)(2,1)S(1)}, bf16[48,3072]{1,0:T(8,128)(2,1)S(1)}, u32[]{:S(2)}, u32[]{:S(2)}) collective-permute-start(bf16[48,3072]{1,0:T(8,128)(2,1)S(1)} %gate_up.15.refs_1_), channel_id=1, source_target_pairs={{0,1},{1,0},{2,3},{3,2},{4,5},{5,4},{6,7},{7,6},{8,9},{9,8},{10,11... | collective-permute-start | bytes 884744 | tf_op jit(solution)/shard_map/ppermute | solution.py:289
  54.1 34.3 %collective-permute-start.14 = (bf16[42,2048]{1,0:T(8,128)(2,1)S(1)}, bf16[42,2048]{1,0:T(8,128)(2,1)S(1)}, u32[]{:S(2)}, u32[]{:S(2)}) collective-permute-start(bf16[42,2048]{1,0:T(8,128)(2,1)S(1)} %slice.99), channel_id=1, source_target_pairs={{0,4},{2,6},{4,0},{6,2},{8,12},{10,14},{12,8},{14,10},{1,5},{3,7},... | collective-permute-start | bytes 516104 | tf_op jit(solution)/shard_map/ppermute | solution.py:292
  58.9 17.6 %collective-permute-start.17 = (bf16[88,1536]{1,0:T(8,128)(2,1)S(1)}, bf16[88,1536]{1,0:T(8,128)(2,1)S(1)}, u32[]{:S(2)}, u32[]{:S(2)}) collective-permute-start(bf16[88,1536]{1,0:T(8,128)(2,1)S(1)} %hidden.9.refs_0_.hidden_ref), channel_id=1, source_target_pairs={{0,1},{1,0},{2,3},{3,2},{4,5},{5,4},{6,7},{7,6},{8,9},{9,8},{10,11... | collective-permute-start | bytes 811016 | tf_op jit(solution)/shard_map/ppermute | solution.py:289
  61.7 20.4 %collective-permute-start.22 = (bf16[32,3072]{1,0:T(8,128)(2,1)S(1)}, bf16[32,3072]{1,0:T(8,128)(2,1)S(1)}, u32[]{:S(2)}, u32[]{:S(2)}) collective-permute-start(bf16[32,3072]{1,0:T(8,128)(2,1)S(1)} %gate_up.17.refs_1_), channel_id=1, source_target_pairs={{0,1},{1,0},{2,3},{3,2},{4,5},{5,4},{6,7},{7,6},{8,9},{9,8},{10,11... | collective-permute-start | bytes 589832 | tf_op jit(solution)/shard_map/ppermute | solution.py:289
  66.9 2.2 %collective-permute-start.15 = (bf16[42,2048]{1,0:T(8,128)(2,1)S(1)}, bf16[42,2048]{1,0:T(8,128)(2,1)S(1)}, u32[]{:S(2)}, u32[]{:S(2)}) collective-permute-start(bf16[42,2048]{1,0:T(8,128)(2,1)S(1)} %slice.98), channel_id=1, source_target_pairs={{0,2},{2,0},{4,6},{6,4},{8,10},{10,8},{12,14},{14,12},{1,3},{3,1},... | collective-permute-start | bytes 516104 | tf_op jit(solution)/shard_map/ppermute | solution.py:292
  69.1 19.3 %collective-permute-start.16 = (bf16[42,2048]{1,0:T(8,128)(2,1)S(1)}, bf16[42,2048]{1,0:T(8,128)(2,1)S(1)}, u32[]{:S(2)}, u32[]{:S(2)}) collective-permute-start(bf16[42,2048]{1,0:T(8,128)(2,1)S(1)} %fusion.1.refs_1_), channel_id=1, source_target_pairs={{0,8},{2,10},{4,12},{6,14},{8,0},{10,2},{12,4},{14,6},{1,9},{3,11}... | collective-permute-start | bytes 516104 | tf_op jit(solution)/shard_map/ppermute | solution.py:292
  70.9 12.3 %collective-permute-start.21 = (bf16[48,1536]{1,0:T(8,128)(2,1)S(1)}, bf16[48,1536]{1,0:T(8,128)(2,1)S(1)}, u32[]{:S(2)}, u32[]{:S(2)}) collective-permute-start(bf16[48,1536]{1,0:T(8,128)(2,1)S(1)} %hidden.10.refs_0_.hidden_ref), channel_id=1, source_target_pairs={{0,1},{1,0},{2,3},{3,2},{4,5},{5,4},{6,7},{7,6},{8,9},{9,8},{10,11... | collective-permute-start | bytes 442376 | tf_op jit(solution)/shard_map/ppermute | solution.py:289
  79.4 13.3 %collective-permute-start.20 = (bf16[42,2048]{1,0:T(8,128)(2,1)S(1)}, bf16[42,2048]{1,0:T(8,128)(2,1)S(1)}, u32[]{:S(2)}, u32[]{:S(2)}) collective-permute-start(bf16[42,2048]{1,0:T(8,128)(2,1)S(1)} %fusion.refs_1_), channel_id=1, source_target_pairs={{0,12},{2,14},{4,8},{6,10},{8,4},{10,6},{12,0},{14,2},{1,13},{3,15... | collective-permute-start | bytes 516104 | tf_op jit(solution)/shard_map/ppermute | solution.py:292
  82.2 4.8 %collective-permute-start.24 = (bf16[32,1536]{1,0:T(8,128)(2,1)S(1)}, bf16[32,1536]{1,0:T(8,128)(2,1)S(1)}, u32[]{:S(2)}, u32[]{:S(2)}) collective-permute-start(bf16[32,1536]{1,0:T(8,128)(2,1)S(1)} %hidden.11.refs_1_.hidden_ref), channel_id=1, source_target_pairs={{0,1},{1,0},{2,3},{3,2},{4,5},{5,4},{6,7},{7,6},{8,9},{9,8},{10,11... | collective-permute-start | bytes 294920 | tf_op jit(solution)/shard_map/ppermute | solution.py:289
  84.5 8.2 %collective-permute-start.23 = (bf16[42,2048]{1,0:T(8,128)(2,1)S(1)}, bf16[42,2048]{1,0:T(8,128)(2,1)S(1)}, u32[]{:S(2)}, u32[]{:S(2)}) collective-permute-start(bf16[42,2048]{1,0:T(8,128)(2,1)S(1)} %bitcast.5), channel_id=1, source_target_pairs={{0,6},{2,4},{4,2},{6,0},{8,14},{10,12},{12,10},{14,8},{1,7},{3,5},... | collective-permute-start | bytes 516104 | tf_op jit(solution)/shard_map/ppermute | solution.py:292
  88.3 4.4 %collective-permute-start.25 = (bf16[42,2048]{1,0:T(8,128)(2,1)S(1)}, bf16[42,2048]{1,0:T(8,128)(2,1)S(1)}, u32[]{:S(2)}, u32[]{:S(2)}) collective-permute-start(bf16[42,2048]{1,0:T(8,128)(2,1)S(1)} %pad_maximum_fusion.4), channel_id=1, source_target_pairs={{0,2},{2,0},{4,6},{6,4},{8,10},{10,8},{12,14},{14,12},{1,3},{3,1},... | collective-permute-start | bytes 516104 | tf_op jit(solution)/shard_map/ppermute | solution.py:292
  (4 other events, 9.9 us)
